TPU v7x, 32 devices: a whole 2x2x4 slice. The times are simulated.
32 devices in a mesh: img: 4 (over y, x), band: 8 (over z, core).
Axes of the slice: x: 2, y: 2, z: 4, core: 2. Of those that a mesh axis runs over, the one named last changes fastest.
Arguments:
- patches: bfloat16 [16, 2048, 768], P('img', 'band'), may hold values from -6 to 6
- cotangent: bfloat16 [16, 2048, 768], P('img', 'band')
- valid_counts: int32 [16], P('img'), may hold values from 512 to 2048, as said below
- qkv_master: float32 [768, 2304], P(('img', 'band')), may hold values from -0.21875 to 0.21875
- out_master: float32 [768, 768], P(None, ('img', 'band')), may hold values from -1.75 to 1.75
- in_master: float32 [768, 4096], P(('img', 'band')), may hold values from -0.21875 to 0.21875
- down_master: float32 [2048, 768], P(None, ('img', 'band')), may hold values from -0.125 to 0.125
- gain_master: float32 [2, 768], P(None, ('img', 'band'))
- qkv_first: float32 [768, 2304], P(('img', 'band')), may hold values from -0.00024414062 to 0.00024414062
- out_first: float32 [768, 768], P(None, ('img', 'band')), may hold values from -0.00024414062 to 0.00024414062
- in_first: float32 [768, 4096], P(('img', 'band')), may hold values from -0.00024414062 to 0.00024414062
- down_first: float32 [2048, 768], P(None, ('img', 'band')), may hold values from -0.00024414062 to 0.00024414062
- gain_first: float32 [2, 768], P(None, ('img', 'band')), may hold values from -0.0007324219 to 0.0007324219
- qkv_second: float32 [768, 2304], P(('img', 'band')), may hold values from 1.4128508e-10 to 5.651403e-10
- out_second: float32 [768, 768], P(None, ('img', 'band')), may hold values from 1.4128508e-10 to 5.651403e-10
- in_second: float32 [768, 4096], P(('img', 'band')), may hold values from 1.4128508e-10 to 5.651403e-10
- down_second: float32 [2048, 768], P(None, ('img', 'band')), may hold values from 1.4128508e-10 to 5.651403e-10
- gain_second: float32 [2, 768], P(None, ('img', 'band')), may hold values from 1.2715657e-09 to 5.086263e-09
Outputs:
- output: bfloat16 [16, 2048, 768], P('img', 'band')
- back_input: bfloat16 [16, 2048, 768], P('img', 'band')
- grad_norm: float32 [], replicated
- qkv_new: float32 [768, 2304], P(('img', 'band'))
- out_new: float32 [768, 768], P(None, ('img', 'band'))
- in_new: float32 [768, 4096], P(('img', 'band'))
- down_new: float32 [2048, 768], P(None, ('img', 'band'))
- gain_new: float32 [2, 768], P(None, ('img', 'band'))
- qkv_first_new: float32 [768, 2304], P(('img', 'band'))
- out_first_new: float32 [768, 768], P(None, ('img', 'band'))
- in_first_new: float32 [768, 4096], P(('img', 'band'))
- down_first_new: float32 [2048, 768], P(None, ('img', 'band'))
- gain_first_new: float32 [2, 768], P(None, ('img', 'band'))
- qkv_second_new: float32 [768, 2304], P(('img', 'band'))
- out_second_new: float32 [768, 768], P(None, ('img', 'band'))
- in_second_new: float32 [768, 4096], P(('img', 'band'))
- down_second_new: float32 [2048, 768], P(None, ('img', 'band'))
- gain_second_new: float32 [2, 768], P(None, ('img', 'band'))
- qkv_copy: bfloat16 [768, 2304], P(('img', 'band'))
- out_copy: bfloat16 [768, 768], P(None, ('img', 'band'))
- in_copy: bfloat16 [768, 4096], P(('img', 'band'))
- down_copy: bfloat16 [2048, 768], P(None, ('img', 'band'))
- gain_copy: bfloat16 [2, 768], P(None, ('img', 'band'))
Inputs may be any that keep to these rules, and one draw needn't show every extreme that they name: `valid_counts`: each image's valid patches are its first slots; in each aligned group of 4 images one image has all 2048 slots valid.
All inputs are finite; a program needn't handle non-finite values.
Results may differ from a plain program's by a relative error of at most 0.015.
The roundings to bfloat16 on the way count: a program that leaves them out, or rounds other values in their place, can miss the bound.
Values may be sent and summed in bfloat16 or wider, within the bound.
A program may use at most 256 MiB of HBM per device.

v0:
```python
import jax
import jax.numpy as jnp
from jax import lax
from jax.sharding import PartitionSpec as P

HEADS = 12
HEAD_DIM = 64
STEP = 10


EPS = 1e-06
NEG = -1000000000.0
SCALE = 0.125
CLIP = 1.0
BETA_ONE = 0.9
BETA_TWO = 0.999
ADAM_EPS = 1e-08
RATES = (0.06, 0.5, 0.06, 0.04, 0.5)
DECAYS = (0.1, 0.1, 0.1, 0.1, 0.0)


def rms_norm(value, gain):
    return value * lax.rsqrt(jnp.mean(value * value, -1, keepdims=True) + EPS) * gain


def gated(gate_part, up_part):
    return jax.nn.gelu(gate_part, approximate=True) * up_part


def adam_step(master, grad, first, second, factor, rate, decay):
    clipped = factor * grad
    first_new = BETA_ONE * first + (1.0 - BETA_ONE) * clipped
    second_new = BETA_TWO * second + (1.0 - BETA_TWO) * clipped * clipped
    corrected = first_new / (1.0 - BETA_ONE**STEP)
    spread = jnp.sqrt(second_new / (1.0 - BETA_TWO**STEP)) + ADAM_EPS
    master_new = master - rate * (corrected / spread + decay * master)
    return (master_new, first_new, second_new)


def head_slab(array, pair_index):
    pair_width = 2 * HEAD_DIM
    piece = lax.dynamic_slice_in_dim(array, pair_index * pair_width, pair_width, 2)
    return piece.reshape(array.shape[0], array.shape[1], 2, HEAD_DIM)


def join_pairs(stacked):
    moved = jnp.moveaxis(stacked, 0, 2)
    return moved.reshape(moved.shape[0], moved.shape[1], moved.shape[2] * moved.shape[3])


def masked_scores(query_slab, key_slab, key_mask):
    raw = (
        jnp.einsum("irhd,ilhd->ihrl", query_slab, key_slab, preferred_element_type=jnp.float32)
        * SCALE
    )
    return jnp.where(key_mask[:, None, None, :], raw, NEG)


def score_grads(query_slab, key_slab, value_slab, out_slab, log_sums, key_mask, row_dots):
    scores = masked_scores(query_slab, key_slab, key_mask)
    chances = jnp.exp(scores - log_sums[..., None])
    back_chances = jnp.einsum(
        "irhd,ilhd->ihrl", out_slab, value_slab, preferred_element_type=jnp.float32
    )
    row_dots = jnp.sum(chances * back_chances, -1)
    back_scores = (chances * (back_chances - row_dots[..., None])).astype(jnp.bfloat16)
    return (chances.astype(jnp.bfloat16), back_scores, row_dots)


def on_device(
    patches,
    cotangent,
    valid_counts,
    qkv_master,
    out_master,
    in_master,
    down_master,
    gain_master,
    qkv_first,
    out_first,
    in_first,
    down_first,
    gain_first,
    qkv_second,
    out_second,
    in_second,
    down_second,
    gain_second,
):
    images, band_rows, model_width = patches.shape
    band_place = lax.axis_index("band")
    total_len = band_rows * lax.axis_size("band")
    pair_count = HEADS // 2
    row_ids = band_place * band_rows + jnp.arange(band_rows, dtype=jnp.int32)
    own_mask = row_ids[None, :] < valid_counts[:, None]
    row_keep = own_mask.astype(jnp.float32).reshape(images * band_rows, 1)
    key_valid = jnp.arange(total_len, dtype=jnp.int32)[None, :] < valid_counts[:, None]
    w_qkv, w_out, w_in, w_down, gains = (
        lax.all_gather(qkv_master.astype(jnp.bfloat16), ("img", "band"), axis=0, tiled=True),
        lax.all_gather(out_master.astype(jnp.bfloat16), ("img", "band"), axis=1, tiled=True),
        lax.all_gather(in_master.astype(jnp.bfloat16), ("img", "band"), axis=0, tiled=True),
        lax.all_gather(down_master.astype(jnp.bfloat16), ("img", "band"), axis=1, tiled=True),
        lax.all_gather(gain_master.astype(jnp.bfloat16), ("img", "band"), axis=1, tiled=True),
    )
    gain_one = gains[0].astype(jnp.float32)
    gain_two = gains[1].astype(jnp.float32)
    hidden_units = w_down.shape[0]
    tokens = patches.reshape(images * band_rows, model_width).astype(jnp.float32)
    normed_a = rms_norm(tokens, gain_one).astype(jnp.bfloat16)
    project = jnp.dot(normed_a, w_qkv, preferred_element_type=jnp.float32)
    queries = project[:, :model_width].astype(jnp.bfloat16).reshape(images, band_rows, model_width)
    keys_local = (
        project[:, model_width : 2 * model_width]
        .astype(jnp.bfloat16)
        .reshape(images, band_rows, model_width)
    )
    values_local = (
        project[:, 2 * model_width :].astype(jnp.bfloat16).reshape(images, band_rows, model_width)
    )
    keys_all, values_all = (
        lax.all_gather(keys_local, "band", axis=1, tiled=True),
        lax.all_gather(values_local, "band", axis=1, tiled=True),
    )

    def forward_pair(pair_index):
        scores = masked_scores(
            head_slab(queries, pair_index), head_slab(keys_all, pair_index), key_valid
        )
        highest = jnp.max(scores, -1, keepdims=True)
        powers = jnp.exp(scores - highest)
        denominator = jnp.sum(powers, -1, keepdims=True)
        chances = (powers / denominator).astype(jnp.bfloat16)
        mixed = jnp.einsum(
            "ihrl,ilhd->irhd",
            chances,
            head_slab(values_all, pair_index),
            preferred_element_type=jnp.float32,
        )
        return (
            mixed.reshape(images, band_rows, 2 * HEAD_DIM),
            (highest + jnp.log(denominator))[..., 0],
        )

    mixed_pairs, log_sums = lax.map(forward_pair, jnp.arange(pair_count))
    attended = join_pairs(mixed_pairs).reshape(images * band_rows, model_width).astype(jnp.bfloat16)
    middle = tokens + jnp.dot(attended, w_out, preferred_element_type=jnp.float32)
    normed_b = rms_norm(middle, gain_two).astype(jnp.bfloat16)
    gate_up = jnp.dot(normed_b, w_in, preferred_element_type=jnp.float32)
    gate_part = gate_up[:, :hidden_units]
    up_part = gate_up[:, hidden_units:]
    hidden = gated(gate_part, up_part).astype(jnp.bfloat16)
    result = row_keep * (middle + jnp.dot(hidden, w_down, preferred_element_type=jnp.float32))
    output = result.astype(jnp.bfloat16).reshape(images, band_rows, model_width)
    back_result = row_keep * cotangent.reshape(images * band_rows, model_width).astype(jnp.float32)
    back_low = back_result.astype(jnp.bfloat16)
    grad_down = jnp.dot(hidden.T, back_low, preferred_element_type=jnp.float32)
    back_hidden = jnp.dot(back_low, w_down.T, preferred_element_type=jnp.float32)
    gate_value, gate_back = jax.vjp(gated, gate_part, up_part)
    back_gate, back_up = gate_back(back_hidden)
    back_gate_up = jnp.concatenate([back_gate, back_up], 1).astype(jnp.bfloat16)
    grad_in = jnp.dot(normed_b.T, back_gate_up, preferred_element_type=jnp.float32)
    back_normed_b = jnp.dot(back_gate_up, w_in.T, preferred_element_type=jnp.float32)
    norm_value, second_back = jax.vjp(rms_norm, middle, gain_two)
    back_middle_norm, grad_gain_two = second_back(back_normed_b)
    back_middle = back_result + back_middle_norm
    back_branch = back_middle.astype(jnp.bfloat16)
    grad_out = jnp.dot(attended.T, back_branch, preferred_element_type=jnp.float32)
    back_attended = jnp.dot(back_branch, w_out.T, preferred_element_type=jnp.float32)
    back_attended = back_attended.astype(jnp.bfloat16).reshape(images, band_rows, model_width)

    def backward_pair(pair_index):
        query_slab = head_slab(queries, pair_index)
        key_slab = head_slab(keys_all, pair_index)
        out_slab = head_slab(back_attended, pair_index)
        chances, back_scores, row_dots = score_grads(
            query_slab,
            key_slab,
            head_slab(values_all, pair_index),
            out_slab,
            log_sums[pair_index],
            key_valid,
            None,
        )
        grad_query = (
            jnp.einsum("ihrl,ilhd->irhd", back_scores, key_slab, preferred_element_type=jnp.float32)
            * SCALE
        )
        grad_key = (
            jnp.einsum(
                "ihrl,irhd->ilhd", back_scores, query_slab, preferred_element_type=jnp.float32
            )
            * SCALE
        )
        grad_value = jnp.einsum(
            "ihrl,irhd->ilhd", chances, out_slab, preferred_element_type=jnp.float32
        )
        return (
            grad_query.reshape(images, band_rows, 2 * HEAD_DIM),
            grad_key.reshape(images, total_len, 2 * HEAD_DIM),
            grad_value.reshape(images, total_len, 2 * HEAD_DIM),
        )

    query_pairs, key_pairs, value_pairs = lax.map(backward_pair, jnp.arange(pair_count))
    key_sums, value_sums = (
        lax.psum_scatter(
            join_pairs(key_pairs).astype(jnp.bfloat16), "band", scatter_dimension=1, tiled=True
        ).astype(jnp.float32),
        lax.psum_scatter(
            join_pairs(value_pairs).astype(jnp.bfloat16), "band", scatter_dimension=1, tiled=True
        ).astype(jnp.float32),
    )
    back_project = jnp.concatenate(
        [
            join_pairs(query_pairs).astype(jnp.bfloat16),
            key_sums.astype(jnp.bfloat16),
            value_sums.astype(jnp.bfloat16),
        ],
        2,
    )
    back_project = back_project.reshape(images * band_rows, 3 * model_width)
    grad_qkv = jnp.dot(normed_a.T, back_project, preferred_element_type=jnp.float32)
    back_normed_a = jnp.dot(back_project, w_qkv.T, preferred_element_type=jnp.float32)
    first_value, first_back = jax.vjp(rms_norm, tokens, gain_one)
    back_tokens, grad_gain_one = first_back(back_normed_a)
    back_input = (
        (back_middle + back_tokens).astype(jnp.bfloat16).reshape(images, band_rows, model_width)
    )
    grad_gains = jnp.stack([grad_gain_one, grad_gain_two])
    shards = (
        lax.psum_scatter(grad_qkv, ("img", "band"), scatter_dimension=0, tiled=True),
        lax.psum_scatter(grad_out, ("img", "band"), scatter_dimension=1, tiled=True),
        lax.psum_scatter(grad_in, ("img", "band"), scatter_dimension=0, tiled=True),
        lax.psum_scatter(grad_down, ("img", "band"), scatter_dimension=1, tiled=True),
        lax.psum_scatter(grad_gains, ("img", "band"), scatter_dimension=1, tiled=True),
    )
    squares = jnp.float32(0.0)
    for shard in shards:
        squares = squares + jnp.sum(shard * shard)
    grad_norm = jnp.sqrt(lax.psum(squares, ("img", "band")))
    factor = jnp.minimum(1.0, CLIP / grad_norm)
    masters = (qkv_master, out_master, in_master, down_master, gain_master)
    firsts = (qkv_first, out_first, in_first, down_first, gain_first)
    seconds = (qkv_second, out_second, in_second, down_second, gain_second)
    updated = [
        adam_step(masters[j], shards[j], firsts[j], seconds[j], factor, RATES[j], DECAYS[j])
        for j in range(5)
    ]
    return (
        output,
        back_input,
        grad_norm,
        updated[0][0],
        updated[1][0],
        updated[2][0],
        updated[3][0],
        updated[4][0],
        updated[0][1],
        updated[1][1],
        updated[2][1],
        updated[3][1],
        updated[4][1],
        updated[0][2],
        updated[1][2],
        updated[2][2],
        updated[3][2],
        updated[4][2],
        updated[0][0].astype(jnp.bfloat16),
        updated[1][0].astype(jnp.bfloat16),
        updated[2][0].astype(jnp.bfloat16),
        updated[3][0].astype(jnp.bfloat16),
        updated[4][0].astype(jnp.bfloat16),
    )


def solution(mesh):
    return jax.shard_map(
        on_device,
        mesh=mesh,
        in_specs=(
            P("img", "band", None),
            P("img", "band", None),
            P("img"),
            P(("img", "band"), None),
            P(None, ("img", "band")),
            P(("img", "band"), None),
            P(None, ("img", "band")),
            P(None, ("img", "band")),
            P(("img", "band"), None),
            P(None, ("img", "band")),
            P(("img", "band"), None),
            P(None, ("img", "band")),
            P(None, ("img", "band")),
            P(("img", "band"), None),
            P(None, ("img", "band")),
            P(("img", "band"), None),
            P(None, ("img", "band")),
            P(None, ("img", "band")),
        ),
        out_specs=(
            P("img", "band", None),
            P("img", "band", None),
            P(),
            P(("img", "band"), None),
            P(None, ("img", "band")),
            P(("img", "band"), None),
            P(None, ("img", "band")),
            P(None, ("img", "band")),
            P(("img", "band"), None),
            P(None, ("img", "band")),
            P(("img", "band"), None),
            P(None, ("img", "band")),
            P(None, ("img", "band")),
            P(("img", "band"), None),
            P(None, ("img", "band")),
            P(("img", "band"), None),
            P(None, ("img", "band")),
            P(None, ("img", "band")),
            P(("img", "band"), None),
            P(None, ("img", "band")),
            P(("img", "band"), None),
            P(None, ("img", "band")),
            P(None, ("img", "band")),
        ),
        check_vma=False,
    )
```

profile of v0, /device:TPU:0, one launch (start us, length us, event | category | flops | bytes accessed | tf_op | source)
XLA Modules:
  0.0 1777.3 jit_solution(7436057197855454063)
XLA Ops:
  9.6 43.0 %all-gather = bf16[32,24,2]{1,2,0:T(2,128)(2,1)S(1)} all-gather(bf16[1,24,2]{1,2,0:T(2,128)(2,1)S(1)} %convert_bitcast_fusion.2), channel_id=1, replica_groups=mesh['img'=4,'band'=8] {'img','band'}, dimensions={0}, use_global_device_ids=true | all-gather | bytes 3168 | tf_op jit(solution)/shard_map/all_gather | solution.py:103
  58.6 16.0 all-gather.8.cloned.1.call-done
  94.1 106.7 %all-gather.10.cloned.1.call-done = bf16[4,2048,768]{1,2,0:T(8,128)(2,1)} async-done(((bf16[4,256,768]{1,2,0:T(8,128)(2,1)}), bf16[4,2048,768]{1,2,0:T(8,128)(2,1)}) %all-gather.10.cloned.1.call-update) | async-done | bytes 12582928 | tf_op jit(solution)/shard_map/all_gather | solution.py:122
  200.8 117.0 %all-gather.12.cloned.1.call-done = bf16[4,2048,768]{1,2,0:T(8,128)(2,1)} async-done(((bf16[4,256,768]{1,2,0:T(8,128)(2,1)}), bf16[4,2048,768]{1,2,0:T(8,128)(2,1)}) %all-gather.12.cloned.1.call-update) | async-done | bytes 12582928 | tf_op jit(solution)/shard_map/all_gather | solution.py:121
  317.8 105.7 %while.28 = (s32[]{:T(128)}, bf16[6,4,256,128]{2,3,1,0:T(8,128)(2,1)}, f32[6,4,2,256]{3,2,1,0:T(2,128)}, s32[6]{0:T(128)S(1)}, bf16[4,2048,768]{1,2,0:T(8,128)(2...) while((s32[]{:T(128)}, ...), condition=%wide.region_4.5_spmd.clone, body=%wide.region_1.4_spmd.clone.sunk | while | flops 1124079616 | bytes 64585944 | solution.py:144
  458.7 48.0 %all-gather.18.cloned.1.call-done = bf16[2048,768]{0,1:T(8,128)(2,1)} async-done(((bf16[2048,24]{0,1:T(8,128)(2,1)}), bf16[2048,768]{0,1:T(8,128)(2,1)}) %all-gather.18.cloned.1.call-update) | async-done | bytes 3145744 | tf_op jit(solution)/shard_map/all_gather | solution.py:102
  506.7 18.2 %fusion.21 = (bf16[1024,2048]{1,0:T(8,128)(2,1)}, bf16[1024,2048]{1,0:T(8,128)(2,1)}, bf16[1024,2048]{1,0:T(8,128)(2,1)}) fusion(f32[1024,4096]{1,0:T(8,128)} %fusion.54, bf16[1024,768]{1,0:T(8,128)(2,1)} %fusion.27, bf16[2048,768]{0,1:T(8,128)(2,1)} %all-gather.18.cloned.1.call-done), kind=kOutput, calls=%fused_computation.43 | convolution fusion | flops 3275751424 | bytes 34078720 | tf_op jit(solution)/shard_map/dot_general | solution.py:157
  539.1 389.5 %while.29 = (s32[]{:T(128)}, bf16[6,4,256,128]{2,3,0,1:T(8,128)(2,1)}, bf16[6,4,2048,128]{2,3,0,1:T(8,128)(2,1)}, bf16[6,4,2048,128]{2,3,0,1:T(8,128)(2,1)}, s32...) while((s32[]{:T(128)}, ...), condition=%wide.region_9.10_spmd.clone, body=%wide.region_7.9_spmd.clone.sunk | while | flops 2749634560 | bytes 206922544 | solution.py:203
  558.4 15.2 multiply_reduce_fusion.10
  623.3 15.2 multiply_reduce_fusion.10
  688.2 15.2 multiply_reduce_fusion.10
  753.0 15.2 multiply_reduce_fusion.10
  817.9 15.2 multiply_reduce_fusion.10
  882.9 15.2 multiply_reduce_fusion.10
  928.6 16.7 copy.75
  945.4 16.8 copy.73
  996.4 77.1 %reduce-scatter.10.cloned.1.call-done = bf16[4,256,768]{2,1,0:T(8,128)(2,1)} async-done(((bf16[4,2048,768]{2,1,0:T(8,128)(2,1)}), bf16[4,256,768]{2,1,0:T(8,128)(2,1)}) %reduce-scatter.10.cloned.1.call-update) | async-done | bytes 1572880 | tf_op jit(solution)/shard_map/reduce_scatter | solution.py:208
  1073.5 129.9 %reduce-scatter.8.cloned.1.call-done = bf16[4,256,768]{2,1,0:T(8,128)(2,1)} async-done(((bf16[4,2048,768]{2,1,0:T(8,128)(2,1)}), bf16[4,256,768]{2,1,0:T(8,128)(2,1)}) %reduce-scatter.8.cloned.1.call-update) | async-done | bytes 1572880 | tf_op jit(solution)/shard_map/reduce_scatter | solution.py:205
  1221.7 84.5 %reduce-scatter.14.cloned.1.call-done = f32[768,24]{0,1:T(8,128)} async-done(((f32[768,768]{0,1:T(8,128)}), f32[768,24]{0,1:T(8,128)}) %reduce-scatter.14.cloned.1.call-update) | async-done | bytes 73744 | tf_op jit(solution)/shard_map/reduce_scatter | solution.py:231
  1307.7 118.5 %reduce-scatter.18.cloned.1.call-done = f32[2048,24]{0,1:T(8,128)} async-done(((f32[2048,768]{0,1:T(8,128)}), f32[2048,24]{0,1:T(8,128)}) %reduce-scatter.18.cloned.1.call-update) | async-done | bytes 196624 | tf_op jit(solution)/shard_map/reduce_scatter | solution.py:233
  1427.8 159.1 %reduce-scatter.16.cloned.1.call-done = f32[24,4096]{1,0:T(8,128)} async-done(((f32[768,4096]{1,0:T(8,128)}), f32[24,4096]{1,0:T(8,128)}) %reduce-scatter.16.cloned.1.call-update) | async-done | bytes 393232 | tf_op jit(solution)/shard_map/reduce_scatter | solution.py:232
  1597.5 40.0 %all-reduce = f32[2,768]{1,0:T(2,128)S(1)} all-reduce(f32[2,768]{1,0:T(2,128)S(1)} %pad_maximum_fusion.4), channel_id=8, replica_groups=mesh['img'=4,'band'=8] {'img','band'}, use_global_device_ids=true, to_apply=%region_23.24.clone | all-reduce | flops 1536 | bytes 12288
  1638.2 73.4 %reduce-scatter.12.cloned.1.call-done = f32[24,2304]{1,0:T(8,128)} async-done(((f32[768,2304]{1,0:T(8,128)}), f32[24,2304]{1,0:T(8,128)}) %reduce-scatter.12.cloned.1.call-update) | async-done | bytes 221200 | tf_op jit(solution)/shard_map/reduce_scatter | solution.py:230
  1721.6 40.1 %psum.7 = f32[]{:T(128)} all-reduce(f32[]{:T(128)S(6)} %add.209), channel_id=1, replica_groups=mesh['img'=4,'band'=8] {'img','band'}, use_global_device_ids=true, to_apply=%region_25.26 | all-reduce | flops 1 | bytes 8 | tf_op jit(solution)/shard_map/psum | solution.py:239
  (423 shorter events, 540.5 us)
Async XLA Ops:
  7.2 67.4 %all-gather.8.cloned.1.call-start = ((), (), s32[]{:S(2)}) async-start(), calls=%async_computation.6 | async-start | bytes 3649536 | tf_op jit(solution)/shard_map/all_gather | solution.py:99
  8.9 191.9 %all-gather.10.cloned.1.call-start = ((), (), s32[]{:S(2)}) async-start(), calls=%async_computation.7 | async-start | bytes 14155776 | tf_op jit(solution)/shard_map/all_gather | solution.py:122
  84.7 233.1 %all-gather.12.cloned.1.call-start = ((), (), s32[]{:S(2)}) async-start(), calls=%async_computation.8 | async-start | bytes 14155776 | tf_op jit(solution)/shard_map/all_gather | solution.py:121
  86.3 340.3 %all-gather.14.cloned.1.call-start = ((), (), s32[]{:S(2)}) async-start(), calls=%async_computation.9 | async-start | bytes 1216512 | tf_op jit(solution)/shard_map/all_gather | solution.py:100
  88.0 357.6 %all-gather.16.cloned.1.call-start = ((), (), s32[]{:S(2)}) async-start(), calls=%async_computation.10 | async-start | bytes 6488064 | tf_op jit(solution)/shard_map/all_gather | solution.py:101
  88.8 417.9 %all-gather.18.cloned.1.call-start = ((), (), s32[]{:S(2)}) async-start(), calls=%async_computation.11 | async-start | bytes 3244032 | tf_op jit(solution)/shard_map/all_gather | solution.py:102
  90.4 983.1 %reduce-scatter.10.cloned.1.call-start = ((), (), s32[]{:S(2)}) async-start(), calls=%async_computation.13 | async-start | bytes 14155776 | tf_op jit(solution)/shard_map/reduce_scatter | solution.py:208
  90.9 226.8 %copy-start.30 = (f32[1,2,4,128]{3,1,2,0:T(2,128)}, f32[1,2,4,128]{3,1,2,0:T(2,128)S(1)}, u32[]{:S(2)}) copy-start(f32[1,2,4,128]{3,1,2,0:T(2,128)S(1)} %copy.99) | copy-start | bytes 12292
  431.6 103.6 %copy-start.37 = (f32[1024]{0:T(1024)}, f32[1024]{0:T(1024)S(1)}, u32[]{:S(2)}) copy-start(f32[1024]{0:T(1024)S(1)} %fusion.46) | copy-start | bytes 12292
  458.7 66.3 %copy-start.6 = (f32[1024,768]{1,0:T(8,128)S(1)}, f32[1024,768]{1,0:T(8,128)}, u32[]{:S(2)}) copy-start(f32[1024,768]{1,0:T(8,128)} %get-tuple-element.312) | copy-start | bytes 9437188
  945.3 258.1 %reduce-scatter.8.cloned.1.call-start = ((), (), s32[]{:S(2)}) async-start(), calls=%async_computation.12 | async-start | bytes 14155776 | tf_op jit(solution)/shard_map/reduce_scatter | solution.py:205
  962.2 344.0 %reduce-scatter.14.cloned.1.call-start = ((), (), s32[]{:S(2)}) async-start(), calls=%async_computation.15 | async-start | bytes 2433024 | tf_op jit(solution)/shard_map/reduce_scatter | solution.py:231
  968.5 457.8 %reduce-scatter.18.cloned.1.call-start = ((), (), s32[]{:S(2)}) async-start(), calls=%async_computation.17 | async-start | bytes 6488064 | tf_op jit(solution)/shard_map/reduce_scatter | solution.py:233
  977.3 609.6 %reduce-scatter.16.cloned.1.call-start = ((), (), s32[]{:S(2)}) async-start(), calls=%async_computation.16 | async-start | bytes 12976128 | tf_op jit(solution)/shard_map/reduce_scatter | solution.py:232
  994.2 209.3 %copy-start.1 = (bf16[4,256,768]{2,1,0:T(8,128)(2,1)S(1)}, bf16[4,256,768]{2,1,0:T(8,128)(2,1)}, u32[]{:S(2)}) copy-start(bf16[4,256,768]{2,1,0:T(8,128)(2,1)} %param.22) | copy-start | bytes 4718596
  994.2 209.3 %copy-start.27 = (f32[768]{0:T(1024)S(1)}, f32[768]{0:T(1024)}, u32[]{:S(2)}) copy-start(f32[768]{0:T(1024)} %copy-done.26) | copy-start | bytes 9220
  994.2 209.3 %copy-start.39 = (f32[4,256]{1,0:T(4,128)S(1)}, f32[4,256]{1,0:T(4,128)}, u32[]{:S(2)}) copy-start(f32[4,256]{1,0:T(4,128)} %get-tuple-element.309) | copy-start | bytes 12292
  994.2 717.4 %reduce-scatter.12.cloned.1.call-start = ((), (), s32[]{:S(2)}) async-start(), calls=%async_computation.14 | async-start | bytes 7299072 | tf_op jit(solution)/shard_map/reduce_scatter | solution.py:230
  1716.6 48.6 %copy-start.17 = (f32[768,24]{0,1:T(8,128)S(1)}, f32[768,24]{0,1:T(8,128)}, u32[]{:S(2)}) copy-start(f32[768,24]{0,1:T(8,128)} %param.26) | copy-start | bytes 221188
  1716.6 48.6 %copy-start.18 = (f32[768,24]{0,1:T(8,128)S(1)}, f32[768,24]{0,1:T(8,128)}, u32[]{:S(2)}) copy-start(f32[768,24]{0,1:T(8,128)} %reduce-scatter.14.cloned.1.call-done) | copy-start | bytes 221188
  1716.6 48.6 %copy-start.21 = (f32[768,24]{0,1:T(8,128)S(1)}, f32[768,24]{0,1:T(8,128)}, u32[]{:S(2)}) copy-start(f32[768,24]{0,1:T(8,128)} %param.31) | copy-start | bytes 221188
  1716.6 49.3 %copy-start.10 = (f32[24,4096]{1,0:T(8,128)S(1)}, f32[24,4096]{1,0:T(8,128)}, u32[]{:S(2)}) copy-start(f32[24,4096]{1,0:T(8,128)} %param.27) | copy-start | bytes 1179652
  1716.6 49.3 %copy-start.11 = (f32[24,4096]{1,0:T(8,128)S(1)}, f32[24,4096]{1,0:T(8,128)}, u32[]{:S(2)}) copy-start(f32[24,4096]{1,0:T(8,128)} %reduce-scatter.16.cloned.1.call-done) | copy-start | bytes 1179652
  1716.6 49.3 %copy-start.16 = (f32[24,4096]{1,0:T(8,128)S(1)}, f32[24,4096]{1,0:T(8,128)}, u32[]{:S(2)}) copy-start(f32[24,4096]{1,0:T(8,128)} %param.32) | copy-start | bytes 1179652
  (81 other events, 1179.6 us)
Sparse Core Ops, SparseCore 0:
  11.6 62.9 all-gather.7
  84.8 115.9 all-gather.9
  202.4 115.3 all-gather.11
  321.2 52.3 all-gather.13
  377.1 68.5 all-gather.15
  449.1 57.6 all-gather.17
  945.5 128.0 reduce-scatter.9
  1075.8 127.5 reduce-scatter.7
  1208.8 97.4 reduce-scatter.13
  1312.6 113.5 reduce-scatter.17
  1432.3 154.6 reduce-scatter.15
  1593.4 118.1 reduce-scatter.11
where the time goes:
time: 1780 us
  waiting for transfers between devices  945 us (53%)
  matrix products  380 us (21%)
  local copies, waits for them, and re-layouts  162 us (9%)
  other arithmetic  126 us (7%)
  blocking collectives  123 us (7%)
  loops' own time  20.4 us (1%)
  between operations  20 us (1%)
    reduce_scatter x1, waiting for transfers between devices, on_device(): lax.psum_scatter(grad_in, ('img', 'band'), scatter_dimension=0, tiled=True)  159 us
    reduce_scatter x1, waiting for transfers between devices, on_device(): lax.psum_scatter(join_pairs(key_pairs).astype(jnp.bfloat16), 'band', scat...  130 us
    reduce_scatter x1, waiting for transfers between devices, on_device(): lax.psum_scatter(grad_down, ('img', 'band'), scatter_dimension=1, tiled=T...  119 us
    all_gather x1, waiting for transfers between devices, on_device(): lax.all_gather(keys_local, 'band', axis=1, tiled=True)  117 us
    all_gather x1, waiting for transfers between devices, on_device(): lax.all_gather(values_local, 'band', axis=1, tiled=True)  107 us
    dot_general x6, matrix products, score_grads(): jnp.einsum('irhd,ilhd->ihrl', out_slab, value_slab, preferred_element_typ...  91.2 us
    reduce_scatter x1, waiting for transfers between devices, on_device(): lax.psum_scatter(grad_out, ('img', 'band'), scatter_dimension=1, tiled=True)  84.5 us
    reduce_scatter x1, waiting for transfers between devices, on_device(): lax.psum_scatter(join_pairs(value_pairs).astype(jnp.bfloat16), 'band', sc...  77.1 us
  transfers between devices with their start and end apart: 12, of which 11 were waited for; matrix products, arithmetic and copies ran while one was open for 12% of the time, Pallas kernels for 0%

commit v1 on v0

v1 whole, which is shorter than its diff:
```python
import functools

import jax
import jax.numpy as jnp
from jax import lax
from jax.experimental import pallas as pl
from jax.experimental.pallas import tpu as pltpu
from jax.sharding import PartitionSpec as P

HEADS = 12
HEAD_DIM = 64
PAIR = 2 * HEAD_DIM
STEP = 10
EPS = 1e-06
NEG = -1000000000.0
SCALE = 0.125
CLIP = 1.0
BETA_ONE = 0.9
BETA_TWO = 0.999
ADAM_EPS = 1e-08
RATES = (0.06, 0.5, 0.06, 0.04, 0.5)
DECAYS = (0.1, 0.1, 0.1, 0.1, 0.0)
BF = jnp.bfloat16
F32 = jnp.float32
MESH = pl.DeviceIdType.MESH
ANY = pl.BlockSpec(memory_space=pl.ANY)
MIB = 2**20


class Net:
    def __init__(self, dims, send, recv, local):
        self.dims = dims
        big_y, big_x, big_z, share = dims
        img, band = lax.axis_index("img"), lax.axis_index("band")
        self.y, self.x = img // big_x, img % big_x
        self.z, self.c = band // 2, band % 2
        self.image, self.part = band // share, band % share
        self.images = 2 * big_z // share
        self.send, self.recv, self.local = send, recv, local
        self.used, self.used_local = 0, 0

    def device(self, y, x, z, c):
        return (y * self.dims[1] + x, z * 2 + c)

    def line(self, name):
        size = dict(zip("yxz", self.dims))[name] if name in "yxz" else 2
        places = []
        for d in range(1, size):
            at = dict(y=self.y, x=self.x, z=self.z, c=self.c)
            at[name] = lax.rem(at[name] + d, size)
            places.append((at[name], self.device(**at)))
        return places

    def holders(self):
        img = lax.axis_index("img")
        places = []
        for d in range(1, self.images):
            other = lax.rem(self.image + d, self.images)
            places.append((other, (img, other * self.dims[3] + self.part)))
        return places

    def sharers(self):
        img = lax.axis_index("img")
        places = []
        for d in range(1, self.dims[3]):
            other = lax.rem(self.part + d, self.dims[3])
            places.append((other, (img, self.image * self.dims[3] + other)))
        return places

    def greet(self, kinds):
        barrier = pltpu.get_barrier_semaphore()
        count = 0
        for kind in kinds:
            if kind == "image":
                places = self.holders()
            elif kind == "share":
                places = self.sharers()
            else:
                places = self.line(kind)
            for _, target in places:
                pl.semaphore_signal(barrier, inc=1, device_id=target, device_id_type=MESH)
            count += len(places)
        pl.semaphore_wait(barrier, count)

    def copy(self, source, target_ref, target):
        at = self.used
        self.used += 1
        made = pltpu.make_async_remote_copy(
            src_ref=source,
            dst_ref=target_ref,
            send_sem=self.send.at[at],
            recv_sem=self.recv.at[at],
            device_id=target,
            device_id_type=MESH,
        )
        made.start()
        return made

    def local_copy(self, source, target_ref):
        made = pltpu.make_async_copy(source, target_ref, self.local.at[self.used_local])
        self.used_local += 1
        made.start()
        return made


def drive(tasks):
    waiting = list(tasks)
    turn = 0
    while waiting:
        left = []
        for start, task in waiting:
            if start <= turn:
                try:
                    next(task)
                except StopIteration:
                    continue
            left.append((start, task))
        waiting = left
        turn += 1


def exchange_images(net, source, target):
    moves = [net.copy(source.at[other], target.at[net.image], dev) for other, dev in net.holders()]
    own = net.local_copy(source.at[net.image], target.at[net.image])
    yield
    yield
    yield
    yield
    for move in moves:
        move.wait_recv()
    own.wait()
    for move in moves:
        move.wait_send()


def exchange_shares(net, source, target):
    moves = [net.copy(source, target.at[net.part], dev) for _, dev in net.sharers()]
    own = net.local_copy(source, target.at[net.part])
    yield
    for move in moves:
        move.wait_recv()
    own.wait()
    for move in moves:
        move.wait_send()


def gather(net, source, target, columns, order):
    cols = pl.ds(*columns)
    y, x, z, c = net.y, net.x, net.z, net.c
    own = net.local_copy(source.at[:, cols], target.at[y, x, z, c, :, cols])
    sent = [net.copy(source.at[:, cols], target.at[y, x, z, c, :, cols], dev) for _, dev in net.line("z")]
    yield
    own.wait()
    for move in sent:
        move.wait_recv()
    part = target.at[y, x, :, c, :, cols]
    moves = [net.copy(part, part, dev) for _, dev in net.line(order[0])]
    sent += moves
    yield
    for move in moves:
        move.wait_recv()
    part = target.at[y, :, :, c, :, cols] if order[0] == "x" else target.at[:, x, :, c, :, cols]
    moves = [net.copy(part, part, dev) for _, dev in net.line(order[1])]
    sent += moves
    yield
    for move in moves:
        move.wait_recv()
    part = target.at[:, :, :, c, :, cols]
    moves = [net.copy(part, part, dev) for _, dev in net.line("c")]
    sent += moves
    yield
    for move in moves:
        move.wait_recv()
    for move in sent:
        move.wait_send()


def gather_copies(dims):
    return dims[0] + dims[1] + dims[2] - 3 + 1


def add_into(own, others, places):
    for at, slots in places:
        total = own[at].astype(F32)
        for slot in slots:
            total = total + others[slot].astype(F32)
        own[at] = total.astype(own.dtype)


def scatter(net, grad, held, from_core, from_first, from_second, from_z, out, columns, order):
    big_y, big_x, big_z, _ = net.dims
    cols = pl.ds(*columns)
    y, x, z, c = net.y, net.x, net.z, net.c
    sent = []
    (_, twin), = net.line("c")
    moves = [net.copy(grad.at[:, :, :, 1 - c, :, cols], from_core, twin)]
    sent += moves
    own = net.local_copy(grad.at[:, :, :, c, :, cols], held)
    yield
    own.wait()
    moves[0].wait_recv()

    def first_add(at, _):
        a, b, d = at // (big_x * big_z), (at // big_z) % big_x, at % big_z
        held[a, b, d] = (held[a, b, d].astype(F32) + from_core[a, b, d].astype(F32)).astype(BF)
        return 0

    lax.fori_loop(0, big_y * big_x * big_z, first_add, 0)
    moves = []
    for slot, (other, dev) in enumerate(net.line(order[0])):
        part = held.at[:, other] if order[0] == "x" else held.at[other]
        moves.append(net.copy(part, from_first.at[slot], dev))
    sent += moves
    yield
    for move in moves:
        move.wait_recv()
    left = big_y if order[0] == "x" else big_x

    def second_add(at, _):
        a, d = at // big_z, at % big_z
        place = (a, x, d) if order[0] == "x" else (y, a, d)
        total = held[place].astype(F32)
        for slot in range(len(moves)):
            total = total + from_first[slot, a, d].astype(F32)
        held[place] = total.astype(BF)
        return 0

    lax.fori_loop(0, left * big_z, second_add, 0)
    moves = []
    for slot, (other, dev) in enumerate(net.line(order[1])):
        part = held.at[other, x] if order[1] == "y" else held.at[y, other]
        moves.append(net.copy(part, from_second.at[slot], dev))
    sent += moves
    yield
    for move in moves:
        move.wait_recv()

    def third_add(d, _):
        total = held[y, x, d].astype(F32)
        for slot in range(len(moves)):
            total = total + from_second[slot, d].astype(F32)
        held[y, x, d] = total.astype(BF)
        return 0

    lax.fori_loop(0, big_z, third_add, 0)
    moves = []
    for slot, (other, dev) in enumerate(net.line("z")):
        moves.append(net.copy(held.at[y, x, other], from_z.at[slot], dev))
    sent += moves
    yield
    for move in moves:
        move.wait_recv()
    total = held[y, x, z].astype(F32)
    for slot in range(len(moves)):
        total = total + from_z[slot].astype(F32)
    out[:, columns[0] : columns[0] + columns[1]] = total
    for move in sent:
        move.wait_send()


def scatter_scratch(dims, rows, columns, order):
    big_y, big_x, big_z, _ = dims
    width = columns[1]
    ahead, left = (big_x, big_y) if order[0] == "x" else (big_y, big_x)
    return [
        pltpu.VMEM((big_y, big_x, big_z, rows, width), BF),
        pltpu.VMEM((big_y, big_x, big_z, rows, width), BF),
        pltpu.VMEM((ahead - 1, left, big_z, rows, width), BF),
        pltpu.VMEM((left - 1, big_z, rows, width), BF),
        pltpu.VMEM((big_z - 1, rows, width), BF),
    ]


def sum_tiles(net, tile, slots):
    first = 0
    for name in "cxyz":
        places = net.line(name)
        me = dict(y=net.y, x=net.x, z=net.z, c=net.c)[name]
        size = len(places) + 1
        slots[first + me] = tile[...]
        moves = [net.copy(tile, slots.at[first + me], dev) for _, dev in places]
        for move in moves:
            move.wait_recv()
        for move in moves:
            move.wait_send()
        total = slots[first]
        for d in range(1, size):
            total = total + slots[first + d]
        tile[...] = total
        first += size


def sems(count):
    return pltpu.SemaphoreType.DMA((max(count, 1),))


def halves(width):
    units = width // 128
    low = (units + 1) // 2 * 128
    if low == width:
        return [((0, width), "xy")]
    return [((0, low), "xy"), ((low, width - low), "yx")]


def gather_call(dims, name, number, blocks, images=None):
    big_y, big_x, big_z, share = dims
    parts = [halves(block.shape[1]) for block in blocks]
    copies = sum(len(p) for p in parts) * gather_copies(dims)
    local = sum(len(p) for p in parts)
    n = len(blocks)
    with_images = images is not None
    if with_images:
        copies += images.shape[0] - 1
        local += 1

    def body(*refs):
        ins, rest = refs[: n + with_images], refs[n + with_images :]
        outs, (send, recv, local_sem) = rest[: n + with_images], rest[n + with_images :]
        net = Net(dims, send, recv, local_sem)
        net.greet("zxyc" if not with_images else ["z", "x", "y", "c", "image"])
        tasks = []
        for j in range(n):
            for columns, order in parts[j]:
                tasks.append((0, gather(net, ins[j], outs[j], columns, order)))
        if with_images:
            tasks.append((0, exchange_images(net, ins[n], outs[n])))
        drive(tasks)

    args = list(blocks) + ([images] if with_images else [])
    shapes = [jax.ShapeDtypeStruct((big_y, big_x, big_z, 2) + b.shape, b.dtype) for b in blocks]
    if with_images:
        shapes.append(jax.ShapeDtypeStruct(images.shape, images.dtype))
    return pl.pallas_call(
        body,
        out_shape=shapes,
        in_specs=[ANY] * len(args),
        out_specs=[ANY] * len(shapes),
        scratch_shapes=[sems(copies), sems(copies), sems(local)],
        compiler_params=pltpu.CompilerParams(collective_id=number, has_side_effects=True),
        name=name,
    )(*args)


def scatter_call(dims, name, number, grads, images, squares=None):
    big_y, big_x, big_z, _ = dims
    rows = grads[0].shape[4]
    parts = [(j, columns, order) for j, g in enumerate(grads) for columns, order in halves(g.shape[5])]
    copies = len(parts) * gather_copies(dims) + images.shape[0] - 1
    with_squares = squares is not None
    if with_squares:
        copies += gather_copies(dims)
    local = len(parts) + 1
    n = len(grads)
    scratch = [sems(copies), sems(copies), sems(local)]
    for _, columns, order in parts:
        scratch += scatter_scratch(dims, rows, columns, order)
    if with_squares:
        scratch += [
            pltpu.VMEM((8, 128), F32),
            pltpu.VMEM((2 + big_x + big_y + big_z, 8, 128), F32),
        ]

    def body(*refs):
        n_in = n + 1 + with_squares
        n_out = n + 1 + with_squares
        ins, outs, rest = refs[:n_in], refs[n_in : n_in + n_out], refs[n_in + n_out :]
        net = Net(dims, *rest[:3])
        net.greet(["z", "x", "y", "c", "image"])
        tasks = []
        for k, (j, columns, order) in enumerate(parts):
            buffers = rest[3 + 5 * k : 8 + 5 * k]
            tasks.append((0, scatter(net, ins[j], *buffers, outs[j], columns, order)))
        tasks.append((0, exchange_images(net, ins[n], outs[n])))
        drive(tasks)
        if with_squares:
            tile, slots = rest[3 + 5 * len(parts) :]
            total = ins[n + 1][...]
            for j in range(n):
                value = outs[j][...]
                total = total + jnp.sum(value * value)
            tile[...] = total
            sum_tiles(net, tile, slots)
            outs[n + 1][...] = tile[...]

    vmem = pl.BlockSpec(memory_space=pltpu.VMEM)
    shapes = [jax.ShapeDtypeStruct((rows, g.shape[5]), F32) for g in grads]
    shapes.append(jax.ShapeDtypeStruct(images.shape, images.dtype))
    args = list(grads) + [images]
    in_specs, out_specs = [ANY] * (n + 1), [vmem] * n + [ANY]
    if with_squares:
        shapes.append(jax.ShapeDtypeStruct((8, 128), F32))
        args.append(jnp.broadcast_to(squares, (8, 128)))
        in_specs.append(vmem)
        out_specs.append(vmem)
    return pl.pallas_call(
        body,
        out_shape=shapes,
        in_specs=in_specs,
        out_specs=out_specs,
        scratch_shapes=scratch,
        compiler_params=pltpu.CompilerParams(
            collective_id=number, has_side_effects=True, vmem_limit_bytes=60 * MIB
        ),
        name=name,
    )(*args)


def share_call(dims, number, block):
    share = dims[3]

    def body(source, target, send, recv, local):
        net = Net(dims, send, recv, local)
        net.greet(["share"])
        drive([(0, exchange_shares(net, source, target))])

    return pl.pallas_call(
        body,
        out_shape=jax.ShapeDtypeStruct((share,) + block.shape, block.dtype),
        in_specs=[ANY],
        out_specs=ANY,
        scratch_shapes=[sems(share - 1), sems(share - 1), sems(1)],
        compiler_params=pltpu.CompilerParams(collective_id=number, has_side_effects=True),
        name="share_keys",
    )(block)


def return_call(dims, number, block):
    share = dims[3]

    def body(source, target, send, recv, local):
        net = Net(dims, send, recv, local)
        net.greet(["share"])
        moves = [
            net.copy(source.at[other], target.at[slot], dev)
            for slot, (other, dev) in enumerate(net.sharers())
        ]
        for move in moves:
            move.wait_recv()
        for move in moves:
            move.wait_send()

    return pl.pallas_call(
        body,
        out_shape=jax.ShapeDtypeStruct((share - 1,) + block.shape[1:], block.dtype),
        in_specs=[ANY],
        out_specs=ANY,
        scratch_shapes=[sems(share - 1), sems(share - 1), sems(1)],
        compiler_params=pltpu.CompilerParams(collective_id=number, has_side_effects=True),
        name="return_keys",
    )(block)


def mm(a, b, ca, cb):
    return lax.dot_general(a, b, (((ca,), (cb,)), ((), ())), preferred_element_type=F32)


def attend_kernel(q_ref, k_ref, v_ref, bias_ref, o_ref, l_ref, *, block):
    lane = lax.broadcasted_iota(jnp.int32, (1, PAIR), 1) < HEAD_DIM
    k, v, bias = k_ref[...], v_ref[...], bias_ref[...]

    def step(i, _):
        rows = pl.ds(pl.multiple_of(i * block, block), block)
        q = q_ref[rows, :] * jnp.asarray(SCALE, BF)
        mixed, logs = [], []
        for h in range(2):
            mine = lane if h == 0 else ~lane
            scores = mm(jnp.where(mine, q, jnp.zeros_like(q)), k, 1, 1) + bias
            highest = jnp.max(scores, -1, keepdims=True)
            powers = jnp.exp(scores - highest)
            total = jnp.sum(powers, -1, keepdims=True)
            mixed.append(mm(powers.astype(BF), v, 1, 0) / total)
            logs.append(highest + jnp.log(total))
        o_ref[rows, :] = jnp.where(lane, mixed[0], mixed[1]).astype(BF)
        l_ref[rows, :] = jnp.where(lane, logs[0], logs[1])
        return 0

    lax.fori_loop(0, q_ref.shape[0] // block, step, 0)


def attend(q, kv, bias, block):
    rows, width = q.shape
    keys = kv.shape[0]
    pairs = width // PAIR
    own = pl.BlockSpec((rows, PAIR), lambda h: (0, h))
    return pl.pallas_call(
        functools.partial(attend_kernel, block=block),
        grid=(pairs,),
        in_specs=[
            own,
            pl.BlockSpec((keys, PAIR), lambda h: (0, h)),
            pl.BlockSpec((keys, PAIR), lambda h: (0, h + pairs)),
            pl.BlockSpec((1, keys), lambda h: (0, 0)),
        ],
        out_specs=[own, own],
        out_shape=[jax.ShapeDtypeStruct((rows, width), BF), jax.ShapeDtypeStruct((rows, width), F32)],
        compiler_params=pltpu.CompilerParams(vmem_limit_bytes=56 * MIB),
        cost_estimate=pl.CostEstimate(
            flops=16 * rows * keys * width, bytes_accessed=2 * 4 * keys * width, transcendentals=rows * keys * HEADS
        ),
        name="attend",
    )(q, kv, kv, bias)


def attend_back_kernel(
    q_ref, k_ref, v_ref, bias_ref, o_ref, l_ref, do_ref, dq_ref, dk_ref, dv_ref, dk_sum, dv_sum, *, block
):
    lane = lax.broadcasted_iota(jnp.int32, (1, PAIR), 1) < HEAD_DIM
    k, v = k_ref[...], v_ref[...]
    bias = jnp.transpose(jnp.broadcast_to(bias_ref[...], (8, k.shape[0])))[:, :1]
    dk_sum[...] = jnp.zeros_like(dk_sum)
    dv_sum[...] = jnp.zeros_like(dv_sum)

    def step(i, _):
        rows = pl.ds(pl.multiple_of(i * block, block), block)
        q, do = q_ref[rows, :] * jnp.asarray(SCALE, BF), do_ref[rows, :]
        logs = jnp.transpose(l_ref[rows, :])
        products = jnp.transpose(do.astype(F32) * o_ref[rows, :].astype(F32))
        dqs, dks, dvs = [], [], []
        for h in range(2):
            mine = lane if h == 0 else ~lane
            low, high = h * HEAD_DIM, (h + 1) * HEAD_DIM
            q_h = jnp.where(mine, q, jnp.zeros_like(q))
            do_h = jnp.where(mine, do, jnp.zeros_like(do))
            row_dots = jnp.sum(products[low:high, :], 0, keepdims=True)
            chances = jnp.exp(mm(k, q_h, 1, 1) + bias - logs[low : low + 1, :])
            back = mm(v, do_h, 1, 1)
            scores = (chances * (back - row_dots)).astype(BF)
            dqs.append(mm(scores, k, 0, 0))
            dks.append(mm(scores, q_h, 1, 0))
            dvs.append(mm(chances.astype(BF), do_h, 1, 0))
        dq_ref[rows, :] = (jnp.where(lane, dqs[0], dqs[1]) * SCALE).astype(BF)
        dk_sum[...] += dks[0] + dks[1]
        dv_sum[...] += dvs[0] + dvs[1]
        return 0

    lax.fori_loop(0, q_ref.shape[0] // block, step, 0)
    dk_ref[...] = dk_sum[...].astype(BF)
    dv_ref[...] = dv_sum[...].astype(BF)


def attend_back(q, kv, bias, mixed, logs, back, block):
    rows, width = q.shape
    keys = kv.shape[0]
    pairs = width // PAIR
    own = pl.BlockSpec((rows, PAIR), lambda h: (0, h))
    key = pl.BlockSpec((keys, PAIR), lambda h: (0, h))
    return pl.pallas_call(
        functools.partial(attend_back_kernel, block=block),
        grid=(pairs,),
        in_specs=[
            own,
            key,
            pl.BlockSpec((keys, PAIR), lambda h: (0, h + pairs)),
            pl.BlockSpec((1, keys), lambda h: (0, 0)),
            own,
            own,
            own,
        ],
        out_specs=[own, key, key],
        out_shape=[
            jax.ShapeDtypeStruct((rows, width), BF),
            jax.ShapeDtypeStruct((keys, width), BF),
            jax.ShapeDtypeStruct((keys, width), BF),
        ],
        scratch_shapes=[pltpu.VMEM((keys, PAIR), F32), pltpu.VMEM((keys, PAIR), F32)],
        compiler_params=pltpu.CompilerParams(vmem_limit_bytes=56 * MIB),
        cost_estimate=pl.CostEstimate(
            flops=40 * rows * keys * width, bytes_accessed=2 * 8 * keys * width, transcendentals=rows * keys * HEADS
        ),
        name="attend_back",
    )(q, kv, kv, bias, mixed, logs, back)


def rms_norm(value, gain):
    return value * lax.rsqrt(jnp.mean(value * value, -1, keepdims=True) + EPS) * gain


def gated(gate_part, up_part):
    return jax.nn.gelu(gate_part, approximate=True) * up_part


def adam_step(master, grad, first, second, factor, rate, decay):
    clipped = factor * grad
    first_new = BETA_ONE * first + (1.0 - BETA_ONE) * clipped
    second_new = BETA_TWO * second + (1.0 - BETA_TWO) * clipped * clipped
    corrected = first_new / (1.0 - BETA_ONE**STEP)
    spread = jnp.sqrt(second_new / (1.0 - BETA_TWO**STEP)) + ADAM_EPS
    master_new = master - rate * (corrected / spread + decay * master)
    return (master_new, first_new, second_new)


def grid_of(n_img):
    big_y = max(d for d in range(1, n_img + 1) if n_img % d == 0 and d * d <= n_img)
    return big_y, n_img // big_y


def on_device(
    patches,
    cotangent,
    valid_counts,
    qkv_master,
    out_master,
    in_master,
    down_master,
    gain_master,
    qkv_first,
    out_first,
    in_first,
    down_first,
    gain_first,
    qkv_second,
    out_second,
    in_second,
    down_second,
    gain_second,
):
    images, band_rows, width = patches.shape
    n_img, n_band = lax.axis_size("img"), lax.axis_size("band")
    share = n_band // images
    big_y, big_x = grid_of(n_img)
    dims = (big_y, big_x, n_band // 2, share)
    rows = images * band_rows
    shard = qkv_master.shape[0]
    own_comm = shard % 8 == 0
    both = ("img", "band")

    def gather_all(number, blocks, chunks):
        if own_comm:
            got = gather_call(dims, "gather_%d" % number, number, blocks, chunks)
        else:
            got = [lax.all_gather(b, both, axis=0, tiled=True) for b in blocks]
            groups = [[s * share + r for s in range(images)] for r in range(share)]
            got.append(lax.all_to_all(chunks, "band", 0, 0, axis_index_groups=groups, tiled=True))
        return [g.reshape(width, g.shape[-1]) for g in got[:-1]] + [got[-1]]

    def scatter_all(number, grads, chunks, squares=None):
        if own_comm:
            shaped = [g.astype(BF).reshape(dims[:3] + (2, shard, g.shape[1])) for g in grads]
            return scatter_call(dims, "scatter_%d" % number, number, shaped, chunks, squares)
        sums = [lax.psum_scatter(g, both, scatter_dimension=0, tiled=True) for g in grads]
        groups = [[s * share + r for s in range(images)] for r in range(share)]
        got = sums + [lax.all_to_all(chunks, "band", 0, 0, axis_index_groups=groups, tiled=True)]
        if squares is not None:
            total = squares
            for s in sums:
                total = total + jnp.sum(s * s)
            got.append(lax.psum(jnp.broadcast_to(total, (8, 128)), both))
        return got

    gains_block = jnp.pad(jnp.transpose(gain_master).astype(BF), ((0, 0), (0, 126)))
    w_qkv, gains, tokens_low = gather_all(0, [qkv_master.astype(BF), gains_block], patches)
    w_in, w_out_t, w_down_t, cotangent_low = gather_all(
        1,
        [in_master.astype(BF), jnp.transpose(out_master).astype(BF), jnp.transpose(down_master).astype(BF)],
        cotangent,
    )
    gain_one = gains[:, 0].astype(F32)
    gain_two = gains[:, 1].astype(F32)
    hidden_units = w_down_t.shape[1]

    band = lax.axis_index("band")
    image, part = band // share, band % share
    count = lax.dynamic_index_in_dim(valid_counts, image, 0, keepdims=False)
    own_places = (
        (jnp.arange(images, dtype=jnp.int32)[:, None] * share + part) * band_rows
        + jnp.arange(band_rows, dtype=jnp.int32)[None, :]
    ).reshape(rows, 1)
    row_keep = (own_places < count).astype(F32)
    key_places = (
        (
            jnp.arange(images, dtype=jnp.int32)[None, :, None] * share
            + jnp.arange(share, dtype=jnp.int32)[:, None, None]
        )
        * band_rows
        + jnp.arange(band_rows, dtype=jnp.int32)[None, None, :]
    ).reshape(1, share * rows)
    bias = jnp.where(key_places < count, 0.0, NEG).astype(F32)

    tokens = tokens_low.reshape(rows, width).astype(F32)
    normed_a = rms_norm(tokens, gain_one).astype(BF)
    project = jnp.dot(normed_a, w_qkv, preferred_element_type=F32).astype(BF)
    queries = project[:, :width]
    kv = share_call(dims, 2, project[:, width:]).reshape(share * rows, 2 * width)
    attended, log_sums = attend(queries, kv, bias, 256)

    middle = tokens + mm(attended, w_out_t, 1, 1)
    normed_b = rms_norm(middle, gain_two).astype(BF)
    gate_up = jnp.dot(normed_b, w_in, preferred_element_type=F32)
    gate_part = gate_up[:, :hidden_units]
    up_part = gate_up[:, hidden_units:]
    hidden = gated(gate_part, up_part).astype(BF)
    result = row_keep * (middle + mm(hidden, w_down_t, 1, 1))
    result_low = result.astype(BF).reshape(images, band_rows, width)
    back_result = row_keep * cotangent_low.reshape(rows, width).astype(F32)
    back_low = back_result.astype(BF)
    grad_down_t = mm(back_low, hidden, 0, 0)
    back_hidden = jnp.dot(back_low, w_down_t, preferred_element_type=F32)
    _, gate_back = jax.vjp(gated, gate_part, up_part)
    back_gate, back_up = gate_back(back_hidden)
    back_gate_up = jnp.concatenate([back_gate, back_up], 1).astype(BF)
    grad_in = mm(normed_b, back_gate_up, 0, 0)
    back_normed_b = mm(back_gate_up, w_in, 1, 1)
    _, second_back = jax.vjp(rms_norm, middle, gain_two)
    back_middle_norm, grad_gain_two = second_back(back_normed_b)
    back_middle = back_result + back_middle_norm
    back_branch = back_middle.astype(BF)
    grad_out_t = mm(back_branch, attended, 0, 0)
    back_attended = jnp.dot(back_branch, w_out_t, preferred_element_type=F32).astype(BF)

    in_sum, out_sum, down_sum, output = scatter_all(3, [grad_in, grad_out_t, grad_down_t], result_low)
    squares = jnp.sum(in_sum * in_sum) + jnp.sum(out_sum * out_sum) + jnp.sum(down_sum * down_sum)

    back_q, part_k, part_v = attend_back(queries, kv, bias, attended, log_sums, back_attended, 256)
    part_kv = jnp.concatenate([part_k, part_v], 1).reshape(share, rows, 2 * width)
    arrived = return_call(dims, 4, part_kv)
    back_kv = lax.dynamic_index_in_dim(part_kv, part, 0, keepdims=False).astype(F32)
    for slot in range(share - 1):
        back_kv = back_kv + arrived[slot].astype(F32)
    back_project = jnp.concatenate([back_q, back_kv.astype(BF)], 1)
    grad_qkv = mm(normed_a, back_project, 0, 0)
    back_normed_a = mm(back_project, w_qkv, 1, 1)
    _, first_back = jax.vjp(rms_norm, tokens, gain_one)
    back_tokens, grad_gain_one = first_back(back_normed_a)
    back_rows = (back_middle + back_tokens).astype(BF).reshape(images, band_rows, width)
    grad_gains = jnp.pad(jnp.stack([grad_gain_one, grad_gain_two], 1), ((0, 0), (0, 126)))
    qkv_sum, gain_sum, back_input, total = scatter_all(5, [grad_qkv, grad_gains], back_rows, squares)
    grad_norm = jnp.sqrt(total[0, 0])
    factor = jnp.minimum(1.0, CLIP / grad_norm)
    shards = (
        qkv_sum,
        jnp.transpose(out_sum),
        in_sum,
        jnp.transpose(down_sum),
        jnp.transpose(gain_sum[:, :2]),
    )
    masters = (qkv_master, out_master, in_master, down_master, gain_master)
    firsts = (qkv_first, out_first, in_first, down_first, gain_first)
    seconds = (qkv_second, out_second, in_second, down_second, gain_second)
    updated = [
        adam_step(masters[j], shards[j], firsts[j], seconds[j], factor, RATES[j], DECAYS[j]) for j in range(5)
    ]
    return (
        (output, back_input, grad_norm)
        + tuple(updated[j][0] for j in range(5))
        + tuple(updated[j][1] for j in range(5))
        + tuple(updated[j][2] for j in range(5))
        + tuple(updated[j][0].astype(BF) for j in range(5))
    )


def solution(mesh):
    rows_split, columns_split = P(("img", "band"), None), P(None, ("img", "band"))
    weights = (rows_split, columns_split, rows_split, columns_split, columns_split)
    tokens = P("img", "band", None)
    return jax.shard_map(
        on_device,
        mesh=mesh,
        in_specs=(tokens, tokens, P("img")) + weights * 3,
        out_specs=(tokens, tokens, P()) + weights * 4,
        check_vma=False,
    )
```

time: 1780 us -> 685 us (0.38)
  waiting for transfers between devices: 945 us -> 0 us
  Pallas kernels: 0 us -> 513 us
  matrix products: 380 us -> 90.4 us
  local copies, waits for them, and re-layouts: 162 us -> 27.7 us
  blocking collectives: 123 us -> 0 us
  other arithmetic: 126 us -> 37.4 us
  loops' own time: 20.4 us -> 0 us
    reduce_scatter x6 -> x0, waiting for transfers between devices: 643 us -> none  [the longest x1 159 us: on_device(): lax.psum_scatter(grad_in, ('img', 'band'), scatter_dimension=0, tiled=True)]
    pallas_call x0 -> x8, Pallas kernels: none -> 513 us  [the longest x2 142 us: scatter_call(): pl.pallas_call(body, out_shape=shapes, in_specs=in_specs, out_specs=out_s...]
    all_gather x6 -> x0, waiting for transfers between devices: 302 us -> none  [the longest x1 117 us: on_device(): lax.all_gather(keys_local, 'band', axis=1, tiled=True)]
    dot_general x54 -> x12, matrix products: 380 us -> 90.4 us  [the longest x8 53.1 us: mm(): lax.dot_general(a, b, (((ca,), (cb,)), ((), ())), preferred_element_type=...]
    dynamic_slice x54 -> x1, local copies, waits for them, and re-layouts: 71.4 us -> 1.24 us  [on_device(): count = lax.dynamic_index_in_dim(valid_counts, image, 0, keepdims=False)]
    convert_element_type x18 -> x17, other arithmetic: 84.9 us -> 19.9 us  [the longest x5 5.23 us: on_device(): updated[j][0].astype(BF)]
    all_gather x1 -> x0, blocking collectives: 43 us -> none  [on_device(): lax.all_gather(gain_master.astype(jnp.bfloat16), ('img', 'band'), axis=1,...]
    psum x1 -> x0, blocking collectives: 40.1 us -> none  [on_device(): grad_norm = jnp.sqrt(lax.psum(squares, ('img', 'band')))]
  transfers between devices with their start and end apart: 12 -> 0, of which waited for: 11 -> 0; matrix products, arithmetic and copies ran while one was open for 12% -> 0% of each run, Pallas kernels for 0% -> 0%
where the time goes in v1:
time: 685 us; the launch traced here: 674 us
  Pallas kernels  513 us (75%)
  matrix products  90.4 us (13%)
  other arithmetic  37.4 us (5%)
  local copies, waits for them, and re-layouts  27.7 us (4%)
    pallas_call x2, Pallas kernels, scatter_call(): pl.pallas_call(body, out_shape=shapes, in_specs=in_specs, out_specs=out_s...  142 us
    pallas_call x2, Pallas kernels, gather_call(): pl.pallas_call(body, out_shape=shapes, in_specs=[ANY] * len(args), out_sp...  138 us
    pallas_call x1, Pallas kernels, share_call(): pl.pallas_call(body, out_shape=jax.ShapeDtypeStruct((share,) + block.shap...  96.8 us
    pallas_call x1, Pallas kernels, attend_back(): pl.pallas_call(functools.partial(attend_back_kernel, block=block), grid=(...  79.5 us
    dot_general x8, matrix products, mm(): lax.dot_general(a, b, (((ca,), (cb,)), ((), ())), preferred_element_type=...  53.1 us
    pallas_call x1, Pallas kernels, attend(): pl.pallas_call(functools.partial(attend_kernel, block=block), grid=(pairs...  50.5 us
    unnamed x94, local copies, waits for them, and re-layouts  14.3 us
    dot_general x1, matrix products, on_device(): back_hidden = jnp.dot(back_low, w_down_t, preferred_element_type=F32)  14.3 us

profile of v1, /device:TPU:0, one launch (start us, length us, event | category | flops | bytes accessed | tf_op | source)
XLA Modules:
  0.0 674.1 jit_solution(13750276346083912060)
XLA Ops:
  6.2 51.7 %gather_0.1 = (bf16[2,2,4,2,24,2304]{5,4,3,2,1,0:T(8,128)(2,1)}, bf16[2,2,4,2,24,128]{5,4,3,2,1,0:T(8,128)(2,1)}, bf16[4,256,768]{2,1,0:T(8,128)(2,1)}) custom-call(bf16[24,2304]{1,0:T(8,128)(2,1)} %convert_element_type.159.refs_0_, bf16[24,128]{1,0:T(8,128)(2,1)} %pad.9.refs_1_, bf16[4,256,768]{2,1,0:T(8,128)(2,1)} %refs_2_.1), custom_call_target="tpu_custom_call" | custom-call | tf_op jit(solution)/shard_map/gather_0/pallas_call | solution.py:333
  62.4 6.0 convolution_convert_fusion.1
  72.5 96.8 %share_keys.1 = bf16[2,1024,1536]{2,1,0:T(8,128)(2,1)} custom-call(bf16[1024,1536]{1,0:T(8,128)(2,1)} %slice.34.source), custom_call_target="tpu_custom_call" | custom-call | tf_op jit(solution)/shard_map/share_keys/pallas_call | solution.py:416
  169.3 2.7 slice.33.q_ref
  172.0 50.5 %attend.1 = (bf16[1024,768]{1,0:T(8,128)(2,1)}, f32[1024,768]{1,0:T(8,128)}) custom-call(bf16[1024,768]{1,0:T(8,128)(2,1)} %slice.33.q_ref, bf16[2048,1536]{1,0:T(8,128)(2,1)} %bitcast.93, bf16[2048,1536]{1,0:T(8,128)(2,1)} %bitcast.94, f32[1,2048]{1,0:T(1,128)} %select_n.28.bias_ref), custom_call_target="tpu_custom_call" | custom-call | flops 25769803776 | bytes 12582912 | tf_op jit(solution)/shard_map/attend/pallas_call | solution.py:485
  224.4 86.3 %gather_1.1 = (bf16[2,2,4,2,24,4096]{5,4,3,2,1,0:T(8,128)(2,1)}, bf16[2,2,4,2,24,768]{5,4,3,2,1,0:T(8,128)(2,1)}, bf16[2,2,4,2,24,2048]{5,4,3,2,1,0:T(8,128)(2,1)}, bf16[4,256,768]{2,1,0:T(8,128)(2,1)}) custom-call(bf16[24,4096]{1,0:T(8,128)(2,1)} %convert_element_type.170.refs_0_, bf16[24,768]{1,0:T(8,128)(2,1)} %convert_bitcast_fusion.1.refs_1_, ...), custom_call_target="tpu_custom_call" | custom-call | tf_op jit(solution)/shard_map/gather_1/pallas_call | solution.py:333
  310.7 5.0 multiply_reduce_fusion.2
  315.9 13.1 %fusion.42 = f32[1024,4096]{1,0:T(8,128)} fusion(bf16[768,4096]{1,0:T(8,128)(2,1)} %bitcast.112, f32[1024,768]{1,0:T(8,128)} %get-tuple-element.174, f32[768]{0:T(1024)S(1)} %convert_reduce_fusion, f32[1024]{0:T(1024)S(1)} %fusion.34), kind=kOutput, calls=%fused_computation.109 | convolution fusion | flops 6444810240 | bytes 26221568 | tf_op jit(solution)/shard_map/dot_general | solution.py:688
  330.9 14.3 %fusion.6 = (bf16[1024,2048]{1,0:T(8,128)(2,1)}, bf16[1024,2048]{1,0:T(8,128)(2,1)}, bf16[1024,2048]{1,0:T(8,128)(2,1)S(1)}) fusion(f32[1024,4096]{1,0:T(8,128)} %fusion.42, bf16[1024,768]{1,0:T(8,128)(2,1)S(1)} %bitcast.102, bf16[768,2048]{1,0:T(8,128)(2,1)S(1)} %bitcast.116), kind=kOutput, calls=%fused_computation.8 | convolution fusion | flops 3275751424 | bytes 34078720 | tf_op jit(solution)/shard_map/dot_general | solution.py:697
  345.3 4.8 multiply_convert_fusion.2
  350.1 11.5 %multiply_reduce_fusion = (bf16[768]{0:T(1024)(128)(2,1)S(1)}, f32[1024]{0:T(1024)S(1)}, f32[1024,768]{1,0:T(8,128)S(1)}) fusion(f32[1024,768]{1,0:T(8,128)S(1)} %copy-done.6, f32[1024]{0:T(1024)S(1)} %fusion.34, f32[768]{0:T(1024)S(1)} %convert_reduce_fusion, bf16[768,4096]{1,0:T(8,128)(2,1)} %bitcast.113, bf16[1024,2048]{1,0:T(8,128)(2,1)} %get-tuple-element.159, ...), kind=kOutput, calls=%fused_computation.42 | convolution fusion | flops 6463944704 | bytes 20984320 | tf_op jit(solution)/shard_map/dot_general | solution.py:454
  363.8 5.2 convolution_convert_fusion.3
  369.1 2.5 convolution_convert_fusion.5
  371.6 13.1 %convolution_convert_fusion = bf16[768,4096]{1,0:T(8,128)(2,1)} fusion(bf16[1024,2048]{1,0:T(8,128)(2,1)} %get-tuple-element.159, bf16[1024,2048]{1,0:T(8,128)(2,1)} %get-tuple-element.158, f32[1024,768]{1,0:T(8,128)S(1)} %copy-done.6, f32[768]{0:T(1024)S(1)} %convert_reduce_fusion, f32[1024]{0:T(1024)S(1)} %fusion.34), kind=kOutput, calls=%fused_computation.13 | convolution fusion | flops 6464733184 | bytes 17832960 | tf_op jit(solution)/shard_map/dot_general | solution.py:454
  384.6 81.7 %scatter_3.1 = (f32[24,4096]{1,0:T(8,128)}, f32[24,768]{1,0:T(8,128)}, f32[24,2048]{1,0:T(8,128)}, bf16[4,256,768]{2,1,0:T(8,128)(2,1)}) custom-call(bf16[2,2,4,2,24,4096]{5,4,3,2,1,0:T(8,128)(2,1)} %bitcast.97, bf16[2,2,4,2,24,768]{5,4,3,2,1,0:T(8,128)(2,1)} %bitcast.104, bf16[2,2,4,2,24,2048]{5,4,3,2,1,0:T(8,128)(2,1)} %bitcast.100, ...), custom_call_target="tpu_custom_call" | custom-call | tf_op jit(solution)/shard_map/scatter_3/pallas_call | solution.py:395
  473.7 3.8 convolution_convert_fusion.4.do_ref
  477.5 79.5 %attend_back.1 = (bf16[1024,768]{1,0:T(8,128)(2,1)}, bf16[2048,768]{1,0:T(8,128)(2,1)}, bf16[2048,768]{1,0:T(8,128)(2,1)}) custom-call(bf16[1024,768]{1,0:T(8,128)(2,1)} %slice.33.q_ref, bf16[2048,1536]{1,0:T(8,128)(2,1)} %bitcast.95, bf16[2048,1536]{1,0:T(8,128)(2,1)} %bitcast.96, f32[1,2048]{1,0:T(1,128)} %select_n.28.bias_ref, ...), custom_call_target="tpu_custom_call" | custom-call | flops 64424509440 | bytes 25165824 | tf_op jit(solution)/shard_map/attend_back/pallas_call | solution.py:547
  557.0 5.9 pad_maximum_fusion.1
  562.9 6.0 return_keys.1
  569.0 3.8 fusion.11
  573.8 5.7 fusion.19
  580.5 4.5 fusion.10
  585.0 5.3 convolution_convert_fusion.2
  590.4 60.8 %scatter_5.1 = (f32[24,2304]{1,0:T(8,128)}, f32[24,128]{1,0:T(8,128)}, bf16[4,256,768]{2,1,0:T(8,128)(2,1)}, f32[8,128]{1,0:T(8,128)}) custom-call(bf16[2,2,4,2,24,2304]{5,4,3,2,1,0:T(8,128)(2,1)} %bitcast.99, bf16[2,2,4,2,24,128]{5,4,3,2,1,0:T(8,128)(2,1)} %bitcast.105, bf16[4,256,768]{2,1,0:T(8,128)(2,1)} %bitcast.98, f32[8,128]{1,0:T(8,128)} %broadcast_in_dim.18.refs_3_), custom_call_target="tpu_custom_call" | custom-call | tf_op jit(solution)/shard_map/scatter_5/pallas_call | solution.py:395
  (144 shorter events, 48.2 us)
Async XLA Ops:
  171.9 50.5 %copy-start.11 = (f32[24,4096]{1,0:T(8,128)S(1)}, f32[24,4096]{1,0:T(8,128)}, u32[]{:S(2)}) copy-start(f32[24,4096]{1,0:T(8,128)} %param.23) | copy-start | bytes 1179652
  172.0 51.2 %copy-start.15 = (f32[2048,24]{0,1:T(8,128)S(1)}, f32[2048,24]{0,1:T(8,128)}, u32[]{:S(2)}) copy-start(f32[2048,24]{0,1:T(8,128)} %param.24) | copy-start | bytes 589828
  172.0 51.8 %copy-start.20 = (f32[768,24]{0,1:T(8,128)S(1)}, f32[768,24]{0,1:T(8,128)}, u32[]{:S(2)}) copy-start(f32[768,24]{0,1:T(8,128)} %param.22) | copy-start | bytes 221188
  315.9 14.0 %copy-start.3 = (bf16[4,256,768]{2,1,0:T(8,128)(2,1)S(1)}, bf16[4,256,768]{2,1,0:T(8,128)(2,1)}, u32[]{:S(2)}) copy-start(bf16[4,256,768]{2,1,0:T(8,128)(2,1)} %get-tuple-element.48) | copy-start | bytes 4718596
  330.9 14.3 %copy-start.6 = (f32[1024,768]{1,0:T(8,128)S(1)}, f32[1024,768]{1,0:T(8,128)}, u32[]{:S(2)}) copy-start(f32[1024,768]{1,0:T(8,128)} %get-tuple-element.174) | copy-start | bytes 9437188
  350.1 11.5 %copy-start.4 = (bf16[4,256,768]{2,1,0:T(8,128)(2,1)S(1)}, bf16[4,256,768]{2,1,0:T(8,128)(2,1)}, u32[]{:S(2)}) copy-start(bf16[4,256,768]{2,1,0:T(8,128)(2,1)} %get-tuple-element.48) | copy-start | bytes 4718596
  362.9 110.8 %copy-start.2 = (f32[1024,768]{1,0:T(8,128)}, f32[1024,768]{1,0:T(8,128)S(1)}, u32[]{:S(2)}) copy-start(f32[1024,768]{1,0:T(8,128)S(1)} %get-tuple-element.164) | copy-start | bytes 9437188
  590.3 63.0 %copy-start.33 = (f32[2,24]{1,0:T(2,128)S(1)}, f32[2,24]{1,0:T(2,128)}, u32[]{:S(2)}) copy-start(f32[2,24]{1,0:T(2,128)} %param.30) | copy-start | bytes 580
  590.3 76.1 %copy-start.16 = (f32[2048,24]{0,1:T(8,128)S(1)}, f32[2048,24]{0,1:T(8,128)}, u32[]{:S(2)}) copy-start(f32[2048,24]{0,1:T(8,128)} %param.24) | copy-start | bytes 589828
  590.3 76.1 %copy-start.17 = (f32[24,2048]{1,0:T(8,128)S(1)}, f32[24,2048]{1,0:T(8,128)}, u32[]{:S(2)}) copy-start(f32[24,2048]{1,0:T(8,128)} %get-tuple-element.58) | copy-start | bytes 589828
  590.3 76.1 %copy-start.26 = (f32[2048,24]{0,1:T(8,128)S(1)}, f32[2048,24]{0,1:T(8,128)}, u32[]{:S(2)}) copy-start(f32[2048,24]{0,1:T(8,128)} %param.29) | copy-start | bytes 589828
  590.3 76.1 %copy-start.27 = (f32[2048,24]{0,1:T(8,128)S(1)}, f32[2048,24]{0,1:T(8,128)}, u32[]{:S(2)}) copy-start(f32[2048,24]{0,1:T(8,128)} %param.34) | copy-start | bytes 589828
  590.3 77.1 %copy-start.12 = (f32[24,4096]{1,0:T(8,128)S(1)}, f32[24,4096]{1,0:T(8,128)}, u32[]{:S(2)}) copy-start(f32[24,4096]{1,0:T(8,128)} %param.23) | copy-start | bytes 1179652
  590.3 77.1 %copy-start.13 = (f32[24,4096]{1,0:T(8,128)S(1)}, f32[24,4096]{1,0:T(8,128)}, u32[]{:S(2)}) copy-start(f32[24,4096]{1,0:T(8,128)} %get-tuple-element.56) | copy-start | bytes 1179652
  590.3 77.1 %copy-start.18 = (f32[24,4096]{1,0:T(8,128)S(1)}, f32[24,4096]{1,0:T(8,128)}, u32[]{:S(2)}) copy-start(f32[24,4096]{1,0:T(8,128)} %param.28) | copy-start | bytes 1179652
  590.4 77.1 %copy-start.19 = (f32[24,4096]{1,0:T(8,128)S(1)}, f32[24,4096]{1,0:T(8,128)}, u32[]{:S(2)}) copy-start(f32[24,4096]{1,0:T(8,128)} %param.33) | copy-start | bytes 1179652
  651.1 17.6 %copy-start.21 = (f32[768,24]{0,1:T(8,128)S(1)}, f32[768,24]{0,1:T(8,128)}, u32[]{:S(2)}) copy-start(f32[768,24]{0,1:T(8,128)} %param.22) | copy-start | bytes 221188
  651.1 17.6 %copy-start.22 = (f32[24,768]{1,0:T(8,128)S(1)}, f32[24,768]{1,0:T(8,128)}, u32[]{:S(2)}) copy-start(f32[24,768]{1,0:T(8,128)} %get-tuple-element.57) | copy-start | bytes 221188
  651.2 17.5 %copy-start.28 = (f32[768,24]{0,1:T(8,128)S(1)}, f32[768,24]{0,1:T(8,128)}, u32[]{:S(2)}) copy-start(f32[768,24]{0,1:T(8,128)} %param.27) | copy-start | bytes 221188
  651.2 17.5 %copy-start.29 = (f32[768,24]{0,1:T(8,128)S(1)}, f32[768,24]{0,1:T(8,128)}, u32[]{:S(2)}) copy-start(f32[768,24]{0,1:T(8,128)} %param.32) | copy-start | bytes 221188
  651.2 18.3 %copy-start.14 = (f32[24,2304]{1,0:T(8,128)S(1)}, f32[24,2304]{1,0:T(8,128)}, u32[]{:S(2)}) copy-start(f32[24,2304]{1,0:T(8,128)} %param.21) | copy-start | bytes 663556
  651.2 18.3 %copy-start.23 = (f32[24,2304]{1,0:T(8,128)S(1)}, f32[24,2304]{1,0:T(8,128)}, u32[]{:S(2)}) copy-start(f32[24,2304]{1,0:T(8,128)} %param.26) | copy-start | bytes 663556
  651.2 18.2 %copy-start.24 = (f32[24,2304]{1,0:T(8,128)S(1)}, f32[24,2304]{1,0:T(8,128)}, u32[]{:S(2)}) copy-start(f32[24,2304]{1,0:T(8,128)} %param.31) | copy-start | bytes 663556
  651.2 18.2 %copy-start.25 = (f32[24,2304]{1,0:T(8,128)S(1)}, f32[24,2304]{1,0:T(8,128)}, u32[]{:S(2)}) copy-start(f32[24,2304]{1,0:T(8,128)} %get-tuple-element.61) | copy-start | bytes 663556
  (17 other events, 64.3 us)

commit v2 on v1

v2 whole, which is shorter than its diff:
```python
import functools

import jax
import jax.numpy as jnp
from jax import lax
from jax.experimental import pallas as pl
from jax.experimental.pallas import tpu as pltpu
from jax.sharding import PartitionSpec as P

HEADS = 12
HEAD_DIM = 64
PAIR = 2 * HEAD_DIM
STEP = 10
EPS = 1e-06
NEG = -1000000000.0
SCALE = 0.125
CLIP = 1.0
BETA_ONE = 0.9
BETA_TWO = 0.999
ADAM_EPS = 1e-08
RATES = (0.06, 0.5, 0.06, 0.04, 0.5)
DECAYS = (0.1, 0.1, 0.1, 0.1, 0.0)
BF = jnp.bfloat16
F32 = jnp.float32
MESH = pl.DeviceIdType.MESH
ANY = pl.BlockSpec(memory_space=pl.ANY)
MIB = 2**20


class Net:
    def __init__(self, dims, send, recv, local):
        self.dims = dims
        big_y, big_x, big_z, share = dims
        img, band = lax.axis_index("img"), lax.axis_index("band")
        self.y, self.x = img // big_x, img % big_x
        self.z, self.c = band // 2, band % 2
        self.twin = 1 - self.c
        image, self.part = band // share, band % share
        self.image, self.images = image, 2 * big_z // share
        self.send, self.recv, self.local = send, recv, local
        self.used, self.used_local = 0, 0
        self.lines = {}
        for name, size in zip("yxzc", (big_y, big_x, big_z, 2)):
            places = []
            for d in range(1, size):
                at = dict(y=self.y, x=self.x, z=self.z, c=self.c)
                at[name] = lax.rem(at[name] + d, size)
                places.append((at[name], (at["y"] * big_x + at["x"], at["z"] * 2 + at["c"])))
            self.lines[name] = places
        self.lines["image"] = []
        for d in range(1, self.images):
            other = lax.rem(image + d, self.images)
            self.lines["image"].append((other, (img, other * share + self.part)))
        self.lines["share"] = []
        for d in range(1, share):
            other = lax.rem(self.part + d, share)
            self.lines["share"].append((other, (img, image * share + other)))

    def line(self, name):
        return self.lines[name]

    def greet(self, kinds):
        barrier = pltpu.get_barrier_semaphore()
        count = 0
        for kind in kinds:
            for _, target in self.lines[kind]:
                pl.semaphore_signal(barrier, inc=1, device_id=target, device_id_type=MESH)
            count += len(self.lines[kind])
        pl.semaphore_wait(barrier, count)

    def copy(self, source, target_ref, target):
        made = self.plan(source, target_ref, target)
        made.start()
        return made

    def plan(self, source, target_ref, target):
        self.used += 1
        return Move(source, target_ref, self.send, self.recv, self.used - 1, target)

    def local_copy(self, source, target_ref):
        self.used_local += 1
        made = Move(source, target_ref, None, self.local, self.used_local - 1, None)
        made.start()
        return made


class Part:
    def __init__(self, ref, index=None):
        self.ref, self.index = ref, index

    def __getitem__(self, index):
        return Part(self.ref, index)

    def view(self):
        return self.ref if self.index is None else self.ref.at[self.index]


class Move:
    def __init__(self, source, target_ref, send, recv, at, target):
        self.source, self.target_ref = source, target_ref
        self.send, self.recv, self.at, self.target = send, recv, at, target

    def build(self):
        if self.target is None:
            return pltpu.make_async_copy(self.source.view(), self.target_ref.view(), self.recv.at[self.at])
        return pltpu.make_async_remote_copy(
            src_ref=self.source.view(),
            dst_ref=self.target_ref.view(),
            send_sem=self.send.at[self.at],
            recv_sem=self.recv.at[self.at],
            device_id=self.target,
            device_id_type=MESH,
        )

    def start(self):
        self.build().start()

    def wait(self):
        self.build().wait()

    def wait_recv(self):
        self.build().wait_recv()

    def wait_send(self):
        self.build().wait_send()


def drive(tasks):
    waiting = list(tasks)
    turn = 0
    while waiting:
        left = []
        for start, task in waiting:
            if start <= turn:
                try:
                    next(task)
                except StopIteration:
                    continue
            left.append((start, task))
        waiting = left
        turn += 1


def exchange_images(net, source, target):
    moves = [net.copy(Part(source)[other], Part(target)[net.image], dev) for other, dev in net.line("image")]
    own = net.local_copy(Part(source)[net.image], Part(target)[net.image])
    yield
    yield
    yield
    yield
    for move in moves:
        move.wait_recv()
    own.wait()
    for move in moves:
        move.wait_send()


def gather(net, source, target, columns, order):
    cols = pl.ds(*columns)
    y, x, z, c = net.y, net.x, net.z, net.c
    own = net.local_copy(Part(source)[:, cols], Part(target)[y, x, z, c, :, cols])
    sent = [net.copy(Part(source)[:, cols], Part(target)[y, x, z, c, :, cols], dev) for _, dev in net.line("z")]
    yield
    own.wait()
    for move in sent:
        move.wait_recv()
    part = Part(target)[y, x, :, c, :, cols]
    moves = [net.copy(part, part, dev) for _, dev in net.line(order[0])]
    sent += moves
    yield
    for move in moves:
        move.wait_recv()
    part = Part(target)[y, :, :, c, :, cols] if order[0] == "x" else Part(target)[:, x, :, c, :, cols]
    moves = [net.copy(part, part, dev) for _, dev in net.line(order[1])]
    sent += moves
    yield
    for move in moves:
        move.wait_recv()
    part = Part(target)[:, :, :, c, :, cols]
    moves = [net.copy(part, part, dev) for _, dev in net.line("c")]
    sent += moves
    yield
    for move in moves:
        move.wait_recv()
    for move in sent:
        move.wait_send()


def gather_copies(dims):
    return dims[0] + dims[1] + dims[2] - 3 + 1


def scatter(net, grad, held, from_core, from_first, from_second, from_z, out, squares, columns, order):
    big_y, big_x, big_z, _ = net.dims
    cols = pl.ds(*columns)
    y, x, z, c = net.y, net.x, net.z, net.c
    sent = []
    (_, twin), = net.line("c")
    moves = [net.copy(Part(grad)[:, :, :, net.twin, :, cols], Part(from_core), twin)]
    sent += moves
    own = net.local_copy(Part(grad)[:, :, :, c, :, cols], Part(held))
    yield
    own.wait()
    moves[0].wait_recv()

    def first_add(at, _):
        a, b, d = at // (big_x * big_z), (at // big_z) % big_x, at % big_z
        held[a, b, d] = (held[a, b, d].astype(F32) + from_core[a, b, d].astype(F32)).astype(BF)
        return 0

    lax.fori_loop(0, big_y * big_x * big_z, first_add, 0)
    moves = []
    for slot, (other, dev) in enumerate(net.line(order[0])):
        part = Part(held)[:, other] if order[0] == "x" else Part(held)[other]
        moves.append(net.copy(part, Part(from_first)[slot], dev))
    sent += moves
    yield
    for move in moves:
        move.wait_recv()
    left = big_y if order[0] == "x" else big_x

    def second_add(at, _):
        a, d = at // big_z, at % big_z
        place = (a, x, d) if order[0] == "x" else (y, a, d)
        total = held[place].astype(F32)
        for slot in range(len(moves)):
            total = total + from_first[slot, a, d].astype(F32)
        held[place] = total.astype(BF)
        return 0

    lax.fori_loop(0, left * big_z, second_add, 0)
    moves = []
    for slot, (other, dev) in enumerate(net.line(order[1])):
        part = Part(held)[other, x] if order[1] == "y" else Part(held)[y, other]
        moves.append(net.copy(part, Part(from_second)[slot], dev))
    sent += moves
    yield
    for move in moves:
        move.wait_recv()

    def third_add(d, _):
        total = held[y, x, d].astype(F32)
        for slot in range(len(moves)):
            total = total + from_second[slot, d].astype(F32)
        held[y, x, d] = total.astype(BF)
        return 0

    lax.fori_loop(0, big_z, third_add, 0)
    moves = []
    for slot, (other, dev) in enumerate(net.line("z")):
        moves.append(net.copy(Part(held)[y, x, other], Part(from_z)[slot], dev))
    sent += moves
    yield
    for move in moves:
        move.wait_recv()
    total = held[y, x, z].astype(F32)
    for slot in range(len(moves)):
        total = total + from_z[slot].astype(F32)
    out[:, columns[0] : columns[0] + columns[1]] = total
    tile = squares[...]
    for a in range(total.shape[0] // 8):
        for b in range(columns[1] // 128):
            piece = total[8 * a : 8 * a + 8, 128 * b : 128 * b + 128]
            tile = tile + piece * piece
    squares[...] = tile
    for move in sent:
        move.wait_send()


def scatter_scratch(dims, rows, columns, order):
    big_y, big_x, big_z, _ = dims
    width = columns[1]
    ahead, left = (big_x, big_y) if order[0] == "x" else (big_y, big_x)
    return [
        pltpu.VMEM((big_y, big_x, big_z, rows, width), BF),
        pltpu.VMEM((big_y, big_x, big_z, rows, width), BF),
        pltpu.VMEM((ahead - 1, left, big_z, rows, width), BF),
        pltpu.VMEM((left - 1, big_z, rows, width), BF),
        pltpu.VMEM((big_z - 1, rows, width), BF),
    ]


def sum_tiles(net, tile, slots):
    first = 0
    for name in "cxyz":
        places = net.line(name)
        me = dict(y=net.y, x=net.x, z=net.z, c=net.c)[name]
        size = len(places) + 1
        slots[first + me] = tile[...]
        moves = [net.copy(Part(tile), Part(slots)[first + me], dev) for _, dev in places]
        for move in moves:
            move.wait_recv()
        for move in moves:
            move.wait_send()
        total = slots[first]
        for d in range(1, size):
            total = total + slots[first + d]
        tile[...] = total
        first += size


def sems(count):
    return pltpu.SemaphoreType.DMA((max(count, 1),))


def halves(width):
    units = width // 128
    low = (units + 1) // 2 * 128
    if low == width:
        return [((0, width), "xy")]
    return [((0, low), "xy"), ((low, width - low), "yx")]


def gather_call(dims, name, number, blocks, images=None):
    big_y, big_x, big_z, share = dims
    parts = [halves(block.shape[1]) for block in blocks]
    copies = sum(len(p) for p in parts) * gather_copies(dims)
    local = sum(len(p) for p in parts)
    n = len(blocks)
    with_images = images is not None
    if with_images:
        copies += images.shape[0] - 1
        local += 1

    def body(*refs):
        ins, rest = refs[: n + with_images], refs[n + with_images :]
        outs, (send, recv, local_sem) = rest[: n + with_images], rest[n + with_images :]
        net = Net(dims, send, recv, local_sem)
        net.greet("zxyc" if not with_images else ["z", "x", "y", "c", "image"])
        tasks = []
        for j in range(n):
            for columns, order in parts[j]:
                tasks.append((0, gather(net, ins[j], outs[j], columns, order)))
        if with_images:
            tasks.append((0, exchange_images(net, ins[n], outs[n])))
        drive(tasks)

    args = list(blocks) + ([images] if with_images else [])
    shapes = [jax.ShapeDtypeStruct((big_y, big_x, big_z, 2) + b.shape, b.dtype) for b in blocks]
    if with_images:
        shapes.append(jax.ShapeDtypeStruct(images.shape, images.dtype))
    return pl.pallas_call(
        body,
        out_shape=shapes,
        in_specs=[ANY] * len(args),
        out_specs=[ANY] * len(shapes),
        scratch_shapes=[sems(copies), sems(copies), sems(local)],
        compiler_params=pltpu.CompilerParams(collective_id=number, has_side_effects=True),
        name=name,
    )(*args)


def scatter_call(dims, name, number, grads, images, squares):
    big_y, big_x, big_z, _ = dims
    rows = grads[0].shape[4]
    parts = [(j, columns, order) for j, g in enumerate(grads) for columns, order in halves(g.shape[5])]
    copies = (len(parts) + 1) * gather_copies(dims) + images.shape[0] - 1
    local = len(parts) + 1
    n = len(grads)
    scratch = [sems(copies), sems(copies), sems(local)]
    for _, columns, order in parts:
        scratch += scatter_scratch(dims, rows, columns, order)
    scratch += [pltpu.VMEM((8, 128), F32), pltpu.VMEM((2 + big_x + big_y + big_z, 8, 128), F32)]

    def body(*refs):
        ins, outs, rest = refs[: n + 2], refs[n + 2 : 2 * n + 4], refs[2 * n + 4 :]
        tile, slots = rest[3 + 5 * len(parts) :]
        net = Net(dims, *rest[:3])
        net.greet(["z", "x", "y", "c", "image"])
        tile[...] = ins[n + 1][...]
        tasks = []
        for k, (j, columns, order) in enumerate(parts):
            buffers = rest[3 + 5 * k : 8 + 5 * k]
            tasks.append((0, scatter(net, ins[j], *buffers, outs[j], tile, columns, order)))
        tasks.append((0, exchange_images(net, ins[n], outs[n])))
        drive(tasks)
        sum_tiles(net, tile, slots)
        outs[n + 1][...] = jnp.broadcast_to(jnp.sum(tile[...], keepdims=True), (8, 128))

    vmem = pl.BlockSpec(memory_space=pltpu.VMEM)
    shapes = [jax.ShapeDtypeStruct((rows, g.shape[5]), F32) for g in grads]
    shapes += [jax.ShapeDtypeStruct(images.shape, images.dtype), jax.ShapeDtypeStruct((8, 128), F32)]
    return pl.pallas_call(
        body,
        out_shape=shapes,
        in_specs=[ANY] * (n + 1) + [vmem],
        out_specs=[vmem] * n + [ANY, vmem],
        scratch_shapes=scratch,
        compiler_params=pltpu.CompilerParams(
            collective_id=number, has_side_effects=True, vmem_limit_bytes=60 * MIB
        ),
        name=name,
    )(*grads, images, squares)


def mm(a, b, ca, cb):
    return lax.dot_general(a, b, (((ca,), (cb,)), ((), ())), preferred_element_type=F32)


def at_turn(turn, events):
    for when in sorted(events):

        @pl.when(turn == when)
        def _(when=when):
            for task in events[when]:
                next(task, None)


def schedule(tasks, turns, last):
    events, tail = {}, []
    for task, when in zip(tasks, turns):
        for turn in when:
            if turn < last:
                events.setdefault(turn, []).append(task)
            else:
                tail.append(task)
    return events, tail


def lanes_of(h):
    lane = lax.broadcasted_iota(jnp.int32, (1, PAIR), 1) < HEAD_DIM
    return lane if h == 0 else ~lane


def attend(dims, number, project, bias, block, weights):
    big_y, big_x, big_z, share = dims
    rows, width = project.shape[0], project.shape[1] // 3
    pairs = width // PAIR
    others = share - 1
    blocks = rows // block
    n = len(weights)
    parts = [(j, columns, order) for j, w in enumerate(weights) for columns, order in halves(w.shape[1])]
    copies = len(parts) * gather_copies(dims) + others * 2 * pairs
    per_turn = max(blocks // 4, 1)

    def body(*refs):
        q_ref, k_ref, v_ref, project_ref, bias_ref = refs[:5]
        blocks_in, refs = refs[5 : 5 + n], refs[5 + n :]
        o_ref, l_ref, kv_out, refs = refs[0], refs[1], refs[2], refs[3:]
        gathered, (kv_held, send, recv, local) = refs[:n], refs[n:]
        h = pl.program_id(0)
        net = Net(dims, send, recv, local)

        def move_keys(j):
            moves = []
            for slot, (_, target) in enumerate(net.line("share")):
                source = Part(project_ref)[:, pl.ds(width + PAIR * j, PAIR)]
                moves.append(net.plan(source, Part(kv_held)[others - 1 - slot, j], target))
            return moves

        key_moves = [move_keys(j) for j in range(2 * pairs)]
        keep = Move(Part(kv_held), Part(kv_out), None, local, len(parts), None)
        tasks = [gather(net, blocks_in[j], gathered[j], columns, order) for j, columns, order in parts]
        turns = []
        for j, columns, order in parts:
            turns.append([GATHER_TURNS[j][0]] + [t for t in GATHER_TURNS[j][1:]])
        events, tail = schedule(tasks, turns, 4 * pairs)

        @pl.when(h == 0)
        def _():
            net.greet(["z", "x", "y", "c"] + (["share"] if share > 2 else []))
            for j in range(pairs):
                for move in key_moves[j] + key_moves[j + pairs]:
                    move.start()

        for j in range(pairs):

            @pl.when(h == j)
            def _(j=j):
                for move in key_moves[j] + key_moves[j + pairs]:
                    move.wait_recv()
                if j == pairs - 1:
                    keep.start()

        def step(i, _):
            at_turn(h * 4 + i // per_turn, events)
            at = pl.ds(pl.multiple_of(i * block, block), block)
            k = jnp.concatenate([k_ref[...]] + [kv_held[s, h] for s in range(others)], 0)
            v = jnp.concatenate([v_ref[...]] + [kv_held[s, h + pairs] for s in range(others)], 0)
            q = q_ref[at, :] * jnp.asarray(SCALE, BF)
            mixed, logs = [], []
            for half in range(2):
                scores = mm(jnp.where(lanes_of(half), q, jnp.zeros_like(q)), k, 1, 1) + bias_ref[...]
                highest = jnp.max(scores, -1, keepdims=True)
                powers = jnp.exp(scores - highest)
                total = jnp.sum(powers, -1, keepdims=True)
                mixed.append(mm(powers.astype(BF), v, 1, 0) / total)
                logs.append(highest + jnp.log(total))
            o_ref[at, :] = jnp.where(lanes_of(0), mixed[0], mixed[1]).astype(BF)
            l_ref[at, :] = jnp.where(lanes_of(0), logs[0], logs[1])
            return 0

        lax.fori_loop(0, blocks, step, 0)

        @pl.when(h == pairs - 1)
        def _():
            for task in tail:
                next(task, None)
            for moves in key_moves:
                for move in moves:
                    move.wait_send()
            keep.wait()

    column = lambda first: pl.BlockSpec((rows, PAIR), lambda h: (0, h + first))
    keys = rows * share
    shapes = [
        jax.ShapeDtypeStruct((rows, width), BF),
        jax.ShapeDtypeStruct((rows, width), F32),
        jax.ShapeDtypeStruct((others, 2 * pairs, rows, PAIR), BF),
    ] + [jax.ShapeDtypeStruct((big_y, big_x, big_z, 2) + w.shape, w.dtype) for w in weights]
    return pl.pallas_call(
        body,
        grid=(pairs,),
        in_specs=[column(0), column(pairs), column(2 * pairs), ANY, pl.BlockSpec((1, keys), lambda h: (0, 0))]
        + [ANY] * n,
        out_specs=[column(0), column(0), ANY] + [ANY] * n,
        out_shape=shapes,
        scratch_shapes=[
            pltpu.VMEM((others, 2 * pairs, rows, PAIR), BF),
            sems(copies),
            sems(copies),
            sems(len(parts) + 1),
        ],
        compiler_params=pltpu.CompilerParams(
            collective_id=number, has_side_effects=True, vmem_limit_bytes=56 * MIB
        ),
        cost_estimate=pl.CostEstimate(
            flops=16 * rows * keys * width, bytes_accessed=8 * keys * width, transcendentals=rows * keys * HEADS
        ),
        name="attend",
    )(project, project, project, project, bias, *weights)


GATHER_TURNS = ((0, 8, 11, 17, 21), (1, 4, 6, 9, 12), (3, 12, 15, 21, 24))
SCATTER_TURNS = ((0, 2, 8, 14, 20), (1, 3, 9, 15, 21), (1, 4, 11, 17, 24))


def attend_back(dims, number, project, kv, bias, mixed, logs, back, block, grads):
    big_y, big_x, big_z, share = dims
    rows, width = mixed.shape
    pairs = width // PAIR
    others = share - 1
    blocks = rows // block
    keys = rows * share
    n = len(grads)
    parts = [(j, columns, order) for j, g in enumerate(grads) for columns, order in halves(g.shape[5])]
    copies = len(parts) * gather_copies(dims) + others * 2 * pairs
    per_turn = max(blocks // 4, 1)

    def body(*refs):
        q_ref, k_ref, v_ref, k_other, v_other, bias_ref, mixed_ref, logs_ref, back_ref = refs[:9]
        grads_in, refs = refs[9 : 9 + n], refs[9 + n :]
        out_ref, sums, squares, refs = refs[0], refs[1 : 1 + n], refs[1 + n], refs[2 + n :]
        dk_sum, dv_sum, dk_own, dv_own, parted, arrived, bias_column = refs[:7]
        send, recv, local = refs[7:10]
        buffers = refs[10:]
        h = pl.program_id(0)
        net = Net(dims, send, recv, local)

        def move_keys(j):
            moves = []
            for slot, (_, target) in enumerate(net.line("share")):
                moves.append(net.plan(Part(parted)[slot, j], Part(arrived)[others - 1 - slot, j], target))
            return moves

        key_moves = [move_keys(j) for j in range(2 * pairs)]
        tasks = [
            scatter(net, grads_in[j], *buffers[5 * k : 5 * k + 5], sums[j], squares, columns, order)
            for k, (j, columns, order) in enumerate(parts)
        ]
        events, tail = schedule(tasks, [SCATTER_TURNS[j] for j, _, _ in parts], 4 * pairs)

        @pl.when(h == 0)
        def _():
            net.greet(["z", "x", "y", "c"] + (["share"] if share > 2 else []))
            squares[...] = jnp.zeros_like(squares)
            bias_column[...] = jnp.transpose(jnp.broadcast_to(bias_ref[...], (PAIR, keys)))

        dk_sum[...] = jnp.zeros_like(dk_sum)
        dv_sum[...] = jnp.zeros_like(dv_sum)

        def step(i, _):
            at_turn(h * 4 + i // per_turn, events)
            at = pl.ds(pl.multiple_of(i * block, block), block)
            k = jnp.concatenate([k_ref[...]] + [k_other[s, 0] for s in range(others)], 0)
            v = jnp.concatenate([v_ref[...]] + [v_other[s, 0] for s in range(others)], 0)
            q, do = q_ref[at, :] * jnp.asarray(SCALE, BF), back_ref[at, :]
            lse = jnp.transpose(logs_ref[at, :])
            products = jnp.transpose(do.astype(F32) * mixed_ref[at, :].astype(F32))
            dqs, dks, dvs = [], [], []
            for half in range(2):
                low, high = half * HEAD_DIM, (half + 1) * HEAD_DIM
                q_h = jnp.where(lanes_of(half), q, jnp.zeros_like(q))
                do_h = jnp.where(lanes_of(half), do, jnp.zeros_like(do))
                row_dots = jnp.sum(products[low:high, :], 0, keepdims=True)
                chances = jnp.exp(mm(k, q_h, 1, 1) + bias_column[:, :1] - lse[low : low + 1, :])
                slopes = mm(v, do_h, 1, 1)
                scores = (chances * (slopes - row_dots)).astype(BF)
                dqs.append(mm(scores, k, 0, 0))
                dks.append(mm(scores, q_h, 1, 0))
                dvs.append(mm(chances.astype(BF), do_h, 1, 0))
            dq = (jnp.where(lanes_of(0), dqs[0], dqs[1]) * SCALE).astype(BF)
            out_ref[at, pl.ds(pl.multiple_of(h * PAIR, PAIR), PAIR)] = dq
            dk_sum[...] += dks[0] + dks[1]
            dv_sum[...] += dvs[0] + dvs[1]
            return 0

        lax.fori_loop(0, blocks, step, 0)

        def finish(j):
            for move in key_moves[j] + key_moves[j + pairs]:
                move.wait_recv()
            for first, kept, total in ((0, j, dk_own), (pairs, j + pairs, dv_own)):
                value = total[...]
                for slot in range(others):
                    value = value + arrived[slot, kept].astype(F32)
                out_ref[:, width + PAIR * kept : width + PAIR * (kept + 1)] = value.astype(BF)

        for j in range(pairs):

            @pl.when(h == j)
            def _(j=j):
                if j > 0:
                    finish(j - 1)
                dk_own[...] = dk_sum[0:rows, :]
                dv_own[...] = dv_sum[0:rows, :]
                for slot in range(others):
                    away = slice(rows * (slot + 1), rows * (slot + 2))
                    parted[slot, j] = dk_sum[away, :].astype(BF)
                    parted[slot, j + pairs] = dv_sum[away, :].astype(BF)
                for move in key_moves[j] + key_moves[j + pairs]:
                    move.start()
                if j == pairs - 1:
                    for task in tail:
                        next(task, None)
                    finish(j)
                    for moves in key_moves:
                        for move in moves:
                            move.wait_send()

    column = lambda first: pl.BlockSpec((rows, PAIR), lambda h: (0, h + first))
    other = lambda first: pl.BlockSpec((others, 1, rows, PAIR), lambda h: (0, h + first, 0, 0))
    whole = lambda shape: pl.BlockSpec(shape, lambda h: (0,) * len(shape))
    shard = grads[0].shape[4] if n else 0
    shapes = (
        [jax.ShapeDtypeStruct((rows, 3 * width), BF)]
        + [jax.ShapeDtypeStruct((shard, g.shape[5]), F32) for g in grads]
        + [jax.ShapeDtypeStruct((8, 128), F32)]
    )
    scratch = [
        pltpu.VMEM((keys, PAIR), F32),
        pltpu.VMEM((keys, PAIR), F32),
        pltpu.VMEM((rows, PAIR), F32),
        pltpu.VMEM((rows, PAIR), F32),
        pltpu.VMEM((others, 2 * pairs, rows, PAIR), BF),
        pltpu.VMEM((others, 2 * pairs, rows, PAIR), BF),
        pltpu.VMEM((keys, PAIR), F32),
        sems(copies),
        sems(copies),
        sems(len(parts)),
    ]
    for j, columns, order in parts:
        scratch += scatter_scratch(dims, shard, columns, order)
    return pl.pallas_call(
        body,
        grid=(pairs,),
        in_specs=[
            column(0),
            column(pairs),
            column(2 * pairs),
            other(0),
            other(pairs),
            whole((1, keys)),
            column(0),
            column(0),
            column(0),
        ]
        + [ANY] * n,
        out_specs=[whole(s.shape) for s in shapes],
        out_shape=shapes,
        scratch_shapes=scratch,
        compiler_params=pltpu.CompilerParams(
            collective_id=number, has_side_effects=True, vmem_limit_bytes=60 * MIB
        ),
        cost_estimate=pl.CostEstimate(
            flops=40 * rows * keys * width, bytes_accessed=16 * keys * width, transcendentals=rows * keys * HEADS
        ),
        name="attend_back",
    )(project, project, project, kv, kv, bias, mixed, logs, back, *grads)


def rms_norm(value, gain):
    return value * lax.rsqrt(jnp.mean(value * value, -1, keepdims=True) + EPS) * gain


def gated(gate_part, up_part):
    return jax.nn.gelu(gate_part, approximate=True) * up_part


def adam_step(master, grad, first, second, factor, rate, decay):
    clipped = factor * grad
    first_new = BETA_ONE * first + (1.0 - BETA_ONE) * clipped
    second_new = BETA_TWO * second + (1.0 - BETA_TWO) * clipped * clipped
    corrected = first_new / (1.0 - BETA_ONE**STEP)
    spread = jnp.sqrt(second_new / (1.0 - BETA_TWO**STEP)) + ADAM_EPS
    master_new = master - rate * (corrected / spread + decay * master)
    return (master_new, first_new, second_new)


def grid_of(n_img):
    big_y = max(d for d in range(1, n_img + 1) if n_img % d == 0 and d * d <= n_img)
    return big_y, n_img // big_y


def on_device(
    patches,
    cotangent,
    valid_counts,
    qkv_master,
    out_master,
    in_master,
    down_master,
    gain_master,
    qkv_first,
    out_first,
    in_first,
    down_first,
    gain_first,
    qkv_second,
    out_second,
    in_second,
    down_second,
    gain_second,
):
    images, band_rows, width = patches.shape
    n_img, n_band = lax.axis_size("img"), lax.axis_size("band")
    share = n_band // images
    big_y, big_x = grid_of(n_img)
    dims = (big_y, big_x, n_band // 2, share)
    rows = images * band_rows
    shard = qkv_master.shape[0]
    own_comm = shard % 8 == 0
    both = ("img", "band")

    places = [[s * share + r for s in range(images)] for r in range(share)]

    def exchange(chunks):
        return lax.all_to_all(chunks, "band", 0, 0, axis_index_groups=places, tiled=True)

    def flat(got):
        return [g.reshape(width, g.shape[-1]) for g in got]

    def blocks_of(grads):
        return [g.astype(BF).reshape(dims[:3] + (2, shard, g.shape[1])) for g in grads]

    gains_block = jnp.pad(jnp.transpose(gain_master).astype(BF), ((0, 0), (0, 126)))
    early = [qkv_master.astype(BF), gains_block]
    late = [
        jnp.transpose(out_master).astype(BF),
        in_master.astype(BF),
        jnp.transpose(down_master).astype(BF),
    ]
    if own_comm:
        w_qkv, gains, tokens_low = gather_call(dims, "gather", 0, early, patches)
        w_qkv, gains = flat([w_qkv, gains])
    else:
        w_qkv, gains = [lax.all_gather(b, both, axis=0, tiled=True) for b in early]
        tokens_low = exchange(patches)
    gain_one = gains[:, 0].astype(F32)
    gain_two = gains[:, 1].astype(F32)

    band = lax.axis_index("band")
    image, part = band // share, band % share
    count = lax.dynamic_index_in_dim(valid_counts, image, 0, keepdims=False)
    own_places = (
        (jnp.arange(images, dtype=jnp.int32)[:, None] * share + part) * band_rows
        + jnp.arange(band_rows, dtype=jnp.int32)[None, :]
    ).reshape(rows, 1)
    row_keep = (own_places < count).astype(F32)
    key_places = (
        (
            jnp.arange(images, dtype=jnp.int32)[None, :, None] * share
            + lax.rem(part + jnp.arange(share, dtype=jnp.int32), share)[:, None, None]
        )
        * band_rows
        + jnp.arange(band_rows, dtype=jnp.int32)[None, None, :]
    ).reshape(1, share * rows)
    bias = jnp.where(key_places < count, 0.0, NEG).astype(F32)

    tokens = tokens_low.reshape(rows, width).astype(F32)
    normed_a = rms_norm(tokens, gain_one).astype(BF)
    project = jnp.dot(normed_a, w_qkv, preferred_element_type=F32).astype(BF)
    attended, log_sums, kv, *late_all = attend(dims, 1, project, bias, 256, late if own_comm else [])
    if own_comm:
        w_out_t, w_in, w_down_t = flat(late_all)
    else:
        w_out_t, w_in, w_down_t = [lax.all_gather(b, both, axis=0, tiled=True) for b in late]
    hidden_units = w_down_t.shape[1]
    cotangent_later, attended = lax.optimization_barrier((cotangent, attended))
    cotangent_low = exchange(cotangent_later)

    middle = tokens + mm(attended, w_out_t, 1, 1)
    normed_b = rms_norm(middle, gain_two).astype(BF)
    gate_up = jnp.dot(normed_b, w_in, preferred_element_type=F32)
    gate_part = gate_up[:, :hidden_units]
    up_part = gate_up[:, hidden_units:]
    hidden = gated(gate_part, up_part).astype(BF)
    result = row_keep * (middle + mm(hidden, w_down_t, 1, 1))
    result_low = result.astype(BF).reshape(images, band_rows, width)
    back_result = row_keep * cotangent_low.reshape(rows, width).astype(F32)
    back_low = back_result.astype(BF)
    grad_down_t = mm(back_low, hidden, 0, 0)
    back_hidden = jnp.dot(back_low, w_down_t, preferred_element_type=F32)
    _, gate_back = jax.vjp(gated, gate_part, up_part)
    back_gate, back_up = gate_back(back_hidden)
    back_gate_up = jnp.concatenate([back_gate, back_up], 1).astype(BF)
    grad_in = mm(normed_b, back_gate_up, 0, 0)
    back_normed_b = mm(back_gate_up, w_in, 1, 1)
    _, second_back = jax.vjp(rms_norm, middle, gain_two)
    back_middle_norm, grad_gain_two = second_back(back_normed_b)
    back_middle = back_result + back_middle_norm
    back_branch = back_middle.astype(BF)
    grad_out_t = mm(back_branch, attended, 0, 0)
    back_attended = jnp.dot(back_branch, w_out_t, preferred_element_type=F32).astype(BF)

    output = exchange(result_low)
    late_grads = [grad_out_t, grad_in, grad_down_t]
    back_project, *late_sums, squares = attend_back(
        dims,
        2,
        project,
        kv,
        bias,
        attended,
        log_sums,
        back_attended,
        256,
        blocks_of(late_grads) if own_comm else [],
    )
    if not own_comm:
        late_sums = [lax.psum_scatter(g, both, scatter_dimension=0, tiled=True) for g in late_grads]
    out_sum, in_sum, down_sum = late_sums
    back_project, output = lax.optimization_barrier((back_project, output))
    grad_qkv = mm(normed_a, back_project, 0, 0)
    back_normed_a = mm(back_project, w_qkv, 1, 1)
    _, first_back = jax.vjp(rms_norm, tokens, gain_one)
    back_tokens, grad_gain_one = first_back(back_normed_a)
    back_rows = (back_middle + back_tokens).astype(BF).reshape(images, band_rows, width)
    grad_gains = jnp.pad(jnp.stack([grad_gain_one, grad_gain_two], 1), ((0, 0), (0, 126)))
    early_grads = [grad_qkv, grad_gains]
    if own_comm:
        qkv_sum, gain_sum, back_input, total = scatter_call(
            dims, "scatter", 3, blocks_of(early_grads), back_rows, squares
        )
    else:
        qkv_sum, gain_sum = [lax.psum_scatter(g, both, scatter_dimension=0, tiled=True) for g in early_grads]
        back_input = exchange(back_rows)
        squares = sum(jnp.sum(g * g) for g in late_sums + [qkv_sum, gain_sum])
        total = lax.psum(jnp.broadcast_to(squares, (8, 128)), both)
    grad_norm = jnp.sqrt(total[0, 0])
    factor = jnp.minimum(1.0, CLIP / grad_norm)
    shards = (
        qkv_sum,
        jnp.transpose(out_sum),
        in_sum,
        jnp.transpose(down_sum),
        jnp.transpose(gain_sum[:, :2]),
    )
    masters = (qkv_master, out_master, in_master, down_master, gain_master)
    firsts = (qkv_first, out_first, in_first, down_first, gain_first)
    seconds = (qkv_second, out_second, in_second, down_second, gain_second)
    updated = [
        adam_step(masters[j], shards[j], firsts[j], seconds[j], factor, RATES[j], DECAYS[j]) for j in range(5)
    ]
    return (
        (output, back_input, grad_norm)
        + tuple(updated[j][0] for j in range(5))
        + tuple(updated[j][1] for j in range(5))
        + tuple(updated[j][2] for j in range(5))
        + tuple(updated[j][0].astype(BF) for j in range(5))
    )


def solution(mesh):
    rows_split, columns_split = P(("img", "band"), None), P(None, ("img", "band"))
    weights = (rows_split, columns_split, rows_split, columns_split, columns_split)
    tokens = P("img", "band", None)
    return jax.shard_map(
        on_device,
        mesh=mesh,
        in_specs=(tokens, tokens, P("img")) + weights * 3,
        out_specs=(tokens, tokens, P()) + weights * 4,
        check_vma=False,
    )
```

time: 685 us -> 475 us (0.69)
  Pallas kernels: 513 us -> 302 us
  other arithmetic: 37.4 us -> 23.2 us
  waiting for transfers between devices: 0 us -> 13 us
  starting transfers between devices: 0 us -> 11.4 us
    pallas_call x6 -> x3, Pallas kernels: 375 us -> 251 us  [the longest x1 94.7 us: attend(): pl.pallas_call(body, grid=(pairs,), in_specs=[column(0), column(pairs), c...]
    pallas_call x2 -> x1, Pallas kernels: 138 us -> 51.7 us  [gather_call(): pl.pallas_call(body, out_shape=shapes, in_specs=[ANY] * len(args), out_sp...]
    all_to_all x0 -> x2, waiting for transfers between devices: none -> 13 us  [exchange(): lax.all_to_all(chunks, 'band', 0, 0, axis_index_groups=places, tiled=True)]
    all_to_all x0 -> x2, starting transfers between devices: none -> 11.4 us  [exchange(): lax.all_to_all(chunks, 'band', 0, 0, axis_index_groups=places, tiled=True)]
    unnamed x94 -> x88, local copies, waits for them, and re-layouts: 14.3 us -> 13.3 us
  transfers between devices with their start and end apart: 0 -> 2, of which waited for: 0 -> 1; matrix products, arithmetic and copies ran while one was open for 0% -> 4% of each run, Pallas kernels for 0% -> 20%
where the time goes in v2:
time: 475 us; the launch traced here: 469 us
  Pallas kernels  302 us (64%)
  matrix products  90.7 us (19%)
  local copies, waits for them, and re-layouts  24.4 us (5%)
  other arithmetic  23.2 us (5%)
  waiting for transfers between devices  13 us (3%)
  starting transfers between devices  11.4 us (2%)
    pallas_call x1, Pallas kernels, attend(): pl.pallas_call(body, grid=(pairs,), in_specs=[column(0), column(pairs), c...  94.7 us
    pallas_call x1, Pallas kernels, attend_back(): pl.pallas_call(body, grid=(pairs,), in_specs=[column(0), column(pairs), c...  93.1 us
    pallas_call x1, Pallas kernels, scatter_call(): pl.pallas_call(body, out_shape=shapes, in_specs=[ANY] * (n + 1) + [vmem],...  62.9 us
    dot_general x8, matrix products, mm(): lax.dot_general(a, b, (((ca,), (cb,)), ((), ())), preferred_element_type=...  55 us
    pallas_call x1, Pallas kernels, gather_call(): pl.pallas_call(body, out_shape=shapes, in_specs=[ANY] * len(args), out_sp...  51.7 us
    dot_general x1, matrix products, on_device(): back_hidden = jnp.dot(back_low, w_down_t, preferred_element_type=F32)  15.2 us
    unnamed x88, local copies, waits for them, and re-layouts  13.3 us
    all_to_all x2, waiting for transfers between devices, exchange(): lax.all_to_all(chunks, 'band', 0, 0, axis_index_groups=places, tiled=True)  13 us
  transfers between devices with their start and end apart: 2, of which 1 were waited for; matrix products, arithmetic and copies ran while one was open for 4% of the time, Pallas kernels for 20%

profile of v2, /device:TPU:0, one launch (start us, length us, event | category | flops | bytes accessed | tf_op | source)
XLA Modules:
  0.0 468.6 jit_solution(2626333768038994523)
XLA Ops:
  0.7 1.7 convert_element_type.145.refs_0_
  3.8 51.7 %gather.1 = (bf16[2,2,4,2,24,2304]{5,4,3,2,1,0:T(8,128)(2,1)}, bf16[2,2,4,2,24,128]{5,4,3,2,1,0:T(8,128)(2,1)}, bf16[4,256,768]{2,1,0:T(8,128)(2,1)}) custom-call(bf16[24,2304]{1,0:T(8,128)(2,1)} %convert_element_type.145.refs_0_, bf16[24,128]{1,0:T(8,128)(2,1)} %pad.9.refs_1_, bf16[4,256,768]{2,1,0:T(8,128)(2,1)} %refs_2_.1), custom_call_target="tpu_custom_call" | custom-call | tf_op jit(solution)/shard_map/gather/pallas_call | solution.py:342
  56.9 1.8 fusion.15
  63.2 5.4 %convolution_convert_fusion.1.refs_0_.refs_1_.refs_2_.refs_3_ = bf16[1024,2304]{1,0:T(8,128)(2,1)} fusion(bf16[1024,768]{1,0:T(8,128)(2,1)S(1)} %bitcast.93, bf16[768,2304]{1,0:T(8,128)(2,1)S(1)} %bitcast.102), kind=kOutput, calls=%fused_computation.14 | convolution fusion | flops 3626237952 | bytes 9830400 | tf_op jit(solution)/shard_map/dot_general | solution.py:792
  68.7 94.7 %attend.1 = (bf16[1024,768]{1,0:T(8,128)(2,1)}, f32[1024,768]{1,0:T(8,128)}, bf16[1,12,1024,128]{3,2,1,0:T(8,128)(2,1)}, bf16[2,2,4,2,24,768]{5,4,3,2,1,0:T(8,12...) custom-call(bf16[1024,2304]{1,0:T(8,128)(2,1)} %convolution_convert_fusion.1.refs_0_.refs_1_.ref, ...), custom_call_target="tpu_custom_call" | custom-call | flops 25769803776 | bytes 12582912 | tf_op jit(solution)/shard_map/attend/pallas_call | solution.py:511
  163.4 7.6 %all-to-all-start = ((bf16[4,256,768]{2,1,0:T(8,128)(2,1)}), bf16[4,256,768]{2,1,0:T(8,128)(2,1)S(1)}, u32[]{:S(2)}, u32[]{:S(2)}) async-start(bf16[4,256,768]{2,1,0:T(8,128)(2,1)} %param.19), calls=%async_computation | async-start | bytes 3145728 | tf_op jit(solution)/shard_map/all_to_all | solution.py:748
  175.2 3.3 multiply_reduce_fusion.2
  180.2 12.5 %fusion.39 = f32[1024,4096]{1,0:T(8,128)} fusion(bf16[768,4096]{1,0:T(8,128)(2,1)} %bitcast.103, f32[1024,768]{1,0:T(8,128)S(1)} %get-tuple-element.178, f32[768]{0:T(1024)S(1)} %convert_reduce_fusion, f32[1024]{0:T(1024)S(1)} %fusion.32), kind=kOutput, calls=%fused_computation.102 | convolution fusion | flops 6444810240 | bytes 26221568 | tf_op jit(solution)/shard_map/dot_general | solution.py:804
  192.7 13.0 %all-to-all-done = bf16[4,256,768]{2,1,0:T(8,128)(2,1)S(1)} async-done(((bf16[4,256,768]{2,1,0:T(8,128)(2,1)}), bf16[4,256,768]{2,1,0:T(8,128)(2,1)S(1)}, u32[]{:S(2)}, u32[]{:S(2)}) %all-to-all-start) | async-done | bytes 1572896 | tf_op jit(solution)/shard_map/all_to_all | solution.py:748
  207.6 15.2 %fusion.6 = (bf16[1024,2048]{1,0:T(8,128)(2,1)}, bf16[1024,2048]{1,0:T(8,128)(2,1)}, bf16[1024,2048]{1,0:T(8,128)(2,1)}) fusion(f32[1024,4096]{1,0:T(8,128)} %fusion.39, bf16[1024,768]{1,0:T(8,128)(2,1)S(1)} %bitcast.92, bf16[768,2048]{1,0:T(8,128)(2,1)S(1)} %bitcast.106), kind=kOutput, calls=%fused_computation.8 | convolution fusion | flops 3275751424 | bytes 34078720 | tf_op jit(solution)/shard_map/dot_general | solution.py:813
  222.8 11.4 %multiply_reduce_fusion = (bf16[768]{0:T(1024)(128)(2,1)S(1)}, f32[1024]{0:T(1024)S(1)}, f32[1024,768]{1,0:T(8,128)S(1)}) fusion(f32[1024,768]{1,0:T(8,128)S(1)} %copy-done.4, f32[1024]{0:T(1024)S(1)} %fusion.32, f32[768]{0:T(1024)S(1)} %convert_reduce_fusion, bf16[768,4096]{1,0:T(8,128)(2,1)} %bitcast.104, bf16[1024,2048]{1,0:T(8,128)(2,1)} %get-tuple-element.163, ...), kind=kOutput, calls=%fused_computation.38 | convolution fusion | flops 6463944704 | bytes 20984320 | tf_op jit(solution)/shard_map/dot_general | solution.py:397
  235.7 2.6 convolution_convert_fusion.4.refs_8_
  238.3 2.5 convolution_convert_fusion.5
  240.8 13.2 %convolution_convert_fusion = bf16[768,4096]{1,0:T(8,128)(2,1)} fusion(bf16[1024,2048]{1,0:T(8,128)(2,1)} %get-tuple-element.163, bf16[1024,2048]{1,0:T(8,128)(2,1)} %get-tuple-element.162, f32[1024,768]{1,0:T(8,128)S(1)} %copy-done.4, f32[768]{0:T(1024)S(1)} %convert_reduce_fusion, f32[1024]{0:T(1024)S(1)} %fusion.32), kind=kOutput, calls=%fused_computation.13 | convolution fusion | flops 6464733184 | bytes 17832960 | tf_op jit(solution)/shard_map/dot_general | solution.py:397
  253.9 7.0 %multiply_convert_fusion.2 = bf16[1024,768]{1,0:T(8,128)(2,1)} fusion(f32[1024,768]{1,0:T(8,128)S(1)} %copy-done.4, bf16[1024,2048]{1,0:T(8,128)(2,1)} %get-tuple-element.164, bf16[768,2048]{1,0:T(8,128)(2,1)S(1)} %bitcast.107, f32[1024]{0:T(1024)S(1)} %bitcast.100), kind=kOutput, calls=%fused_computation.39 | convolution fusion | flops 3223584768 | bytes 12062720 | tf_op jit(solution)/shard_map/dot_general | solution.py:397
  261.0 4.9 %convolution_convert_fusion.3 = bf16[768,2048]{1,0:T(8,128)(2,1)} fusion(bf16[1024,768]{1,0:T(8,128)(2,1)S(1)} %get-tuple-element.167, bf16[1024,2048]{1,0:T(8,128)(2,1)S(1)} %copy-done.35), kind=kOutput, calls=%fused_computation.19 | convolution fusion | flops 3222798336 | bytes 8912896 | tf_op jit(solution)/shard_map/dot_general | solution.py:397
  265.8 3.8 all-to-all-start.1
  269.7 93.1 %attend_back.1 = (bf16[1024,2304]{1,0:T(8,128)(2,1)}, f32[24,768]{1,0:T(8,128)}, f32[24,4096]{1,0:T(8,128)}, f32[24,2048]{1,0:T(8,128)}, f32[8,128]{1,0:T(8,128)}) custom-call(bf16[1024,2304]{1,0:T(8,128)(2,1)} %convolution_convert_fusion.1.refs_0_.refs_1_.refs_2_.refs_3_, bf16[1024,2304]{1,0:T(8,128)(2,1)} %convolution_convert_fusion.1.refs_0_.refs_1_.refs_2_.refs_3_, ...), custom_call_target="tpu_custom_call" | custom-call | flops 64424509440 | bytes 25165824 | tf_op jit(solution)/shard_map/attend_back/pallas_call | solution.py:664
  362.8 7.3 %fusion.18 = (f32[1024]{0:T(1024)S(1)}, bf16[768]{0:T(1024)(128)(2,1)S(1)}, f32[1024,768]{1,0:T(8,128)S(1)}) fusion(bf16[4,256,768]{2,1,0:T(8,128)(2,1)S(1)} %copy-done, f32[768]{0:T(1024)S(1)} %copy-done.22, f32[1024]{0:T(1024)S(1)} %copy-done.25, bf16[1024,2304]{1,0:T(8,128)(2,1)} %get-tuple-element.58, bf16[768,2304]{1,0:T(8,128)(2,1)} %bitcast.101), kind=kOutput, calls=%fused_computation.36 | convolution fusion | flops 3629381888 | bytes 12988928 | tf_op jit(solution)/shard_map/dot_general | solution.py:397
  370.2 2.3 fusion.10
  373.1 5.4 %convolution_convert_fusion.2 = bf16[768,2304]{1,0:T(8,128)(2,1)} fusion(bf16[1024,768]{1,0:T(8,128)(2,1)S(1)} %get-tuple-element.166, bf16[1024,2304]{1,0:T(8,128)(2,1)S(1)} %copy-done.37), kind=kOutput, calls=%fused_computation.16 | convolution fusion | flops 3625648128 | bytes 9830400 | tf_op jit(solution)/shard_map/dot_general | solution.py:397
  379.5 62.9 %scatter.1 = (f32[24,2304]{1,0:T(8,128)}, f32[24,128]{1,0:T(8,128)}, bf16[4,256,768]{2,1,0:T(8,128)(2,1)}, f32[8,128]{1,0:T(8,128)}) custom-call(bf16[2,2,4,2,24,2304]{5,4,3,2,1,0:T(8,128)(2,1)} %bitcast.90, bf16[2,2,4,2,24,128]{5,4,3,2,1,0:T(8,128)(2,1)} %bitcast.94, bf16[4,256,768]{2,1,0:T(8,128)(2,1)} %bitcast.89, f32[8,128]{1,0:T(8,128)} %get-tuple-element.59.refs_3_), custom_call_target="tpu_custom_call" | custom-call | tf_op jit(solution)/shard_map/scatter/pallas_call | solution.py:383
  457.7 2.1 fusion.49
  461.4 2.4 fusion.44
  (131 shorter events, 37.4 us)
Async XLA Ops:
  0.7 58.1 %copy-start.31 = (s32[4]{0:T(128)S(1)}, s32[4]{0:T(128)}, u32[]{:S(2)}) copy-start(s32[4]{0:T(128)} %param.20) | copy-start | bytes 52
  0.7 60.1 %copy-start.13 = (f32[768,24]{0,1:T(8,128)S(1)}, f32[768,24]{0,1:T(8,128)}, u32[]{:S(2)}) copy-start(f32[768,24]{0,1:T(8,128)} %param.22) | copy-start | bytes 221188
  0.7 60.7 %copy-start.6 = (f32[24,4096]{1,0:T(8,128)S(1)}, f32[24,4096]{1,0:T(8,128)}, u32[]{:S(2)}) copy-start(f32[24,4096]{1,0:T(8,128)} %param.23) | copy-start | bytes 1179652
  0.7 61.4 %copy-start.9 = (f32[2048,24]{0,1:T(8,128)S(1)}, f32[2048,24]{0,1:T(8,128)}, u32[]{:S(2)}) copy-start(f32[2048,24]{0,1:T(8,128)} %param.24) | copy-start | bytes 589828
  56.9 11.7 %copy-start.21 = (f32[768]{0:T(1024)}, f32[768]{0:T(1024)S(1)}, u32[]{:S(2)}) copy-start(f32[768]{0:T(1024)S(1)} %convert_reduce_fusion.1) | copy-start | bytes 9220
  163.4 7.7 %copy-start.26 = (f32[2,24]{1,0:T(2,128)S(1)}, f32[2,24]{1,0:T(2,128)}, u32[]{:S(2)}) copy-start(f32[2,24]{1,0:T(2,128)} %param.25) | copy-start | bytes 580
  163.4 10.4 %copy-start.28 = (f32[2,24]{1,0:T(2,128)S(1)}, f32[2,24]{1,0:T(2,128)}, u32[]{:S(2)}) copy-start(f32[2,24]{1,0:T(2,128)} %param.35) | copy-start | bytes 580
  163.4 11.1 %copy-start.29 = (f32[2,24]{1,0:T(2,128)S(1)}, f32[2,24]{1,0:T(2,128)}, u32[]{:S(2)}) copy-start(f32[2,24]{1,0:T(2,128)} %param.30) | copy-start | bytes 580
  163.4 42.2 %all-to-all-start = ((bf16[4,256,768]{2,1,0:T(8,128)(2,1)}), bf16[4,256,768]{2,1,0:T(8,128)(2,1)S(1)}, u32[]{:S(2)}, u32[]{:S(2)}) async-start(bf16[4,256,768]{2,1,0:T(8,128)(2,1)} %param.19), calls=%async_computation | async-start | bytes 3145728 | tf_op jit(solution)/shard_map/all_to_all | solution.py:748
  207.6 15.2 %copy-start.4 = (f32[1024,768]{1,0:T(8,128)S(1)}, f32[1024,768]{1,0:T(8,128)}, u32[]{:S(2)}) copy-start(f32[1024,768]{1,0:T(8,128)} %copy-done.3) | copy-start | bytes 9437188
  240.7 13.2 %copy-start.33 = (bf16[2,2,4,2,24,2048]{5,4,3,2,1,0:T(8,128)(2,1)S(1)}, bf16[2,2,4,2,24,2048]{5,4,3,2,1,0:T(8,128)(2,1)}, u32[]{:S(2)}) copy-start(bf16[2,2,4,2,24,2048]{5,4,3,2,1,0:T(8,128)(2,1)} %get-tuple-element.53) | copy-start | bytes 9437188
  265.8 96.9 %all-to-all-start.1 = ((bf16[4,256,768]{2,1,0:T(8,128)(2,1)}), bf16[4,256,768]{2,1,0:T(8,128)(2,1)S(1)}, u32[]{:S(2)}, u32[]{:S(2)}) async-start(bf16[4,256,768]{2,1,0:T(8,128)(2,1)} %bitcast.91), calls=%async_computation.1 | async-start | bytes 3145728 | tf_op jit(solution)/shard_map/all_to_all | solution.py:748
  269.7 93.1 %copy-start.22 = (f32[768]{0:T(1024)S(1)}, f32[768]{0:T(1024)}, u32[]{:S(2)}) copy-start(f32[768]{0:T(1024)} %copy-done.21) | copy-start | bytes 9220
  269.7 93.1 %copy-start.25 = (f32[1024]{0:T(1024)S(1)}, f32[1024]{0:T(1024)}, u32[]{:S(2)}) copy-start(f32[1024]{0:T(1024)} %rsqrt.27) | copy-start | bytes 12292
  378.5 69.9 %copy-start.27 = (f32[2,24]{1,0:T(2,128)S(1)}, f32[2,24]{1,0:T(2,128)}, u32[]{:S(2)}) copy-start(f32[2,24]{1,0:T(2,128)} %param.25) | copy-start | bytes 580
  378.5 72.5 %copy-start.20 = (f32[2,24]{0,1:T(8,128)S(1)}, f32[2,24]{0,1:T(8,128)}, u32[]{:S(2)}) copy-start(f32[2,24]{0,1:T(8,128)} %copy.82) | copy-start | bytes 580
  378.5 79.2 %copy-start.8 = (f32[24,2304]{1,0:T(8,128)S(1)}, f32[24,2304]{1,0:T(8,128)}, u32[]{:S(2)}) copy-start(f32[24,2304]{1,0:T(8,128)} %param.21) | copy-start | bytes 663556
  378.5 79.2 %copy-start.15 = (f32[24,2304]{1,0:T(8,128)S(1)}, f32[24,2304]{1,0:T(8,128)}, u32[]{:S(2)}) copy-start(f32[24,2304]{1,0:T(8,128)} %param.26) | copy-start | bytes 663556
  379.5 80.3 %copy-start.14 = (f32[768,24]{0,1:T(8,128)S(1)}, f32[768,24]{0,1:T(8,128)}, u32[]{:S(2)}) copy-start(f32[768,24]{0,1:T(8,128)} %param.22) | copy-start | bytes 221188
  379.5 80.3 %copy-start.19 = (f32[768,24]{0,1:T(8,128)S(1)}, f32[768,24]{0,1:T(8,128)}, u32[]{:S(2)}) copy-start(f32[768,24]{0,1:T(8,128)} %param.27) | copy-start | bytes 221188
  379.5 81.9 %copy-start.7 = (f32[24,4096]{1,0:T(8,128)S(1)}, f32[24,4096]{1,0:T(8,128)}, u32[]{:S(2)}) copy-start(f32[24,4096]{1,0:T(8,128)} %param.23) | copy-start | bytes 1179652
  379.5 81.9 %copy-start.11 = (f32[24,4096]{1,0:T(8,128)S(1)}, f32[24,4096]{1,0:T(8,128)}, u32[]{:S(2)}) copy-start(f32[24,4096]{1,0:T(8,128)} %param.28) | copy-start | bytes 1179652
  379.5 81.9 %copy-start.12 = (f32[24,4096]{1,0:T(8,128)S(1)}, f32[24,4096]{1,0:T(8,128)}, u32[]{:S(2)}) copy-start(f32[24,4096]{1,0:T(8,128)} %param.33) | copy-start | bytes 1179652
  442.4 21.4 %copy-start.10 = (f32[2048,24]{0,1:T(8,128)S(1)}, f32[2048,24]{0,1:T(8,128)}, u32[]{:S(2)}) copy-start(f32[2048,24]{0,1:T(8,128)} %param.24) | copy-start | bytes 589828
  (16 other events, 68.2 us)

commit v3 on v2

--- a/solution.py
+++ b/solution.py
@@ -141,13 +141,11 @@
         turn += 1
 
 
-def exchange_images(net, source, target):
+def exchange_images(net, source, target, idle=1):
     moves = [net.copy(Part(source)[other], Part(target)[net.image], dev) for other, dev in net.line("image")]
     own = net.local_copy(Part(source)[net.image], Part(target)[net.image])
-    yield
-    yield
-    yield
-    yield
+    for _ in range(idle):
+        yield
     for move in moves:
         move.wait_recv()
     own.wait()
@@ -311,6 +309,14 @@
     return [((0, low), "xy"), ((low, width - low), "yx")]
 
 
+def pieces(width, groups):
+    found = []
+    for group in range(groups):
+        for columns, order in halves(width // groups):
+            found.append((group, (columns[0] + group * (width // groups), columns[1]), order))
+    return found
+
+
 def gather_call(dims, name, number, blocks, images=None):
     big_y, big_x, big_z, share = dims
     parts = [halves(block.shape[1]) for block in blocks]
@@ -332,7 +338,7 @@
             for columns, order in parts[j]:
                 tasks.append((0, gather(net, ins[j], outs[j], columns, order)))
         if with_images:
-            tasks.append((0, exchange_images(net, ins[n], outs[n])))
+            tasks.append((1, exchange_images(net, ins[n], outs[n], 3)))
         drive(tasks)
 
     args = list(blocks) + ([images] if with_images else [])
@@ -372,7 +378,7 @@
         for k, (j, columns, order) in enumerate(parts):
             buffers = rest[3 + 5 * k : 8 + 5 * k]
             tasks.append((0, scatter(net, ins[j], *buffers, outs[j], tile, columns, order)))
-        tasks.append((0, exchange_images(net, ins[n], outs[n])))
+        tasks.append((0, exchange_images(net, ins[n], outs[n], 4)))
         drive(tasks)
         sum_tiles(net, tile, slots)
         outs[n + 1][...] = jnp.broadcast_to(jnp.sum(tile[...], keepdims=True), (8, 128))
@@ -422,21 +428,25 @@
     return lane if h == 0 else ~lane
 
 
-def attend(dims, number, project, bias, block, weights):
+def attend(dims, number, project, bias, block, weights, chunks):
     big_y, big_x, big_z, share = dims
     rows, width = project.shape[0], project.shape[1] // 3
     pairs = width // PAIR
     others = share - 1
     blocks = rows // block
     n = len(weights)
-    parts = [(j, columns, order) for j, w in enumerate(weights) for columns, order in halves(w.shape[1])]
-    copies = len(parts) * gather_copies(dims) + others * 2 * pairs
+    parts = [
+        (j, columns, order, GATHER_TURNS[j][group])
+        for j, w in enumerate(weights)
+        for group, columns, order in pieces(w.shape[1], len(GATHER_TURNS[j]))
+    ]
+    copies = len(parts) * gather_copies(dims) + others * 2 * pairs + chunks.shape[0] - 1
     per_turn = max(blocks // 4, 1)
 
     def body(*refs):
-        q_ref, k_ref, v_ref, project_ref, bias_ref = refs[:5]
-        blocks_in, refs = refs[5 : 5 + n], refs[5 + n :]
-        o_ref, l_ref, kv_out, refs = refs[0], refs[1], refs[2], refs[3:]
+        q_ref, k_ref, v_ref, project_ref, bias_ref, chunks_in = refs[:6]
+        blocks_in, refs = refs[6 : 6 + n], refs[6 + n :]
+        o_ref, l_ref, kv_out, chunks_out, refs = refs[0], refs[1], refs[2], refs[3], refs[4:]
         gathered, (kv_held, send, recv, local) = refs[:n], refs[n:]
         h = pl.program_id(0)
         net = Net(dims, send, recv, local)
@@ -449,16 +459,15 @@
             return moves
 
         key_moves = [move_keys(j) for j in range(2 * pairs)]
-        keep = Move(Part(kv_held), Part(kv_out), None, local, len(parts), None)
-        tasks = [gather(net, blocks_in[j], gathered[j], columns, order) for j, columns, order in parts]
-        turns = []
-        for j, columns, order in parts:
-            turns.append([GATHER_TURNS[j][0]] + [t for t in GATHER_TURNS[j][1:]])
+        keep = Move(Part(kv_held), Part(kv_out), None, local, len(parts) + 1, None)
+        tasks = [gather(net, blocks_in[j], gathered[j], columns, order) for j, columns, order, _ in parts]
+        tasks.append(exchange_images(net, chunks_in, chunks_out))
+        turns = [turn for _, _, _, turn in parts] + [CHUNK_TURNS]
         events, tail = schedule(tasks, turns, 4 * pairs)
 
         @pl.when(h == 0)
         def _():
-            net.greet(["z", "x", "y", "c"] + (["share"] if share > 2 else []))
+            net.greet(["z", "x", "y", "c", "image"] + (["share"] if share > 2 else []))
             for j in range(pairs):
                 for move in key_moves[j] + key_moves[j + pairs]:
                     move.start()
@@ -507,19 +516,20 @@
         jax.ShapeDtypeStruct((rows, width), BF),
         jax.ShapeDtypeStruct((rows, width), F32),
         jax.ShapeDtypeStruct((others, 2 * pairs, rows, PAIR), BF),
+        jax.ShapeDtypeStruct(chunks.shape, chunks.dtype),
     ] + [jax.ShapeDtypeStruct((big_y, big_x, big_z, 2) + w.shape, w.dtype) for w in weights]
     return pl.pallas_call(
         body,
         grid=(pairs,),
         in_specs=[column(0), column(pairs), column(2 * pairs), ANY, pl.BlockSpec((1, keys), lambda h: (0, 0))]
-        + [ANY] * n,
-        out_specs=[column(0), column(0), ANY] + [ANY] * n,
+        + [ANY] * (1 + n),
+        out_specs=[column(0), column(0), ANY, ANY] + [ANY] * n,
         out_shape=shapes,
         scratch_shapes=[
             pltpu.VMEM((others, 2 * pairs, rows, PAIR), BF),
             sems(copies),
             sems(copies),
-            sems(len(parts) + 1),
+            sems(len(parts) + 2),
         ],
         compiler_params=pltpu.CompilerParams(
             collective_id=number, has_side_effects=True, vmem_limit_bytes=56 * MIB
@@ -528,14 +538,20 @@
             flops=16 * rows * keys * width, bytes_accessed=8 * keys * width, transcendentals=rows * keys * HEADS
         ),
         name="attend",
-    )(project, project, project, project, bias, *weights)
-
-
-GATHER_TURNS = ((0, 8, 11, 17, 21), (1, 4, 6, 9, 12), (3, 12, 15, 21, 24))
-SCATTER_TURNS = ((0, 2, 8, 14, 20), (1, 3, 9, 15, 21), (1, 4, 11, 17, 24))
-
-
-def attend_back(dims, number, project, kv, bias, mixed, logs, back, block, grads):
+    )(project, project, project, project, bias, chunks, *weights)
+
+
+GATHER_TURNS = (
+    ((0, 1, 2, 4, 6),),
+    ((0, 3, 6, 11, 13), (1, 7, 13, 18, 20)),
+    ((2, 10, 17, 22, 24),),
+)
+CHUNK_TURNS = (8, 24)
+SCATTER_TURNS = ((1, 4, 11, 17, 24), (0, 2, 8, 14, 20), (1, 3, 9, 15, 21))
+RESULT_TURNS = (0, 24)
+
+
+def attend_back(dims, number, project, kv, bias, mixed, logs, back, block, grads, chunks):
     big_y, big_x, big_z, share = dims
     rows, width = mixed.shape
     pairs = width // PAIR
@@ -544,13 +560,13 @@
     keys = rows * share
     n = len(grads)
     parts = [(j, columns, order) for j, g in enumerate(grads) for columns, order in halves(g.shape[5])]
-    copies = len(parts) * gather_copies(dims) + others * 2 * pairs
+    copies = len(parts) * gather_copies(dims) + others * 2 * pairs + chunks.shape[0] - 1
     per_turn = max(blocks // 4, 1)
 
     def body(*refs):
         q_ref, k_ref, v_ref, k_other, v_other, bias_ref, mixed_ref, logs_ref, back_ref = refs[:9]
-        grads_in, refs = refs[9 : 9 + n], refs[9 + n :]
-        out_ref, sums, squares, refs = refs[0], refs[1 : 1 + n], refs[1 + n], refs[2 + n :]
+        grads_in, chunks_in, refs = refs[9 : 9 + n], refs[9 + n], refs[10 + n :]
+        out_ref, sums, squares, chunks_out, refs = refs[0], refs[1 : 1 + n], refs[1 + n], refs[2 + n], refs[3 + n :]
         dk_sum, dv_sum, dk_own, dv_own, parted, arrived, bias_column = refs[:7]
         send, recv, local = refs[7:10]
         buffers = refs[10:]
@@ -568,11 +584,13 @@
             scatter(net, grads_in[j], *buffers[5 * k : 5 * k + 5], sums[j], squares, columns, order)
             for k, (j, columns, order) in enumerate(parts)
         ]
-        events, tail = schedule(tasks, [SCATTER_TURNS[j] for j, _, _ in parts], 4 * pairs)
+        tasks.append(exchange_images(net, chunks_in, chunks_out))
+        turns = [SCATTER_TURNS[j] for j, _, _ in parts] + [RESULT_TURNS]
+        events, tail = schedule(tasks, turns, 4 * pairs)
 
         @pl.when(h == 0)
         def _():
-            net.greet(["z", "x", "y", "c"] + (["share"] if share > 2 else []))
+            net.greet(["z", "x", "y", "c", "image"] + (["share"] if share > 2 else []))
             squares[...] = jnp.zeros_like(squares)
             bias_column[...] = jnp.transpose(jnp.broadcast_to(bias_ref[...], (PAIR, keys)))
 
@@ -647,6 +665,7 @@
         + [jax.ShapeDtypeStruct((shard, g.shape[5]), F32) for g in grads]
         + [jax.ShapeDtypeStruct((8, 128), F32)]
     )
+    moved = jax.ShapeDtypeStruct(chunks.shape, chunks.dtype)
     scratch = [
         pltpu.VMEM((keys, PAIR), F32),
         pltpu.VMEM((keys, PAIR), F32),
@@ -657,7 +676,7 @@
         pltpu.VMEM((keys, PAIR), F32),
         sems(copies),
         sems(copies),
-        sems(len(parts)),
+        sems(len(parts) + 1),
     ]
     for j, columns, order in parts:
         scratch += scatter_scratch(dims, shard, columns, order)
@@ -675,9 +694,9 @@
             column(0),
             column(0),
         ]
-        + [ANY] * n,
-        out_specs=[whole(s.shape) for s in shapes],
-        out_shape=shapes,
+        + [ANY] * (n + 1),
+        out_specs=[whole(s.shape) for s in shapes] + [ANY],
+        out_shape=shapes + [moved],
         scratch_shapes=scratch,
         compiler_params=pltpu.CompilerParams(
             collective_id=number, has_side_effects=True, vmem_limit_bytes=60 * MIB
@@ -686,15 +705,244 @@
             flops=40 * rows * keys * width, bytes_accessed=16 * keys * width, transcendentals=rows * keys * HEADS
         ),
         name="attend_back",
-    )(project, project, project, kv, kv, bias, mixed, logs, back, *grads)
-
-
-def rms_norm(value, gain):
-    return value * lax.rsqrt(jnp.mean(value * value, -1, keepdims=True) + EPS) * gain
-
-
-def gated(gate_part, up_part):
-    return jax.nn.gelu(gate_part, approximate=True) * up_part
+    )(project, project, project, kv, kv, bias, mixed, logs, back, *grads, chunks)
+
+
+def whole(shape):
+    return pl.BlockSpec(shape, lambda i: (0,) * len(shape))
+
+
+def kept(shape):
+    return pl.BlockSpec(shape, lambda i: (0,) * len(shape), pipeline_mode=pl.Buffered(1))
+
+
+def inverse_rms(value):
+    return lax.rsqrt(jnp.mean(value * value, -1, keepdims=True) + EPS)
+
+
+def norm_back(back, value, scale, gain):
+    scaled = back * gain
+    inner = jnp.mean(scaled * value, -1, keepdims=True)
+    return scale * scaled - value * (scale * scale * scale * inner), back * (value * scale)
+
+
+def project_call(tokens, weight, gains, block):
+    rows, width = tokens.shape
+
+    def body(x_ref, w_ref, g_ref, out_ref, gains_ref):
+        gain_rows = jnp.transpose(g_ref[...].astype(F32))
+        gains_ref[...] = gain_rows[:8]
+        x = x_ref[...].astype(F32)
+        normed = (x * inverse_rms(x) * gain_rows[0:1]).astype(BF)
+        out_ref[...] = mm(normed, w_ref[...], 1, 0).astype(BF)
+
+    return pl.pallas_call(
+        body,
+        grid=(rows // block,),
+        in_specs=[pl.BlockSpec((block, width), lambda i: (i, 0)), kept(weight.shape), kept(gains.shape)],
+        out_specs=[pl.BlockSpec((block, 3 * width), lambda i: (i, 0)), whole((8, width))],
+        out_shape=[jax.ShapeDtypeStruct((rows, 3 * width), BF), jax.ShapeDtypeStruct((8, width), F32)],
+        compiler_params=pltpu.CompilerParams(vmem_limit_bytes=40 * MIB),
+        cost_estimate=pl.CostEstimate(
+            flops=6 * rows * width * width, bytes_accessed=14 * width * width, transcendentals=rows
+        ),
+        name="project",
+    )(tokens, weight, gains)
+
+
+GELU_A = 0.7978845608028654
+GELU_B = 0.044715
+
+
+def mlp_call(tokens, attended, cotangent, keep, w_out_t, w_in, w_down_t, gains, block):
+    rows, width = tokens.shape
+    hidden_units = w_down_t.shape[1]
+    steps = rows // block
+    tile = 512
+    in_tiles, down_tiles = 2 * hidden_units // tile, hidden_units // tile
+    part = 512
+
+    def body(
+        x_ref, a_ref, c_ref, keep_ref, wo_ref, wi_ref, wd_ref, g_ref,
+        result_ref, middle_ref, back_ref, gain_ref, g_out_ref, g_in_ref, g_down_ref,
+        normed_t, low_t, branch_t, mixed, hidden, back_gu,
+    ):
+        i = pl.program_id(0)
+
+        @pl.when(i == 0)
+        def _():
+            gain_ref[...] = jnp.zeros_like(gain_ref)
+
+        @pl.when(i < steps)
+        def _():
+            at = pl.ds(pl.multiple_of(i * block, block), block)
+            gain = g_ref[1:2, :]
+            a = a_ref[...]
+            mixed[at, :] = a
+            middle = x_ref[...].astype(F32) + mm(a, wo_ref[...], 1, 1)
+            scale = inverse_rms(middle)
+            normed = (middle * scale * gain).astype(BF)
+            normed_t[:, at] = jnp.transpose(normed)
+            back_result = keep_ref[...] * c_ref[...].astype(F32)
+            low = back_result.astype(BF)
+            low_t[:, at] = jnp.transpose(low)
+            result, back = middle, jnp.zeros_like(middle)
+            for p in range(hidden_units // part):
+                one = slice(p * part, (p + 1) * part)
+                two = slice(hidden_units + p * part, hidden_units + (p + 1) * part)
+                gate = mm(normed, wi_ref[:, one], 1, 0)
+                up = mm(normed, wi_ref[:, two], 1, 0)
+                back_hidden = mm(low, wd_ref[:, one], 1, 0)
+                square = gate * gate
+                bend = jnp.tanh(GELU_A * (gate + GELU_B * (gate * square)))
+                half = 0.5 + 0.5 * bend
+                curve = gate * half
+                slope = half + (0.5 * GELU_A) * gate * (1.0 - bend * bend) * (1.0 + (3.0 * GELU_B) * square)
+                hid = (curve * up).astype(BF)
+                back_gate = (back_hidden * up * slope).astype(BF)
+                back_up = (back_hidden * curve).astype(BF)
+                hidden[at, one] = hid
+                back_gu[at, one] = back_gate
+                back_gu[at, two] = back_up
+                result = result + mm(hid, wd_ref[:, one], 1, 1)
+                back = back + mm(back_gate, wi_ref[:, one], 1, 1) + mm(back_up, wi_ref[:, two], 1, 1)
+            result_ref[...] = (keep_ref[...] * result).astype(BF)
+            into, gain_rows = norm_back(back, middle, scale, gain)
+            gain_ref[0:1, :] += jnp.sum(gain_rows, 0, keepdims=True)
+            back_middle = back_result + into
+            middle_ref[...] = back_middle
+            branch = back_middle.astype(BF)
+            branch_t[:, at] = jnp.transpose(branch)
+            back_ref[...] = mm(branch, wo_ref[...], 1, 0).astype(BF)
+
+        @pl.when(i == steps)
+        def _():
+            g_out_ref[...] = mm(branch_t[...], mixed[...], 1, 0).astype(BF)
+
+        for t in range(in_tiles):
+
+            @pl.when(i == steps + 1 + t)
+            def _(t=t):
+                g_in_ref[...] = mm(normed_t[...], back_gu[:, t * tile : (t + 1) * tile], 1, 0).astype(BF)
+
+        for t in range(down_tiles):
+
+            @pl.when(i == steps + 1 + in_tiles + t)
+            def _(t=t):
+                g_down_ref[...] = mm(low_t[...], hidden[:, t * tile : (t + 1) * tile], 1, 0).astype(BF)
+
+    row = lambda last: pl.BlockSpec((block, last), lambda i: (jnp.minimum(i, steps - 1), 0))
+    return pl.pallas_call(
+        body,
+        grid=(steps + 1 + in_tiles + down_tiles,),
+        in_specs=[
+            row(width),
+            row(width),
+            row(width),
+            row(1),
+            kept(w_out_t.shape),
+            kept(w_in.shape),
+            kept(w_down_t.shape),
+            kept(gains.shape),
+        ],
+        out_specs=[
+            row(width),
+            row(width),
+            row(width),
+            whole((8, width)),
+            whole((width, width)),
+            pl.BlockSpec((width, tile), lambda i: (0, jnp.clip(i - steps - 1, 0, in_tiles - 1))),
+            pl.BlockSpec((width, tile), lambda i: (0, jnp.clip(i - steps - 1 - in_tiles, 0, down_tiles - 1))),
+        ],
+        out_shape=[
+            jax.ShapeDtypeStruct((rows, width), BF),
+            jax.ShapeDtypeStruct((rows, width), F32),
+            jax.ShapeDtypeStruct((rows, width), BF),
+            jax.ShapeDtypeStruct((8, width), F32),
+            jax.ShapeDtypeStruct((width, width), BF),
+            jax.ShapeDtypeStruct((width, 2 * hidden_units), BF),
+            jax.ShapeDtypeStruct((width, hidden_units), BF),
+        ],
+        scratch_shapes=[
+            pltpu.VMEM((width, rows), BF),
+            pltpu.VMEM((width, rows), BF),
+            pltpu.VMEM((width, rows), BF),
+            pltpu.VMEM((rows, width), BF),
+            pltpu.VMEM((rows, hidden_units), BF),
+            pltpu.VMEM((rows, 2 * hidden_units), BF),
+        ],
+        compiler_params=pltpu.CompilerParams(vmem_limit_bytes=61 * MIB),
+        cost_estimate=pl.CostEstimate(
+            flops=6 * rows * width * (width + 3 * hidden_units),
+            bytes_accessed=8 * width * (width + 3 * hidden_units),
+            transcendentals=rows * hidden_units,
+        ),
+        name="mlp",
+    )(tokens, attended, cotangent, keep, w_out_t, w_in, w_down_t, gains)
+
+
+def finish_call(tokens, back_project, weight, back_middle, gains, gain_two_grad, block):
+    rows, width = tokens.shape
+    steps = rows // block
+    tiles, tile = 3, width
+
+    def body(x_ref, b_ref, w_ref, m_ref, g_ref, two_ref, out_ref, grad_ref, gain_ref, normed_t, held, gain_rows):
+        i = pl.program_id(0)
+
+        @pl.when(i == 0)
+        def _():
+            gain_rows[...] = jnp.zeros_like(gain_rows)
+            gain_rows[1:2, :] = two_ref[0:1, :]
+
+        @pl.when(i < steps)
+        def _():
+            at = pl.ds(pl.multiple_of(i * block, block), block)
+            gain = g_ref[0:1, :]
+            x = x_ref[...].astype(F32)
+            scale = inverse_rms(x)
+            normed_t[:, at] = jnp.transpose((x * scale * gain).astype(BF))
+            back = b_ref[...]
+            held[at, :] = back
+            into, rows_of_gain = norm_back(mm(back, w_ref[...], 1, 1), x, scale, gain)
+            out_ref[...] = (m_ref[...] + into).astype(BF)
+            gain_rows[0:1, :] += jnp.sum(rows_of_gain, 0, keepdims=True)
+
+        for t in range(tiles):
+
+            @pl.when(i == steps + t)
+            def _(t=t):
+                grad_ref[...] = mm(normed_t[...], held[:, t * tile : (t + 1) * tile], 1, 0).astype(BF)
+
+        @pl.when(i == steps)
+        def _():
+            gain_ref[...] = jnp.transpose(gain_rows[...]).astype(BF)
+
+    row = lambda last: pl.BlockSpec((block, last), lambda i: (jnp.minimum(i, steps - 1), 0))
+    return pl.pallas_call(
+        body,
+        grid=(steps + tiles,),
+        in_specs=[row(width), row(3 * width), kept(weight.shape), row(width), kept(gains.shape), kept((8, width))],
+        out_specs=[
+            row(width),
+            pl.BlockSpec((width, tile), lambda i: (0, jnp.clip(i - steps, 0, tiles - 1))),
+            whole((width, 128)),
+        ],
+        out_shape=[
+            jax.ShapeDtypeStruct((rows, width), BF),
+            jax.ShapeDtypeStruct((width, 3 * width), BF),
+            jax.ShapeDtypeStruct((width, 128), BF),
+        ],
+        scratch_shapes=[
+            pltpu.VMEM((width, rows), BF),
+            pltpu.VMEM((rows, 3 * width), BF),
+            pltpu.VMEM((128, width), F32),
+        ],
+        compiler_params=pltpu.CompilerParams(vmem_limit_bytes=48 * MIB),
+        cost_estimate=pl.CostEstimate(
+            flops=12 * rows * width * width, bytes_accessed=28 * width * width, transcendentals=rows
+        ),
+        name="finish",
+    )(tokens, back_project, weight, back_middle, gains, gain_two_grad)
 
 
 def adam_step(master, grad, first, second, factor, rate, decay):
@@ -705,6 +953,38 @@
     spread = jnp.sqrt(second_new / (1.0 - BETA_TWO**STEP)) + ADAM_EPS
     master_new = master - rate * (corrected / spread + decay * master)
     return (master_new, first_new, second_new)
+
+
+def adam_call(squares, grads, masters, firsts, seconds):
+    shard = grads[0].shape[0]
+
+    def body(*refs):
+        squares_ref, refs = refs[0], refs[1:]
+        ins, norm_ref, outs = refs[:20], refs[20], refs[21:]
+        norm = jnp.sqrt(squares_ref[0:1, :])
+        norm_ref[...] = jnp.broadcast_to(norm, norm_ref.shape)
+        factor = jnp.minimum(1.0, CLIP / norm[:, 0:1])
+        for j in range(5):
+            grad = ins[j][...]
+            if j == 4:
+                filled = jnp.concatenate([grad, jnp.zeros((128 - shard, 128), F32)], 0)
+                grad = jnp.transpose(filled)[:2, :shard]
+            made = adam_step(
+                ins[5 + j][...], grad, ins[10 + j][...], ins[15 + j][...], factor, RATES[j], DECAYS[j]
+            )
+            for kind in range(3):
+                outs[5 * kind + j][...] = made[kind]
+            outs[15 + j][...] = made[0].astype(BF)
+
+    shapes = [jax.ShapeDtypeStruct((8, 128), F32)]
+    shapes += [jax.ShapeDtypeStruct(m.shape, F32) for _ in range(3) for m in masters]
+    shapes += [jax.ShapeDtypeStruct(m.shape, BF) for m in masters]
+    return pl.pallas_call(
+        body,
+        out_shape=shapes,
+        compiler_params=pltpu.CompilerParams(vmem_limit_bytes=56 * MIB),
+        name="adam",
+    )(squares, *grads, *masters, *firsts, *seconds)
 
 
 def grid_of(n_img):
@@ -751,7 +1031,7 @@
         return [g.reshape(width, g.shape[-1]) for g in got]
 
     def blocks_of(grads):
-        return [g.astype(BF).reshape(dims[:3] + (2, shard, g.shape[1])) for g in grads]
+        return [g.reshape(dims[:3] + (2, shard, g.shape[1])) for g in grads]
 
     gains_block = jnp.pad(jnp.transpose(gain_master).astype(BF), ((0, 0), (0, 126)))
     early = [qkv_master.astype(BF), gains_block]
@@ -766,9 +1046,6 @@
     else:
         w_qkv, gains = [lax.all_gather(b, both, axis=0, tiled=True) for b in early]
         tokens_low = exchange(patches)
-    gain_one = gains[:, 0].astype(F32)
-    gain_two = gains[:, 1].astype(F32)
-
     band = lax.axis_index("band")
     image, part = band // share, band % share
     count = lax.dynamic_index_in_dim(valid_counts, image, 0, keepdims=False)
@@ -787,45 +1064,28 @@
     ).reshape(1, share * rows)
     bias = jnp.where(key_places < count, 0.0, NEG).astype(F32)
 
-    tokens = tokens_low.reshape(rows, width).astype(F32)
-    normed_a = rms_norm(tokens, gain_one).astype(BF)
-    project = jnp.dot(normed_a, w_qkv, preferred_element_type=F32).astype(BF)
-    attended, log_sums, kv, *late_all = attend(dims, 1, project, bias, 256, late if own_comm else [])
+    tokens = tokens_low.reshape(rows, width)
+    project, gain_rows = project_call(tokens, w_qkv, gains, min(256, rows))
+    attended, log_sums, kv, cotangent_low, *late_all = attend(
+        dims, 1, project, bias, 256, late if own_comm else [], cotangent
+    )
     if own_comm:
         w_out_t, w_in, w_down_t = flat(late_all)
     else:
         w_out_t, w_in, w_down_t = [lax.all_gather(b, both, axis=0, tiled=True) for b in late]
-    hidden_units = w_down_t.shape[1]
-    cotangent_later, attended = lax.optimization_barrier((cotangent, attended))
-    cotangent_low = exchange(cotangent_later)
-
-    middle = tokens + mm(attended, w_out_t, 1, 1)
-    normed_b = rms_norm(middle, gain_two).astype(BF)
-    gate_up = jnp.dot(normed_b, w_in, preferred_element_type=F32)
-    gate_part = gate_up[:, :hidden_units]
-    up_part = gate_up[:, hidden_units:]
-    hidden = gated(gate_part, up_part).astype(BF)
-    result = row_keep * (middle + mm(hidden, w_down_t, 1, 1))
-    result_low = result.astype(BF).reshape(images, band_rows, width)
-    back_result = row_keep * cotangent_low.reshape(rows, width).astype(F32)
-    back_low = back_result.astype(BF)
-    grad_down_t = mm(back_low, hidden, 0, 0)
-    back_hidden = jnp.dot(back_low, w_down_t, preferred_element_type=F32)
-    _, gate_back = jax.vjp(gated, gate_part, up_part)
-    back_gate, back_up = gate_back(back_hidden)
-    back_gate_up = jnp.concatenate([back_gate, back_up], 1).astype(BF)
-    grad_in = mm(normed_b, back_gate_up, 0, 0)
-    back_normed_b = mm(back_gate_up, w_in, 1, 1)
-    _, second_back = jax.vjp(rms_norm, middle, gain_two)
-    back_middle_norm, grad_gain_two = second_back(back_normed_b)
-    back_middle = back_result + back_middle_norm
-    back_branch = back_middle.astype(BF)
-    grad_out_t = mm(back_branch, attended, 0, 0)
-    back_attended = jnp.dot(back_branch, w_out_t, preferred_element_type=F32).astype(BF)
-
-    output = exchange(result_low)
-    late_grads = [grad_out_t, grad_in, grad_down_t]
-    back_project, *late_sums, squares = attend_back(
+    result_low, back_middle, back_attended, gain_two_grad, *late_grads = mlp_call(
+        tokens,
+        attended,
+        cotangent_low.reshape(rows, width),
+        row_keep,
+        w_out_t,
+        w_in,
+        w_down_t,
+        gain_rows,
+        min(512, rows),
+    )
+    result_low = result_low.reshape(images, band_rows, width)
+    back_project, *late_sums, squares, output = attend_back(
         dims,
         2,
         project,
@@ -836,49 +1096,39 @@
         back_attended,
         256,
         blocks_of(late_grads) if own_comm else [],
+        result_low,
     )
     if not own_comm:
-        late_sums = [lax.psum_scatter(g, both, scatter_dimension=0, tiled=True) for g in late_grads]
-    out_sum, in_sum, down_sum = late_sums
-    back_project, output = lax.optimization_barrier((back_project, output))
-    grad_qkv = mm(normed_a, back_project, 0, 0)
-    back_normed_a = mm(back_project, w_qkv, 1, 1)
-    _, first_back = jax.vjp(rms_norm, tokens, gain_one)
-    back_tokens, grad_gain_one = first_back(back_normed_a)
-    back_rows = (back_middle + back_tokens).astype(BF).reshape(images, band_rows, width)
-    grad_gains = jnp.pad(jnp.stack([grad_gain_one, grad_gain_two], 1), ((0, 0), (0, 126)))
-    early_grads = [grad_qkv, grad_gains]
+        late_sums = [lax.psum_scatter(g.astype(F32), both, scatter_dimension=0, tiled=True) for g in late_grads]
+    back_rows, *early_grads = finish_call(
+        tokens, back_project, w_qkv, back_middle, gain_rows, gain_two_grad, min(256, rows)
+    )
+    back_rows = back_rows.reshape(images, band_rows, width)
     if own_comm:
         qkv_sum, gain_sum, back_input, total = scatter_call(
             dims, "scatter", 3, blocks_of(early_grads), back_rows, squares
         )
     else:
-        qkv_sum, gain_sum = [lax.psum_scatter(g, both, scatter_dimension=0, tiled=True) for g in early_grads]
+        qkv_sum, gain_sum = [
+            lax.psum_scatter(g.astype(F32), both, scatter_dimension=0, tiled=True) for g in early_grads
+        ]
         back_input = exchange(back_rows)
         squares = sum(jnp.sum(g * g) for g in late_sums + [qkv_sum, gain_sum])
         total = lax.psum(jnp.broadcast_to(squares, (8, 128)), both)
-    grad_norm = jnp.sqrt(total[0, 0])
-    factor = jnp.minimum(1.0, CLIP / grad_norm)
-    shards = (
-        qkv_sum,
-        jnp.transpose(out_sum),
-        in_sum,
-        jnp.transpose(down_sum),
-        jnp.transpose(gain_sum[:, :2]),
+    out_sum, in_sum, down_sum = late_sums
+
+    def turned(arrays):
+        return [jnp.transpose(a) if j in (1, 3) else a for j, a in enumerate(arrays)]
+
+    norm, *updated = adam_call(
+        total,
+        [qkv_sum, out_sum, in_sum, down_sum, gain_sum],
+        turned([qkv_master, out_master, in_master, down_master, gain_master]),
+        turned([qkv_first, out_first, in_first, down_first, gain_first]),
+        turned([qkv_second, out_second, in_second, down_second, gain_second]),
     )
-    masters = (qkv_master, out_master, in_master, down_master, gain_master)
-    firsts = (qkv_first, out_first, in_first, down_first, gain_first)
-    seconds = (qkv_second, out_second, in_second, down_second, gain_second)
-    updated = [
-        adam_step(masters[j], shards[j], firsts[j], seconds[j], factor, RATES[j], DECAYS[j]) for j in range(5)
-    ]
-    return (
-        (output, back_input, grad_norm)
-        + tuple(updated[j][0] for j in range(5))
-        + tuple(updated[j][1] for j in range(5))
-        + tuple(updated[j][2] for j in range(5))
-        + tuple(updated[j][0].astype(BF) for j in range(5))
-    )
+    updated = [a for kind in range(4) for a in turned(updated[5 * kind : 5 * kind + 5])]
+    return (output, back_input, norm[0, 0]) + tuple(updated)
 
 
 def solution(mesh):

time: 475 us -> 403 us (0.85)
  matrix products: 90.7 us -> 0 us
  Pallas kernels: 302 us -> 370 us
  other arithmetic: 23.2 us -> 8.57 us
  waiting for transfers between devices: 13 us -> 0 us
  starting transfers between devices: 11.4 us -> 0 us
  local copies, waits for them, and re-layouts: 24.4 us -> 16.8 us
    dot_general x12 -> x0, matrix products: 90.7 us -> none  [the longest x8 55 us: mm(): lax.dot_general(a, b, (((ca,), (cb,)), ((), ())), preferred_element_type=...]
    pallas_call x0 -> x4, Pallas kernels: none -> 83.2 us  [the longest x1 59.8 us: mlp_call(): pl.pallas_call(body, grid=(steps + 1 + in_tiles + down_tiles,), in_specs=...]
    pallas_call x1, Pallas kernels: 94.7 us -> 79.3 us  [attend(): pl.pallas_call(body, grid=(pairs,), in_specs=[column(0), column(pairs), c...]
    all_to_all x2 -> x0, waiting for transfers between devices: 13 us -> none  [exchange(): lax.all_to_all(chunks, 'band', 0, 0, axis_index_groups=places, tiled=True)]
    convert_element_type x11 -> x0, other arithmetic: 12.8 us -> none  [the longest x5 8.35 us: on_device(): updated[j][0].astype(BF)]
    all_to_all x2 -> x0, starting transfers between devices: 11.4 us -> none  [exchange(): lax.all_to_all(chunks, 'band', 0, 0, axis_index_groups=places, tiled=True)]
    pallas_call x1, Pallas kernels: 93.1 us -> 101 us  [attend_back(): pl.pallas_call(body, grid=(pairs,), in_specs=[column(0), column(pairs), c...]
    pallas_call x1, Pallas kernels: 51.7 us -> 44.5 us  [gather_call(): pl.pallas_call(body, out_shape=shapes, in_specs=[ANY] * len(args), out_sp...]
  transfers between devices with their start and end apart: 2 -> 0, of which waited for: 1 -> 0; matrix products, arithmetic and copies ran while one was open for 4% -> 0% of each run, Pallas kernels for 20% -> 0%
where the time goes in v3:
time: 403 us; the launch traced here: 396 us
  Pallas kernels  370 us (92%)
  local copies, waits for them, and re-layouts  16.8 us (4%)
  other arithmetic  8.57 us (2%)
    pallas_call x1, Pallas kernels, attend_back(): pl.pallas_call(body, grid=(pairs,), in_specs=[column(0), column(pairs), c...  101 us
    pallas_call x1, Pallas kernels, attend(): pl.pallas_call(body, grid=(pairs,), in_specs=[column(0), column(pairs), c...  79.3 us
    pallas_call x1, Pallas kernels, scatter_call(): pl.pallas_call(body, out_shape=shapes, in_specs=[ANY] * (n + 1) + [vmem],...  61.5 us
    pallas_call x1, Pallas kernels, mlp_call(): pl.pallas_call(body, grid=(steps + 1 + in_tiles + down_tiles,), in_specs=...  59.8 us
    pallas_call x1, Pallas kernels, gather_call(): pl.pallas_call(body, out_shape=shapes, in_specs=[ANY] * len(args), out_sp...  44.5 us
    pallas_call x1, Pallas kernels, finish_call(): pl.pallas_call(body, grid=(steps + tiles,), in_specs=[row(width), row(3 *...  13.8 us
    unnamed x28, local copies, waits for them, and re-layouts  13 us

profile of v3, /device:TPU:0, one launch (start us, length us, event | category | flops | bytes accessed | tf_op | source)
XLA Modules:
  0.0 396.2 jit_solution(2540129578094967922)
XLA Ops:
  0.7 1.2 dynamic_slice.4
  4.1 0.7 fusion
  5.5 1.5 bitcast_convert_fusion.1.refs_6_
  7.0 1.6 bitcast_convert_fusion.refs_8_
  8.5 1.6 convert_element_type.25.refs_0_
  10.1 1.7 convert_element_type.29.refs_7_
  11.8 1.0 copy.45
  12.9 44.5 %gather.1 = (bf16[2,2,4,2,24,2304]{5,4,3,2,1,0:T(8,128)(2,1)}, bf16[2,2,4,2,24,128]{5,4,3,2,1,0:T(8,128)(2,1)}, bf16[4,256,768]{2,1,0:T(8,128)(2,1)}) custom-call(bf16[24,2304]{1,0:T(8,128)(2,1)} %convert_element_type.25.refs_0_, bf16[24,128]{1,0:T(8,128)(2,1)} %pad.4.refs_1_, bf16[4,256,768]{2,1,0:T(8,128)(2,1)} %refs_2_.1), custom_call_target="tpu_custom_call" | custom-call | tf_op jit(solution)/shard_map/gather/pallas_call | solution.py:348
  57.4 2.0 copy-done.2
  59.3 1.4 copy-done.3
  60.8 0.9 copy-done.5
  61.7 5.0 %project.1 = (bf16[1024,2304]{1,0:T(8,128)(2,1)S(1)}, f32[8,768]{1,0:T(8,128)S(1)}) custom-call(bf16[1024,768]{1,0:T(8,128)(2,1)S(1)} %bitcast.43, bf16[768,2304]{1,0:T(8,128)(2,1)S(1)} %bitcast.41, bf16[768,128]{1,0:T(8,128)(2,1)S(1)} %bitcast.45), custom_call_target="tpu_custom_call" | custom-call | flops 3623878656 | bytes 8257536 | tf_op jit(solution)/shard_map/project/pallas_call | solution.py:739
  66.7 2.1 copy-done.6
  69.4 79.3 %attend.1 = (bf16[1024,768]{1,0:T(8,128)(2,1)}, f32[1024,768]{1,0:T(8,128)}, bf16[1,12,1024,128]{3,2,1,0:T(8,128)(2,1)}, bf16[4,256,768]{2,1,0:T(8,128)(2,1)}, b...) custom-call(bf16[1024,2304]{1,0:T(8,128)(2,1)} %copy-done.6, ...), custom_call_target="tpu_custom_call" | custom-call | flops 25769803776 | bytes 12582912 | tf_op jit(solution)/shard_map/attend/pallas_call | solution.py:521
  148.7 59.8 %mlp.1 = (bf16[1024,768]{1,0:T(8,128)(2,1)}, f32[1024,768]{1,0:T(8,128)}, bf16[1024,768]{1,0:T(8,128)(2,1)}, f32[8,768]{1,0:T(8,128)}, bf16[768,768]{1,0:T(8,128...) custom-call(bf16[1024,768]{1,0:T(8,128)(2,1)} %bitcast.42, ...), custom_call_target="tpu_custom_call" | custom-call | flops 32614907904 | bytes 42467328 | tf_op jit(solution)/shard_map/mlp/pallas_call | solution.py:835
  208.6 101.3 %attend_back.1 = (bf16[1024,2304]{1,0:T(8,128)(2,1)}, f32[24,768]{1,0:T(8,128)}, f32[24,4096]{1,0:T(8,128)}, f32[24,2048]{1,0:T(8,128)}, f32[8,128]{1,0:T(8,128)}, /*index=5*/bf16[4,256,768]{2,1,0:T(8,128)(2,1)}) custom-call(bf16[1024,2304]{1,0:T(8,128)(2,1)} %copy-done.6, bf16[1024,2304]{1,0:T(8,128)(2,1)} %copy-done.6, bf16[1024,2304]{1,0:T(8,128)(2,1)} %copy-done.6, ...), custom_call_target="tpu_custom_call" | custom-call | flops 64424509440 | bytes 25165824 | tf_op jit(solution)/shard_map/attend_back/pallas_call | solution.py:683
  309.9 13.8 %finish.1 = (bf16[1024,768]{1,0:T(8,128)(2,1)S(1)}, bf16[768,2304]{1,0:T(8,128)(2,1)}, bf16[768,128]{1,0:T(8,128)(2,1)S(1)}) custom-call(bf16[1024,768]{1,0:T(8,128)(2,1)S(1)} %bitcast.44, bf16[1024,2304]{1,0:T(8,128)(2,1)} %get-tuple-element.94.b_ref, bf16[768,2304]{1,0:T(8,128)(2,1)} %bitcast.40, f32[1024,768]{1,0:T(8,128)} %get-tuple-element.95.m_ref, ...), custom_call_target="tpu_custom_call" | custom-call | flops 7247757312 | bytes 16515072 | tf_op jit(solution)/shard_map/finish/pallas_call | solution.py:921
  323.7 1.1 copy-done
  325.5 61.5 %scatter.1 = (f32[24,2304]{1,0:T(8,128)}, f32[24,128]{1,0:T(8,128)}, bf16[4,256,768]{2,1,0:T(8,128)(2,1)}, f32[8,128]{1,0:T(8,128)}) custom-call(bf16[2,2,4,2,24,2304]{5,4,3,2,1,0:T(8,128)(2,1)} %bitcast.46, bf16[2,2,4,2,24,128]{5,4,3,2,1,0:T(8,128)(2,1)} %bitcast.39, bf16[4,256,768]{2,1,0:T(8,128)(2,1)} %bitcast.38, f32[8,128]{1,0:T(8,128)} %get-tuple-element.100.refs_3_), custom_call_target="tpu_custom_call" | custom-call | tf_op jit(solution)/shard_map/scatter/pallas_call | solution.py:389
  387.1 4.6 %adam.1 = (f32[8,128]{1,0:T(8,128)}, f32[24,2304]{1,0:T(8,128)}, f32[24,768]{1,0:T(8,128)}, f32[24,4096]{1,0:T(8,128)}, f32[24,2048]{1,0:T(8,128)}, /*index=5*/f...) custom-call(f32[8,128]{1,0:T(8,128)} %get-tuple-element.102.refs_0_,, ...), custom_call_target="tpu_custom_call" | custom-call | tf_op jit(solution)/shard_map/adam/pallas_call | solution.py:982
  391.7 1.2 slice.3
  392.9 1.1 copy.48
  394.0 0.8 copy-done.11
  394.9 1.1 copy.49
  (28 shorter events, 4.1 us)
Async XLA Ops:
  57.3 2.0 copy-start.2
  59.3 1.4 copy-start.3
  60.8 0.9 copy-start.5
  66.7 2.1 copy-start.6
  68.8 0.6 copy-start.7
  208.6 101.3 %copy-start.4 = (bf16[4,256,768]{2,1,0:T(8,128)(2,1)S(1)}, bf16[4,256,768]{2,1,0:T(8,128)(2,1)}, u32[]{:S(2)}) copy-start(bf16[4,256,768]{2,1,0:T(8,128)(2,1)} %get-tuple-element.76) | copy-start | bytes 4718596
  208.6 101.3 %copy-start.8 = (f32[8,768]{1,0:T(8,128)S(1)}, f32[8,768]{1,0:T(8,128)}, u32[]{:S(2)}) copy-start(f32[8,768]{1,0:T(8,128)} %copy-done.7) | copy-start | bytes 73732
  208.6 101.3 %copy-start.9 = (f32[8,768]{1,0:T(8,128)S(1)}, f32[8,768]{1,0:T(8,128)}, u32[]{:S(2)}) copy-start(f32[8,768]{1,0:T(8,128)} %get-tuple-element.96.two_ref) | copy-start | bytes 73732
  323.7 1.1 copy-start
  324.9 0.7 copy-start.1
  387.1 5.8 %copy-start.10 = (bf16[4,256,768]{2,1,0:T(8,128)(2,1)S(1)}, bf16[4,256,768]{2,1,0:T(8,128)(2,1)}, u32[]{:S(2)}) copy-start(bf16[4,256,768]{2,1,0:T(8,128)(2,1)} %get-tuple-element.152) | copy-start | bytes 4718596
  392.9 2.0 copy-start.11

commit v4 on v3

--- a/solution.py
+++ b/solution.py
@@ -47,6 +47,14 @@
                 at[name] = lax.rem(at[name] + d, size)
                 places.append((at[name], (at["y"] * big_x + at["x"], at["z"] * 2 + at["c"])))
             self.lines[name] = places
+        self.band, self.img = band, img
+        self.lines["band"], self.lines["img"] = [], []
+        for d in range(1, 2 * big_z):
+            other = lax.rem(band + d, 2 * big_z)
+            self.lines["band"].append((other, (img, other)))
+        for d in range(1, big_y * big_x):
+            other = lax.rem(img + d, big_y * big_x)
+            self.lines["img"].append((other, (other, band)))
         self.lines["image"] = []
         for d in range(1, self.images):
             other = lax.rem(image + d, self.images)
@@ -188,7 +196,7 @@
     return dims[0] + dims[1] + dims[2] - 3 + 1
 
 
-def scatter(net, grad, held, from_core, from_first, from_second, from_z, out, squares, columns, order):
+def scatter(net, grad, held, from_core, from_first, from_second, from_z, out, squares, columns, order, offset=0):
     big_y, big_x, big_z, _ = net.dims
     cols = pl.ds(*columns)
     y, x, z, c = net.y, net.x, net.z, net.c
@@ -254,7 +262,7 @@
     total = held[y, x, z].astype(F32)
     for slot in range(len(moves)):
         total = total + from_z[slot].astype(F32)
-    out[:, columns[0] : columns[0] + columns[1]] = total
+    out[:, offset + columns[0] : offset + columns[0] + columns[1]] = total
     tile = squares[...]
     for a in range(total.shape[0] // 8):
         for b in range(columns[1] // 128):
@@ -280,10 +288,8 @@
 
 def sum_tiles(net, tile, slots):
     first = 0
-    for name in "cxyz":
+    for name, me in (("band", net.band), ("img", net.img)):
         places = net.line(name)
-        me = dict(y=net.y, x=net.x, z=net.z, c=net.c)[name]
-        size = len(places) + 1
         slots[first + me] = tile[...]
         moves = [net.copy(Part(tile), Part(slots)[first + me], dev) for _, dev in places]
         for move in moves:
@@ -291,10 +297,10 @@
         for move in moves:
             move.wait_send()
         total = slots[first]
-        for d in range(1, size):
+        for d in range(1, len(places) + 1):
             total = total + slots[first + d]
         tile[...] = total
-        first += size
+        first += len(places) + 1
 
 
 def sems(count):
@@ -309,11 +315,13 @@
     return [((0, low), "xy"), ((low, width - low), "yx")]
 
 
-def pieces(width, groups):
-    found = []
-    for group in range(groups):
-        for columns, order in halves(width // groups):
-            found.append((group, (columns[0] + group * (width // groups), columns[1]), order))
+def pieces(width, shares):
+    units, found, start = width // 128, [], 0
+    for group in range(len(shares)):
+        stop = units * sum(shares[: group + 1]) // sum(shares) * 128
+        for columns, order in halves(stop - start):
+            found.append((group, (columns[0] + start, columns[1]), order))
+        start = stop
     return found
 
 
@@ -356,47 +364,126 @@
     )(*args)
 
 
-def scatter_call(dims, name, number, grads, images, squares):
+def finale_call(dims, number, tokens, back_project, weight, back_middle, gains, gain_two_grad, squares, images):
     big_y, big_x, big_z, _ = dims
-    rows = grads[0].shape[4]
-    parts = [(j, columns, order) for j, g in enumerate(grads) for columns, order in halves(g.shape[5])]
-    copies = (len(parts) + 1) * gather_copies(dims) + images.shape[0] - 1
-    local = len(parts) + 1
-    n = len(grads)
+    rows, width = tokens.shape
+    block = rows // images
+    devices = 2 * big_x * big_y * big_z
+    shard = width // devices
+    parts = halves(3 * width + 128)
+    tile = 256
+    band_size, img_size = 2 * big_z, big_x * big_y
+    copies = len(parts) * gather_copies(dims) + images - 1 + band_size + img_size - 2
+    local = len(parts) + 5 + 2 * images
     scratch = [sems(copies), sems(copies), sems(local)]
-    for _, columns, order in parts:
-        scratch += scatter_scratch(dims, rows, columns, order)
-    scratch += [pltpu.VMEM((8, 128), F32), pltpu.VMEM((2 + big_x + big_y + big_z, 8, 128), F32)]
+    for columns, order in parts:
+        scratch += scatter_scratch(dims, shard, columns, order)
+    n_fixed = 3 + 5 * len(parts)
+    scratch += [
+        pltpu.VMEM((8, 128), F32),
+        pltpu.VMEM((band_size + img_size, 8, 128), F32),
+        pltpu.VMEM(tokens.shape, BF),
+        pltpu.VMEM(back_project.shape, BF),
+        pltpu.VMEM(weight.shape, BF),
+        pltpu.VMEM(back_middle.shape, F32),
+        pltpu.VMEM((images, block, width), BF),
+        pltpu.VMEM((width, rows), BF),
+        pltpu.VMEM((128, width), F32),
+    ]
+    scratch += [pltpu.VMEM((big_y, big_x, big_z, 2, shard, columns[1]), BF) for columns, _ in parts]
 
     def body(*refs):
-        ins, outs, rest = refs[: n + 2], refs[n + 2 : 2 * n + 4], refs[2 * n + 4 :]
-        tile, slots = rest[3 + 5 * len(parts) :]
+        x_hbm, b_hbm, w_hbm, m_hbm, g_ref, two_ref, squares_ref = refs[:7]
+        sum_ref, moved, total_ref, rest = refs[7], refs[8], refs[9], refs[10:]
+        tally, slots, x_all, b_all, w_all, m_all, sent, normed_t, gain_rows = rest[n_fixed : n_fixed + 9]
+        grads = rest[n_fixed + 9 :]
         net = Net(dims, *rest[:3])
-        net.greet(["z", "x", "y", "c", "image"])
-        tile[...] = ins[n + 1][...]
+        order = [other for other, _ in net.line("image")] + [net.image]
+        load_w = net.local_copy(Part(w_hbm), Part(w_all))
+        loads = []
+        for chunk in order:
+            at = pl.ds(pl.multiple_of(chunk * block, block), block)
+            loads.append([net.local_copy(Part(a)[at, :], Part(b)[at, :]) for a, b in ((b_hbm, b_all), (x_hbm, x_all))])
+            if len(loads) == 1:
+                load_m = net.local_copy(Part(m_hbm), Part(m_all))
+        net.greet(["z", "x", "y", "c", "image", "band", "img"])
+        tally[...] = squares_ref[...]
+        gain_rows[...] = jnp.zeros_like(gain_rows)
+        gain_rows[1:2, :] = two_ref[0:1, :]
+        load_w.wait()
+        moves = []
+        for place, chunk in enumerate(order):
+            for load in loads[place]:
+                load.wait()
+            if place == 0:
+                load_m.wait()
+            at = pl.ds(pl.multiple_of(chunk * block, block), block)
+            gain = g_ref[0:1, :]
+            x = x_all[at, :].astype(F32)
+            scale = inverse_rms(x)
+            normed_t[:, place * block : (place + 1) * block] = jnp.transpose((x * scale * gain).astype(BF))
+            into, rows_of_gain = norm_back(mm(b_all[at, :], w_all[:, : 3 * width], 1, 1), x, scale, gain)
+            sent[chunk] = (m_all[at, :] + into).astype(BF)
+            gain_rows[0:1, :] += jnp.sum(rows_of_gain, 0, keepdims=True)
+            if place < images - 1:
+                moves.append(net.copy(Part(sent)[chunk], Part(moved)[net.image], net.line("image")[place][1]))
+            else:
+                own = net.local_copy(Part(sent)[chunk], Part(moved)[net.image])
         tasks = []
-        for k, (j, columns, order) in enumerate(parts):
+        for k, (columns, turn) in enumerate(parts):
             buffers = rest[3 + 5 * k : 8 + 5 * k]
-            tasks.append((0, scatter(net, ins[j], *buffers, outs[j], tile, columns, order)))
-        tasks.append((0, exchange_images(net, ins[n], outs[n], 4)))
+            for low in range(columns[0], min(columns[0] + columns[1], 3 * width), tile):
+                total = jnp.zeros((width, tile), F32)
+                for place, chunk in enumerate(order):
+                    at = pl.ds(pl.multiple_of(chunk * block, block), block)
+                    inner = slice(place * block, (place + 1) * block)
+                    total = total + mm(normed_t[:, inner], b_all[at, low : low + tile], 1, 0)
+                into = slice(low - columns[0], low - columns[0] + tile)
+                grads[k][..., into] = total.astype(BF).reshape(grads[k].shape[:5] + (tile,))
+            if k == len(parts) - 1:
+                turned = jnp.transpose(gain_rows[...]).astype(BF)
+                grads[k][..., columns[1] - 128 :] = turned.reshape(grads[k].shape[:5] + (128,))
+            task = scatter(net, grads[k], *buffers, sum_ref, tally, (0, columns[1]), turn, columns[0])
+            next(task)
+            tasks.append((0, task))
         drive(tasks)
-        sum_tiles(net, tile, slots)
-        outs[n + 1][...] = jnp.broadcast_to(jnp.sum(tile[...], keepdims=True), (8, 128))
+        sum_tiles(net, tally, slots)
+        total_ref[...] = jnp.broadcast_to(jnp.sum(tally[...], keepdims=True), (8, 128))
+        for move in moves:
+            move.wait_recv()
+        own.wait()
+        for move in moves:
+            move.wait_send()
 
     vmem = pl.BlockSpec(memory_space=pltpu.VMEM)
-    shapes = [jax.ShapeDtypeStruct((rows, g.shape[5]), F32) for g in grads]
-    shapes += [jax.ShapeDtypeStruct(images.shape, images.dtype), jax.ShapeDtypeStruct((8, 128), F32)]
+    shapes = [
+        jax.ShapeDtypeStruct((shard, 3 * width + 128), F32),
+        jax.ShapeDtypeStruct((images, block, width), BF),
+        jax.ShapeDtypeStruct((8, 128), F32),
+    ]
     return pl.pallas_call(
         body,
         out_shape=shapes,
-        in_specs=[ANY] * (n + 1) + [vmem],
-        out_specs=[vmem] * n + [ANY, vmem],
+        in_specs=[ANY] * 4 + [vmem] * 3,
+        out_specs=[vmem, ANY, vmem],
         scratch_shapes=scratch,
         compiler_params=pltpu.CompilerParams(
-            collective_id=number, has_side_effects=True, vmem_limit_bytes=60 * MIB
+            collective_id=number, has_side_effects=True, vmem_limit_bytes=61 * MIB
         ),
-        name=name,
-    )(*grads, images, squares)
+        name="finale",
+    )(tokens, back_project, weight, back_middle, gains, gain_two_grad, squares)
+
+
+def whole(shape):
+    return pl.BlockSpec(shape, lambda i: (0,) * len(shape))
+
+
+def kept(shape):
+    return pl.BlockSpec(shape, lambda i: (0,) * len(shape), pipeline_mode=pl.Buffered(1))
+
+
+def inverse_rms(value):
+    return lax.rsqrt(jnp.mean(value * value, -1, keepdims=True) + EPS)
 
 
 def mm(a, b, ca, cb):
@@ -404,12 +491,26 @@
 
 
 def at_turn(turn, events):
-    for when in sorted(events):
-
-        @pl.when(turn == when)
-        def _(when=when):
-            for task in events[when]:
-                next(task, None)
+    def visit(whens):
+        if len(whens) == 1:
+
+            @pl.when(turn == whens[0])
+            def _():
+                for task in events[whens[0]]:
+                    next(task, None)
+
+        elif whens:
+            middle = len(whens) // 2
+
+            @pl.when(turn < whens[middle])
+            def _():
+                visit(whens[:middle])
+
+            @pl.when(turn >= whens[middle])
+            def _():
+                visit(whens[middle:])
+
+    visit(sorted(events))
 
 
 def schedule(tasks, turns, last):
@@ -428,25 +529,25 @@
     return lane if h == 0 else ~lane
 
 
-def attend(dims, number, project, bias, block, weights, chunks):
+def attend(dims, number, tokens, weight, bias, block, weights, chunks):
     big_y, big_x, big_z, share = dims
-    rows, width = project.shape[0], project.shape[1] // 3
+    rows, width = tokens.shape
     pairs = width // PAIR
     others = share - 1
-    blocks = rows // block
+    blocks = 4
     n = len(weights)
+    last = LEAD + 4 * pairs
     parts = [
-        (j, columns, order, GATHER_TURNS[j][group])
+        (j, columns, order, GATHER_TURNS[group])
         for j, w in enumerate(weights)
-        for group, columns, order in pieces(w.shape[1], len(GATHER_TURNS[j]))
+        for group, columns, order in pieces(w.shape[1], GATHER_SHARES)
     ]
     copies = len(parts) * gather_copies(dims) + others * 2 * pairs + chunks.shape[0] - 1
-    per_turn = max(blocks // 4, 1)
 
     def body(*refs):
-        q_ref, k_ref, v_ref, project_ref, bias_ref, chunks_in = refs[:6]
-        blocks_in, refs = refs[6 : 6 + n], refs[6 + n :]
-        o_ref, l_ref, kv_out, chunks_out, refs = refs[0], refs[1], refs[2], refs[3], refs[4:]
+        x_ref, w_ref, bias_ref, chunks_in = refs[:4]
+        blocks_in, refs = refs[4 : 4 + n], refs[4 + n :]
+        o_ref, l_ref, kv_out, chunks_out, project_ref, gains_ref, refs = refs[:6] + (refs[6:],)
         gathered, (kv_held, send, recv, local) = refs[:n], refs[n:]
         h = pl.program_id(0)
         net = Net(dims, send, recv, local)
@@ -463,11 +564,24 @@
         tasks = [gather(net, blocks_in[j], gathered[j], columns, order) for j, columns, order, _ in parts]
         tasks.append(exchange_images(net, chunks_in, chunks_out))
         turns = [turn for _, _, _, turn in parts] + [CHUNK_TURNS]
-        events, tail = schedule(tasks, turns, 4 * pairs)
+        events, tail = schedule(tasks, turns, last)
 
         @pl.when(h == 0)
         def _():
             net.greet(["z", "x", "y", "c", "image"] + (["share"] if share > 2 else []))
+            gains_ref[...] = jnp.transpose(w_ref[:, 3 * width :].astype(F32))[:8]
+
+        @pl.when(h == 0)
+        def _():
+            def row_step(i, _):
+                at_turn(i, {t: e for t, e in events.items() if t < LEAD})
+                at = pl.ds(pl.multiple_of(i * block, block), block)
+                x = x_ref[at, :].astype(F32)
+                normed = (x * inverse_rms(x) * gains_ref[0:1, :]).astype(BF)
+                project_ref[at, :] = mm(normed, w_ref[:, : 3 * width], 1, 0).astype(BF)
+                return 0
+
+            lax.fori_loop(0, blocks, row_step, 0)
             for j in range(pairs):
                 for move in key_moves[j] + key_moves[j + pairs]:
                     move.start()
@@ -481,12 +595,17 @@
                 if j == pairs - 1:
                     keep.start()
 
+        def own(first):
+            return pl.ds(pl.multiple_of((h + first) * PAIR, PAIR), PAIR)
+
         def step(i, _):
-            at_turn(h * 4 + i // per_turn, events)
+            at_turn(LEAD + h * 4 + i, {t: e for t, e in events.items() if t >= LEAD})
             at = pl.ds(pl.multiple_of(i * block, block), block)
-            k = jnp.concatenate([k_ref[...]] + [kv_held[s, h] for s in range(others)], 0)
-            v = jnp.concatenate([v_ref[...]] + [kv_held[s, h + pairs] for s in range(others)], 0)
-            q = q_ref[at, :] * jnp.asarray(SCALE, BF)
+            k = jnp.concatenate([project_ref[:, own(pairs)]] + [kv_held[s, h] for s in range(others)], 0)
+            v = jnp.concatenate(
+                [project_ref[:, own(2 * pairs)]] + [kv_held[s, h + pairs] for s in range(others)], 0
+            )
+            q = project_ref[at, own(0)] * jnp.asarray(SCALE, BF)
             mixed, logs = [], []
             for half in range(2):
                 scores = mm(jnp.where(lanes_of(half), q, jnp.zeros_like(q)), k, 1, 1) + bias_ref[...]
@@ -517,13 +636,14 @@
         jax.ShapeDtypeStruct((rows, width), F32),
         jax.ShapeDtypeStruct((others, 2 * pairs, rows, PAIR), BF),
         jax.ShapeDtypeStruct(chunks.shape, chunks.dtype),
+        jax.ShapeDtypeStruct((rows, 3 * width), BF),
+        jax.ShapeDtypeStruct((8, width), F32),
     ] + [jax.ShapeDtypeStruct((big_y, big_x, big_z, 2) + w.shape, w.dtype) for w in weights]
     return pl.pallas_call(
         body,
         grid=(pairs,),
-        in_specs=[column(0), column(pairs), column(2 * pairs), ANY, pl.BlockSpec((1, keys), lambda h: (0, 0))]
-        + [ANY] * (1 + n),
-        out_specs=[column(0), column(0), ANY, ANY] + [ANY] * n,
+        in_specs=[kept(tokens.shape), kept(weight.shape), kept((1, keys))] + [ANY] * (1 + n),
+        out_specs=[column(0), column(0), ANY, ANY, kept((rows, 3 * width)), kept((8, width))] + [ANY] * n,
         out_shape=shapes,
         scratch_shapes=[
             pltpu.VMEM((others, 2 * pairs, rows, PAIR), BF),
@@ -532,22 +652,27 @@
             sems(len(parts) + 2),
         ],
         compiler_params=pltpu.CompilerParams(
-            collective_id=number, has_side_effects=True, vmem_limit_bytes=56 * MIB
+            collective_id=number, has_side_effects=True, vmem_limit_bytes=60 * MIB
         ),
         cost_estimate=pl.CostEstimate(
             flops=16 * rows * keys * width, bytes_accessed=8 * keys * width, transcendentals=rows * keys * HEADS
         ),
         name="attend",
-    )(project, project, project, project, bias, chunks, *weights)
-
-
+    )(tokens, weight, bias, chunks, *weights)
+
+
+LEAD = 4
+GATHER_SHARES = (1, 2, 2, 2, 2, 1)
 GATHER_TURNS = (
-    ((0, 1, 2, 4, 6),),
-    ((0, 3, 6, 11, 13), (1, 7, 13, 18, 20)),
-    ((2, 10, 17, 22, 24),),
+    (0, 3, 4, 7, 9),
+    (0, 4, 7, 11, 13),
+    (1, 7, 11, 15, 17),
+    (2, 11, 15, 20, 22),
+    (4, 15, 20, 25, 27),
+    (6, 20, 25, 27, 28),
 )
-CHUNK_TURNS = (8, 24)
-SCATTER_TURNS = ((1, 4, 11, 17, 24), (0, 2, 8, 14, 20), (1, 3, 9, 15, 21))
+CHUNK_TURNS = (12, 28)
+SCATTER_TURNS = (((1, 4, 11, 17, 24),), ((0, 2, 8, 14, 20),), ((1, 3, 9, 15, 21),))
 RESULT_TURNS = (0, 24)
 
 
@@ -556,12 +681,15 @@
     rows, width = mixed.shape
     pairs = width // PAIR
     others = share - 1
-    blocks = rows // block
+    blocks = 4
     keys = rows * share
     n = len(grads)
-    parts = [(j, columns, order) for j, g in enumerate(grads) for columns, order in halves(g.shape[5])]
+    parts = [
+        (j, columns, order, SCATTER_TURNS[j][group])
+        for j, g in enumerate(grads)
+        for group, columns, order in pieces(g.shape[5], (1,) * len(SCATTER_TURNS[j]))
+    ]
     copies = len(parts) * gather_copies(dims) + others * 2 * pairs + chunks.shape[0] - 1
-    per_turn = max(blocks // 4, 1)
 
     def body(*refs):
         q_ref, k_ref, v_ref, k_other, v_other, bias_ref, mixed_ref, logs_ref, back_ref = refs[:9]
@@ -582,10 +710,10 @@
         key_moves = [move_keys(j) for j in range(2 * pairs)]
         tasks = [
             scatter(net, grads_in[j], *buffers[5 * k : 5 * k + 5], sums[j], squares, columns, order)
-            for k, (j, columns, order) in enumerate(parts)
+            for k, (j, columns, order, _) in enumerate(parts)
         ]
         tasks.append(exchange_images(net, chunks_in, chunks_out))
-        turns = [SCATTER_TURNS[j] for j, _, _ in parts] + [RESULT_TURNS]
+        turns = [turn for _, _, _, turn in parts] + [RESULT_TURNS]
         events, tail = schedule(tasks, turns, 4 * pairs)
 
         @pl.when(h == 0)
@@ -598,7 +726,7 @@
         dv_sum[...] = jnp.zeros_like(dv_sum)
 
         def step(i, _):
-            at_turn(h * 4 + i // per_turn, events)
+            at_turn(h * 4 + i, events)
             at = pl.ds(pl.multiple_of(i * block, block), block)
             k = jnp.concatenate([k_ref[...]] + [k_other[s, 0] for s in range(others)], 0)
             v = jnp.concatenate([v_ref[...]] + [v_other[s, 0] for s in range(others)], 0)
@@ -678,7 +806,7 @@
         sems(copies),
         sems(len(parts) + 1),
     ]
-    for j, columns, order in parts:
+    for _, columns, order, _ in parts:
         scratch += scatter_scratch(dims, shard, columns, order)
     return pl.pallas_call(
         body,
@@ -708,66 +836,33 @@
     )(project, project, project, kv, kv, bias, mixed, logs, back, *grads, chunks)
 
 
-def whole(shape):
-    return pl.BlockSpec(shape, lambda i: (0,) * len(shape))
-
-
-def kept(shape):
-    return pl.BlockSpec(shape, lambda i: (0,) * len(shape), pipeline_mode=pl.Buffered(1))
-
-
-def inverse_rms(value):
-    return lax.rsqrt(jnp.mean(value * value, -1, keepdims=True) + EPS)
-
-
 def norm_back(back, value, scale, gain):
     scaled = back * gain
     inner = jnp.mean(scaled * value, -1, keepdims=True)
     return scale * scaled - value * (scale * scale * scale * inner), back * (value * scale)
 
 
-def project_call(tokens, weight, gains, block):
-    rows, width = tokens.shape
-
-    def body(x_ref, w_ref, g_ref, out_ref, gains_ref):
-        gain_rows = jnp.transpose(g_ref[...].astype(F32))
-        gains_ref[...] = gain_rows[:8]
-        x = x_ref[...].astype(F32)
-        normed = (x * inverse_rms(x) * gain_rows[0:1]).astype(BF)
-        out_ref[...] = mm(normed, w_ref[...], 1, 0).astype(BF)
-
-    return pl.pallas_call(
-        body,
-        grid=(rows // block,),
-        in_specs=[pl.BlockSpec((block, width), lambda i: (i, 0)), kept(weight.shape), kept(gains.shape)],
-        out_specs=[pl.BlockSpec((block, 3 * width), lambda i: (i, 0)), whole((8, width))],
-        out_shape=[jax.ShapeDtypeStruct((rows, 3 * width), BF), jax.ShapeDtypeStruct((8, width), F32)],
-        compiler_params=pltpu.CompilerParams(vmem_limit_bytes=40 * MIB),
-        cost_estimate=pl.CostEstimate(
-            flops=6 * rows * width * width, bytes_accessed=14 * width * width, transcendentals=rows
-        ),
-        name="project",
-    )(tokens, weight, gains)
-
-
 GELU_A = 0.7978845608028654
 GELU_B = 0.044715
 
 
-def mlp_call(tokens, attended, cotangent, keep, w_out_t, w_in, w_down_t, gains, block):
+def mlp_call(tokens, attended, cotangent, keep, weights, gains, block):
     rows, width = tokens.shape
-    hidden_units = w_down_t.shape[1]
+    hidden_units = (weights.shape[1] - width) // 3
     steps = rows // block
     tile = 512
     in_tiles, down_tiles = 2 * hidden_units // tile, hidden_units // tile
     part = 512
 
     def body(
-        x_ref, a_ref, c_ref, keep_ref, wo_ref, wi_ref, wd_ref, g_ref,
+        x_ref, a_ref, c_ref, keep_ref, w_ref, g_ref,
         result_ref, middle_ref, back_ref, gain_ref, g_out_ref, g_in_ref, g_down_ref,
         normed_t, low_t, branch_t, mixed, hidden, back_gu,
     ):
         i = pl.program_id(0)
+        wo_ref = w_ref.at[:, :width]
+        wi_ref = w_ref.at[:, width : width + 2 * hidden_units]
+        wd_ref = w_ref.at[:, width + 2 * hidden_units :]
 
         @pl.when(i == 0)
         def _():
@@ -840,9 +935,7 @@
             row(width),
             row(width),
             row(1),
-            kept(w_out_t.shape),
-            kept(w_in.shape),
-            kept(w_down_t.shape),
+            kept(weights.shape),
             kept(gains.shape),
         ],
         out_specs=[
@@ -878,7 +971,7 @@
             transcendentals=rows * hidden_units,
         ),
         name="mlp",
-    )(tokens, attended, cotangent, keep, w_out_t, w_in, w_down_t, gains)
+    )(tokens, attended, cotangent, keep, weights, gains)
 
 
 def finish_call(tokens, back_project, weight, back_middle, gains, gain_two_grad, block):
@@ -903,7 +996,7 @@
             normed_t[:, at] = jnp.transpose((x * scale * gain).astype(BF))
             back = b_ref[...]
             held[at, :] = back
-            into, rows_of_gain = norm_back(mm(back, w_ref[...], 1, 1), x, scale, gain)
+            into, rows_of_gain = norm_back(mm(back, w_ref[:, : 3 * width], 1, 1), x, scale, gain)
             out_ref[...] = (m_ref[...] + into).astype(BF)
             gain_rows[0:1, :] += jnp.sum(rows_of_gain, 0, keepdims=True)
 
@@ -956,35 +1049,80 @@
 
 
 def adam_call(squares, grads, masters, firsts, seconds):
-    shard = grads[0].shape[0]
+    shard, width = grads[0].shape[0], grads[0].shape[1] - 128
 
     def body(*refs):
         squares_ref, refs = refs[0], refs[1:]
-        ins, norm_ref, outs = refs[:20], refs[20], refs[21:]
+        ins, norm_ref, outs = refs[:19], refs[19], refs[20:]
         norm = jnp.sqrt(squares_ref[0:1, :])
-        norm_ref[...] = jnp.broadcast_to(norm, norm_ref.shape)
+        norm_ref[0, 0] = norm[0, 0]
         factor = jnp.minimum(1.0, CLIP / norm[:, 0:1])
         for j in range(5):
-            grad = ins[j][...]
+            grad = ins[0][:, :width] if j == 0 else ins[0][:, width:] if j == 4 else ins[j][...]
             if j == 4:
                 filled = jnp.concatenate([grad, jnp.zeros((128 - shard, 128), F32)], 0)
                 grad = jnp.transpose(filled)[:2, :shard]
             made = adam_step(
-                ins[5 + j][...], grad, ins[10 + j][...], ins[15 + j][...], factor, RATES[j], DECAYS[j]
+                ins[4 + j][...], grad, ins[9 + j][...], ins[14 + j][...], factor, RATES[j], DECAYS[j]
             )
             for kind in range(3):
                 outs[5 * kind + j][...] = made[kind]
             outs[15 + j][...] = made[0].astype(BF)
 
-    shapes = [jax.ShapeDtypeStruct((8, 128), F32)]
+    shapes = [jax.ShapeDtypeStruct((1, 1), F32)]
     shapes += [jax.ShapeDtypeStruct(m.shape, F32) for _ in range(3) for m in masters]
     shapes += [jax.ShapeDtypeStruct(m.shape, BF) for m in masters]
+    vmem = pl.BlockSpec(memory_space=pltpu.VMEM)
     return pl.pallas_call(
         body,
         out_shape=shapes,
-        compiler_params=pltpu.CompilerParams(vmem_limit_bytes=56 * MIB),
+        out_specs=[pl.BlockSpec(memory_space=pltpu.SMEM)] + [vmem] * 20,
+        compiler_params=pltpu.CompilerParams(vmem_limit_bytes=60 * MIB),
         name="adam",
     )(squares, *grads, *masters, *firsts, *seconds)
+
+
+def prepare_call(dims, counts, qkv, out_t, in_up, down_t, gains, rows, band_rows):
+    share = dims[3]
+    images = rows // band_rows
+    shard, width = qkv.shape[0], out_t.shape[1]
+    wide = in_up.shape[1]
+
+    def body(counts_ref, qkv_ref, out_ref, in_ref, down_ref, gain_ref, early_ref, late_ref, keep_ref, bias_ref):
+        early_ref[:, : 3 * width] = qkv_ref[...].astype(BF)
+        filled = jnp.concatenate([gain_ref[...], jnp.zeros((2, 128 - shard), F32)], 1)
+        filled = jnp.concatenate([filled, jnp.zeros((126, 128), F32)], 0)
+        early_ref[:, 3 * width :] = jnp.transpose(filled)[:shard].astype(BF)
+        late_ref[:, :width] = out_ref[...].astype(BF)
+        late_ref[:, width : width + wide] = in_ref[...].astype(BF)
+        late_ref[:, width + wide :] = down_ref[...].astype(BF)
+        band = lax.axis_index("band")
+        image, part = band // share, lax.rem(band, share)
+        count = counts_ref[image]
+        down = lax.broadcasted_iota(jnp.int32, (band_rows, 1), 0)
+        along = lax.broadcasted_iota(jnp.int32, (1, band_rows), 1)
+        for s in range(images):
+            first = (s * share + part) * band_rows
+            keep_ref[s * band_rows : (s + 1) * band_rows, :] = jnp.where(down + first < count, 1.0, 0.0)
+            for other in range(share):
+                first = (s * share + lax.rem(part + other, share)) * band_rows
+                at = (other * images + s) * band_rows
+                bias_ref[:, at : at + band_rows] = jnp.where(along + first < count, 0.0, NEG)
+
+    vmem = pl.BlockSpec(memory_space=pltpu.VMEM)
+    return pl.pallas_call(
+        body,
+        out_shape=[
+            jax.ShapeDtypeStruct((shard, 3 * width + 128), BF),
+            jax.ShapeDtypeStruct((shard, width + wide + down_t.shape[1]), BF),
+            jax.ShapeDtypeStruct((rows, 1), F32),
+            jax.ShapeDtypeStruct((1, share * rows), F32),
+        ],
+        in_specs=[pl.BlockSpec(memory_space=pltpu.SMEM)] + [vmem] * 5,
+        out_specs=[vmem] * 4,
+        compiler_params=pltpu.CompilerParams(vmem_limit_bytes=60 * MIB),
+        name="prepare",
+    )(counts, qkv, out_t, in_up, down_t, gains)
 
 
 def grid_of(n_img):
@@ -1027,60 +1165,41 @@
     def exchange(chunks):
         return lax.all_to_all(chunks, "band", 0, 0, axis_index_groups=places, tiled=True)
 
-    def flat(got):
-        return [g.reshape(width, g.shape[-1]) for g in got]
-
     def blocks_of(grads):
         return [g.reshape(dims[:3] + (2, shard, g.shape[1])) for g in grads]
 
-    gains_block = jnp.pad(jnp.transpose(gain_master).astype(BF), ((0, 0), (0, 126)))
-    early = [qkv_master.astype(BF), gains_block]
-    late = [
-        jnp.transpose(out_master).astype(BF),
-        in_master.astype(BF),
-        jnp.transpose(down_master).astype(BF),
-    ]
-    if own_comm:
-        w_qkv, gains, tokens_low = gather_call(dims, "gather", 0, early, patches)
-        w_qkv, gains = flat([w_qkv, gains])
-    else:
-        w_qkv, gains = [lax.all_gather(b, both, axis=0, tiled=True) for b in early]
-        tokens_low = exchange(patches)
-    band = lax.axis_index("band")
-    image, part = band // share, band % share
-    count = lax.dynamic_index_in_dim(valid_counts, image, 0, keepdims=False)
-    own_places = (
-        (jnp.arange(images, dtype=jnp.int32)[:, None] * share + part) * band_rows
-        + jnp.arange(band_rows, dtype=jnp.int32)[None, :]
-    ).reshape(rows, 1)
-    row_keep = (own_places < count).astype(F32)
-    key_places = (
-        (
-            jnp.arange(images, dtype=jnp.int32)[None, :, None] * share
-            + lax.rem(part + jnp.arange(share, dtype=jnp.int32), share)[:, None, None]
-        )
-        * band_rows
-        + jnp.arange(band_rows, dtype=jnp.int32)[None, None, :]
-    ).reshape(1, share * rows)
-    bias = jnp.where(key_places < count, 0.0, NEG).astype(F32)
-
-    tokens = tokens_low.reshape(rows, width)
-    project, gain_rows = project_call(tokens, w_qkv, gains, min(256, rows))
-    attended, log_sums, kv, cotangent_low, *late_all = attend(
-        dims, 1, project, bias, 256, late if own_comm else [], cotangent
+    early, late, row_keep, bias = prepare_call(
+        dims,
+        valid_counts,
+        qkv_master,
+        jnp.transpose(out_master),
+        in_master,
+        jnp.transpose(down_master),
+        gain_master,
+        rows,
+        band_rows,
     )
     if own_comm:
-        w_out_t, w_in, w_down_t = flat(late_all)
+        w_early, tokens_low = gather_call(dims, "gather", 0, [early], patches)
+        w_early = w_early.reshape(width, early.shape[1])
     else:
-        w_out_t, w_in, w_down_t = [lax.all_gather(b, both, axis=0, tiled=True) for b in late]
+        w_early = lax.all_gather(early, both, axis=0, tiled=True)
+        tokens_low = exchange(patches)
+    tokens = tokens_low.reshape(rows, width)
+    attended, log_sums, kv, cotangent_low, project, gain_rows, *late_all = attend(
+        dims, 1, tokens, w_early, bias, rows // 4, [late] if own_comm else [], cotangent
+    )
+    if own_comm:
+        w_late = late_all[0].reshape(width, late.shape[1])
+    else:
+        w_late = lax.all_gather(late, both, axis=0, tiled=True)
+
     result_low, back_middle, back_attended, gain_two_grad, *late_grads = mlp_call(
         tokens,
         attended,
         cotangent_low.reshape(rows, width),
         row_keep,
-        w_out_t,
-        w_in,
-        w_down_t,
+        w_late,
         gain_rows,
         min(512, rows),
     )
@@ -1094,26 +1213,24 @@
         attended,
         log_sums,
         back_attended,
-        256,
+        rows // 4,
         blocks_of(late_grads) if own_comm else [],
         result_low,
     )
     if not own_comm:
         late_sums = [lax.psum_scatter(g.astype(F32), both, scatter_dimension=0, tiled=True) for g in late_grads]
-    back_rows, *early_grads = finish_call(
-        tokens, back_project, w_qkv, back_middle, gain_rows, gain_two_grad, min(256, rows)
-    )
-    back_rows = back_rows.reshape(images, band_rows, width)
     if own_comm:
-        qkv_sum, gain_sum, back_input, total = scatter_call(
-            dims, "scatter", 3, blocks_of(early_grads), back_rows, squares
+        qkv_sum, back_input, total = finale_call(
+            dims, 3, tokens, back_project, w_early, back_middle, gain_rows, gain_two_grad, squares, images
         )
     else:
-        qkv_sum, gain_sum = [
-            lax.psum_scatter(g.astype(F32), both, scatter_dimension=0, tiled=True) for g in early_grads
-        ]
-        back_input = exchange(back_rows)
-        squares = sum(jnp.sum(g * g) for g in late_sums + [qkv_sum, gain_sum])
+        back_rows, *early_grads = finish_call(
+            tokens, back_project, w_early, back_middle, gain_rows, gain_two_grad, min(256, rows)
+        )
+        grad = jnp.concatenate([g.astype(F32) for g in early_grads], 1)
+        qkv_sum = lax.psum_scatter(grad, both, scatter_dimension=0, tiled=True)
+        back_input = exchange(back_rows.reshape(images, band_rows, width))
+        squares = sum(jnp.sum(g * g) for g in late_sums + [qkv_sum])
         total = lax.psum(jnp.broadcast_to(squares, (8, 128)), both)
     out_sum, in_sum, down_sum = late_sums
 
@@ -1122,13 +1239,13 @@
 
     norm, *updated = adam_call(
         total,
-        [qkv_sum, out_sum, in_sum, down_sum, gain_sum],
+        [qkv_sum, out_sum, in_sum, down_sum],
         turned([qkv_master, out_master, in_master, down_master, gain_master]),
         turned([qkv_first, out_first, in_first, down_first, gain_first]),
         turned([qkv_second, out_second, in_second, down_second, gain_second]),
     )
     updated = [a for kind in range(4) for a in turned(updated[5 * kind : 5 * kind + 5])]
-    return (output, back_input, norm[0, 0]) + tuple(updated)
+    return (output, back_input, norm.reshape(())) + tuple(updated)
 
 
 def solution(mesh):

time: 403 us -> 360 us (0.89); the launches traced: 396 us -> 362 us
  local copies, waits for them, and re-layouts: 16.8 us -> 3.11 us
  Pallas kernels: 370 us -> 358 us
  other arithmetic: 8.57 us -> 0 us
    pallas_call x5 -> x4, Pallas kernels: 164 us -> 150 us  [the longest x1 82 us: attend(): pl.pallas_call(body, grid=(pairs,), in_specs=[kept(tokens.shape), kept(we...]
    unnamed x28 -> x6, local copies, waits for them, and re-layouts: 13 us -> 3.11 us
    convert_element_type x5 -> x0, other arithmetic: 7.04 us -> none  [the longest x1 1.69 us: on_device(): in_master.astype(BF)]
    pallas_call x1, Pallas kernels: 59.8 us -> 64 us  [mlp_call(): pl.pallas_call(body, grid=(steps + 1 + in_tiles + down_tiles,), in_specs=...]
where the time goes in v4:
time: 360 us; the launch traced here: 362 us
  Pallas kernels  358 us (99%)
    pallas_call x1, Pallas kernels, attend_back(): pl.pallas_call(body, grid=(pairs,), in_specs=[column(0), column(pairs), c...  99.5 us
    pallas_call x1, Pallas kernels, attend(): pl.pallas_call(body, grid=(pairs,), in_specs=[kept(tokens.shape), kept(we...  82 us
    pallas_call x1, Pallas kernels, mlp_call(): pl.pallas_call(body, grid=(steps + 1 + in_tiles + down_tiles,), in_specs=...  64 us
    pallas_call x1, Pallas kernels, finale_call(): pl.pallas_call(body, out_shape=shapes, in_specs=[ANY] * 4 + [vmem] * 3, o...  61.5 us
    pallas_call x1, Pallas kernels, gather_call(): pl.pallas_call(body, out_shape=shapes, in_specs=[ANY] * len(args), out_sp...  44.5 us

profile of v4, /device:TPU:0, one launch (start us, length us, event | category | flops | bytes accessed | tf_op | source)
XLA Modules:
  0.0 362.3 jit_solution(882328458365807864)
XLA Ops:
  0.7 2.2 prepare.1
  2.9 44.5 %gather.1 = (bf16[2,2,4,2,24,2432]{5,4,3,2,1,0:T(8,128)(2,1)}, bf16[4,256,768]{2,1,0:T(8,128)(2,1)}) custom-call(bf16[24,2432]{1,0:T(8,128)(2,1)} %get-tuple-element.73.refs_0_, bf16[4,256,768]{2,1,0:T(8,128)(2,1)} %refs_1_.1), custom_call_target="tpu_custom_call" | custom-call | tf_op jit(solution)/shard_map/gather/pallas_call | solution.py:356
  47.4 82.0 %attend.1 = (bf16[1024,768]{1,0:T(8,128)(2,1)}, f32[1024,768]{1,0:T(8,128)}, bf16[1,12,1024,128]{3,2,1,0:T(8,128)(2,1)}, bf16[4,256,768]{2,1,0:T(8,128)(2,1)}, b...) custom-call(bf16[1024,768]{1,0:T(8,128)(2,1)} %bitcast.25, ...), custom_call_target="tpu_custom_call" | custom-call | flops 25769803776 | bytes 12582912 | tf_op jit(solution)/shard_map/attend/pallas_call | solution.py:642
  129.5 64.0 %mlp.1 = (bf16[1024,768]{1,0:T(8,128)(2,1)}, f32[1024,768]{1,0:T(8,128)}, bf16[1024,768]{1,0:T(8,128)(2,1)}, f32[8,768]{1,0:T(8,128)}, bf16[768,768]{1,0:T(8,128...) custom-call(bf16[1024,768]{1,0:T(8,128)(2,1)} %bitcast.26, ...), custom_call_target="tpu_custom_call" | custom-call | flops 32614907904 | bytes 42467328 | tf_op jit(solution)/shard_map/mlp/pallas_call | solution.py:930
  193.5 99.5 %attend_back.1 = (bf16[1024,2304]{1,0:T(8,128)(2,1)}, f32[24,768]{1,0:T(8,128)}, f32[24,4096]{1,0:T(8,128)}, f32[24,2048]{1,0:T(8,128)}, f32[8,128]{1,0:T(8,128)}, /*index=5*/bf16[4,256,768]{2,1,0:T(8,128)(2,1)}) custom-call(bf16[1024,2304]{1,0:T(8,128)(2,1)} %get-tuple-element.78.refs_0_.refs_1_.refs_2_, ...), custom_call_target="tpu_custom_call" | custom-call | flops 64424509440 | bytes 25165824 | tf_op jit(solution)/shard_map/attend_back/pallas_call | solution.py:811
  293.0 61.5 %finale.1 = (f32[24,2432]{1,0:T(8,128)}, bf16[4,256,768]{2,1,0:T(8,128)(2,1)}, f32[8,128]{1,0:T(8,128)}) custom-call(bf16[1024,768]{1,0:T(8,128)(2,1)} %bitcast.27, bf16[1024,2304]{1,0:T(8,128)(2,1)} %get-tuple-element.92.refs_1_, bf16[768,2432]{1,0:T(8,128)(2,1)} %bitcast.24, f32[1024,768]{1,0:T(8,128)} %get-tuple-element.93.refs_3_, ...), custom_call_target="tpu_custom_call" | custom-call | tf_op jit(solution)/shard_map/finale/pallas_call | solution.py:464
  354.5 0.0 copy-start
  354.5 4.4 %adam.1 = (f32[1,1]{1,0:T(1,128)}, f32[24,2304]{1,0:T(8,128)}, f32[24,768]{1,0:T(8,128)}, f32[24,4096]{1,0:T(8,128)}, f32[24,2048]{1,0:T(8,128)}, /*index=5*/f32...) custom-call(f32[8,128]{1,0:T(8,128)} %get-tuple-element.97.refs_0_, ...), custom_call_target="tpu_custom_call" | custom-call | tf_op jit(solution)/shard_map/adam/pallas_call | solution.py:1076
  358.9 0.0 copy-done
  359.0 0.0 copy-start.1
  359.0 1.1 copy.43
  360.1 0.8 copy-done.1
  360.9 1.1 copy.44
Async XLA Ops:
  354.5 4.4 %copy-start = (bf16[4,256,768]{2,1,0:T(8,128)(2,1)S(1)}, bf16[4,256,768]{2,1,0:T(8,128)(2,1)}, u32[]{:S(2)}) copy-start(bf16[4,256,768]{2,1,0:T(8,128)(2,1)} %get-tuple-element.146) | copy-start | bytes 4718596
  359.0 2.0 copy-start.1

commit v5 on v4

--- a/solution.py
+++ b/solution.py
@@ -55,6 +55,13 @@
         for d in range(1, big_y * big_x):
             other = lax.rem(img + d, big_y * big_x)
             self.lines["img"].append((other, (other, band)))
+        across, along = lax.rem(self.x + 1, big_x), lax.rem(self.y + 1, big_y)
+        one = self.c
+        self.near = (jnp.where(one == 0, self.y, along), jnp.where(one == 0, across, self.x))
+        self.next = (jnp.where(one == 0, along, self.y), jnp.where(one == 0, self.x, across))
+        self.far = (along, across)
+        self.near_device = (self.near[0] * big_x + self.near[1], band)
+        self.next_device = (self.next[0] * big_x + self.next[1], band)
         self.lines["image"] = []
         for d in range(1, self.images):
             other = lax.rem(image + d, self.images)
@@ -161,39 +168,57 @@
         move.wait_send()
 
 
-def gather(net, source, target, columns, order):
+def gather(net, source, target, columns):
     cols = pl.ds(*columns)
-    y, x, z, c = net.y, net.x, net.z, net.c
-    own = net.local_copy(Part(source)[:, cols], Part(target)[y, x, z, c, :, cols])
-    sent = [net.copy(Part(source)[:, cols], Part(target)[y, x, z, c, :, cols], dev) for _, dev in net.line("z")]
+    y, x, c = net.y, net.x, net.c
+    (_, twin), = net.line("c")
+
+    def blocks(place):
+        return Part(target)[place[0], place[1], :, c, :, cols]
+
+    here = Part(target)[y, x, net.z, c, :, cols]
+    own = net.local_copy(Part(source)[:, cols], here)
+    from_z = [net.copy(Part(source)[:, cols], here, dev) for _, dev in net.line("z")]
     yield
     own.wait()
-    for move in sent:
+    for move in from_z:
         move.wait_recv()
-    part = Part(target)[y, x, :, c, :, cols]
-    moves = [net.copy(part, part, dev) for _, dev in net.line(order[0])]
-    sent += moves
+    mine = blocks((y, x))
+    first = net.copy(mine, mine, net.near_device)
+    second = net.copy(mine, mine, net.next_device)
+    twins = [net.copy(mine, mine, twin)]
     yield
-    for move in moves:
+    first.wait_recv()
+    near = blocks(net.near)
+    third = net.copy(near, near, net.next_device)
+    twins.append(net.copy(near, near, twin))
+    yield
+    second.wait_recv()
+    third.wait_recv()
+    for place in (net.next, net.far):
+        twins.append(net.copy(blocks(place), blocks(place), twin))
+    yield
+    for move in twins:
         move.wait_recv()
-    part = Part(target)[y, :, :, c, :, cols] if order[0] == "x" else Part(target)[:, x, :, c, :, cols]
-    moves = [net.copy(part, part, dev) for _, dev in net.line(order[1])]
-    sent += moves
-    yield
-    for move in moves:
-        move.wait_recv()
-    part = Part(target)[:, :, :, c, :, cols]
-    moves = [net.copy(part, part, dev) for _, dev in net.line("c")]
-    sent += moves
-    yield
-    for move in moves:
-        move.wait_recv()
-    for move in sent:
+    for move in from_z + [first, second, third] + twins:
         move.wait_send()
 
 
 def gather_copies(dims):
+    return dims[2] - 1 + 3 + 4
+
+
+def scatter_copies(dims):
     return dims[0] + dims[1] + dims[2] - 3 + 1
+
+
+def add_up(own, others):
+    if len(others) == 1:
+        return own + others[0]
+    total = own.astype(F32)
+    for other in others:
+        total = total + other.astype(F32)
+    return total.astype(own.dtype)
 
 
 def scatter(net, grad, held, from_core, from_first, from_second, from_z, out, squares, columns, order, offset=0):
@@ -211,7 +236,7 @@
 
     def first_add(at, _):
         a, b, d = at // (big_x * big_z), (at // big_z) % big_x, at % big_z
-        held[a, b, d] = (held[a, b, d].astype(F32) + from_core[a, b, d].astype(F32)).astype(BF)
+        held[a, b, d] = held[a, b, d] + from_core[a, b, d]
         return 0
 
     lax.fori_loop(0, big_y * big_x * big_z, first_add, 0)
@@ -228,10 +253,7 @@
     def second_add(at, _):
         a, d = at // big_z, at % big_z
         place = (a, x, d) if order[0] == "x" else (y, a, d)
-        total = held[place].astype(F32)
-        for slot in range(len(moves)):
-            total = total + from_first[slot, a, d].astype(F32)
-        held[place] = total.astype(BF)
+        held[place] = add_up(held[place], [from_first[slot, a, d] for slot in range(len(moves))])
         return 0
 
     lax.fori_loop(0, left * big_z, second_add, 0)
@@ -245,10 +267,7 @@
         move.wait_recv()
 
     def third_add(d, _):
-        total = held[y, x, d].astype(F32)
-        for slot in range(len(moves)):
-            total = total + from_second[slot, d].astype(F32)
-        held[y, x, d] = total.astype(BF)
+        held[y, x, d] = add_up(held[y, x, d], [from_second[slot, d] for slot in range(len(moves))])
         return 0
 
     lax.fori_loop(0, big_z, third_add, 0)
@@ -319,15 +338,14 @@
     units, found, start = width // 128, [], 0
     for group in range(len(shares)):
         stop = units * sum(shares[: group + 1]) // sum(shares) * 128
-        for columns, order in halves(stop - start):
-            found.append((group, (columns[0] + start, columns[1]), order))
+        found.append((start, stop - start))
         start = stop
     return found
 
 
 def gather_call(dims, name, number, blocks, images=None):
     big_y, big_x, big_z, share = dims
-    parts = [halves(block.shape[1]) for block in blocks]
+    parts = [[(0, block.shape[1])] for block in blocks]
     copies = sum(len(p) for p in parts) * gather_copies(dims)
     local = sum(len(p) for p in parts)
     n = len(blocks)
@@ -343,8 +361,8 @@
         net.greet("zxyc" if not with_images else ["z", "x", "y", "c", "image"])
         tasks = []
         for j in range(n):
-            for columns, order in parts[j]:
-                tasks.append((0, gather(net, ins[j], outs[j], columns, order)))
+            for columns in parts[j]:
+                tasks.append((0, gather(net, ins[j], outs[j], columns)))
         if with_images:
             tasks.append((1, exchange_images(net, ins[n], outs[n], 3)))
         drive(tasks)
@@ -373,7 +391,7 @@
     parts = halves(3 * width + 128)
     tile = 256
     band_size, img_size = 2 * big_z, big_x * big_y
-    copies = len(parts) * gather_copies(dims) + images - 1 + band_size + img_size - 2
+    copies = len(parts) * scatter_copies(dims) + images - 1 + band_size + img_size - 2
     local = len(parts) + 5 + 2 * images
     scratch = [sems(copies), sems(copies), sems(local)]
     for columns, order in parts:
@@ -538,9 +556,9 @@
     n = len(weights)
     last = LEAD + 4 * pairs
     parts = [
-        (j, columns, order, GATHER_TURNS[group])
+        (j, columns, GATHER_TURNS[group])
         for j, w in enumerate(weights)
-        for group, columns, order in pieces(w.shape[1], GATHER_SHARES)
+        for group, columns in enumerate(pieces(w.shape[1], GATHER_SHARES))
     ]
     copies = len(parts) * gather_copies(dims) + others * 2 * pairs + chunks.shape[0] - 1
 
@@ -561,9 +579,9 @@
 
         key_moves = [move_keys(j) for j in range(2 * pairs)]
         keep = Move(Part(kv_held), Part(kv_out), None, local, len(parts) + 1, None)
-        tasks = [gather(net, blocks_in[j], gathered[j], columns, order) for j, columns, order, _ in parts]
+        tasks = [gather(net, blocks_in[j], gathered[j], columns) for j, columns, _ in parts]
         tasks.append(exchange_images(net, chunks_in, chunks_out))
-        turns = [turn for _, _, _, turn in parts] + [CHUNK_TURNS]
+        turns = [turn for _, _, turn in parts] + [CHUNK_TURNS]
         events, tail = schedule(tasks, turns, last)
 
         @pl.when(h == 0)
@@ -664,15 +682,19 @@
 LEAD = 4
 GATHER_SHARES = (1, 2, 2, 2, 2, 1)
 GATHER_TURNS = (
-    (0, 3, 4, 7, 9),
-    (0, 4, 7, 11, 13),
-    (1, 7, 11, 15, 17),
-    (2, 11, 15, 20, 22),
-    (4, 15, 20, 25, 27),
-    (6, 20, 25, 27, 28),
+    (0, 3, 6, 10, 12),
+    (0, 5, 10, 14, 18),
+    (1, 8, 14, 19, 22),
+    (2, 12, 19, 23, 26),
+    (3, 15, 22, 27, 28),
+    (5, 18, 25, 28, 28),
 )
 CHUNK_TURNS = (12, 28)
-SCATTER_TURNS = (((1, 4, 11, 17, 24),), ((0, 2, 8, 14, 20),), ((1, 3, 9, 15, 21),))
+SCATTER_TURNS = (
+    ((2, 5, 13, 20, 24),),
+    ((0, 2, 8, 15, 21), (0, 3, 10, 17, 23)),
+    ((1, 4, 12, 19, 24),),
+)
 RESULT_TURNS = (0, 24)
 
 
@@ -685,19 +707,20 @@
     keys = rows * share
     n = len(grads)
     parts = [
-        (j, columns, order, SCATTER_TURNS[j][group])
+        (j, (low + first, wide), order, SCATTER_TURNS[j][group])
         for j, g in enumerate(grads)
-        for group, columns, order in pieces(g.shape[5], (1,) * len(SCATTER_TURNS[j]))
+        for group, (first, width_of) in enumerate(pieces(g.shape[5], (1,) * len(SCATTER_TURNS[j])))
+        for (low, wide), order in halves(width_of)
     ]
-    copies = len(parts) * gather_copies(dims) + others * 2 * pairs + chunks.shape[0] - 1
+    copies = len(parts) * scatter_copies(dims) + others * 2 * pairs + chunks.shape[0] - 1
 
     def body(*refs):
         q_ref, k_ref, v_ref, k_other, v_other, bias_ref, mixed_ref, logs_ref, back_ref = refs[:9]
         grads_in, chunks_in, refs = refs[9 : 9 + n], refs[9 + n], refs[10 + n :]
         out_ref, sums, squares, chunks_out, refs = refs[0], refs[1 : 1 + n], refs[1 + n], refs[2 + n], refs[3 + n :]
-        dk_sum, dv_sum, dk_own, dv_own, parted, arrived, bias_column = refs[:7]
-        send, recv, local = refs[7:10]
-        buffers = refs[10:]
+        dk_sums, dv_sums, parted, arrived, bias_column = refs[:5]
+        send, recv, local = refs[5:8]
+        buffers = refs[8:]
         h = pl.program_id(0)
         net = Net(dims, send, recv, local)
 
@@ -722,8 +745,9 @@
             squares[...] = jnp.zeros_like(squares)
             bias_column[...] = jnp.transpose(jnp.broadcast_to(bias_ref[...], (PAIR, keys)))
 
-        dk_sum[...] = jnp.zeros_like(dk_sum)
-        dv_sum[...] = jnp.zeros_like(dv_sum)
+        turn = lax.rem(h, 2)
+        dk_sums[turn] = jnp.zeros((keys, PAIR), F32)
+        dv_sums[turn] = jnp.zeros((keys, PAIR), F32)
 
         def step(i, _):
             at_turn(h * 4 + i, events)
@@ -734,12 +758,13 @@
             lse = jnp.transpose(logs_ref[at, :])
             products = jnp.transpose(do.astype(F32) * mixed_ref[at, :].astype(F32))
             dqs, dks, dvs = [], [], []
+            mask = jnp.concatenate([bias_column[...]] * (block // PAIR), 1)
             for half in range(2):
                 low, high = half * HEAD_DIM, (half + 1) * HEAD_DIM
                 q_h = jnp.where(lanes_of(half), q, jnp.zeros_like(q))
                 do_h = jnp.where(lanes_of(half), do, jnp.zeros_like(do))
                 row_dots = jnp.sum(products[low:high, :], 0, keepdims=True)
-                chances = jnp.exp(mm(k, q_h, 1, 1) + bias_column[:, :1] - lse[low : low + 1, :])
+                chances = jnp.exp(mm(k, q_h, 1, 1) + mask - lse[low : low + 1, :])
                 slopes = mm(v, do_h, 1, 1)
                 scores = (chances * (slopes - row_dots)).astype(BF)
                 dqs.append(mm(scores, k, 0, 0))
@@ -747,8 +772,8 @@
                 dvs.append(mm(chances.astype(BF), do_h, 1, 0))
             dq = (jnp.where(lanes_of(0), dqs[0], dqs[1]) * SCALE).astype(BF)
             out_ref[at, pl.ds(pl.multiple_of(h * PAIR, PAIR), PAIR)] = dq
-            dk_sum[...] += dks[0] + dks[1]
-            dv_sum[...] += dvs[0] + dvs[1]
+            dk_sums[turn] += dks[0] + dks[1]
+            dv_sums[turn] += dvs[0] + dvs[1]
             return 0
 
         lax.fori_loop(0, blocks, step, 0)
@@ -756,8 +781,8 @@
         def finish(j):
             for move in key_moves[j] + key_moves[j + pairs]:
                 move.wait_recv()
-            for first, kept, total in ((0, j, dk_own), (pairs, j + pairs, dv_own)):
-                value = total[...]
+            for kept, sums_of in ((j, dk_sums), (j + pairs, dv_sums)):
+                value = sums_of[j % 2, 0:rows, :]
                 for slot in range(others):
                     value = value + arrived[slot, kept].astype(F32)
                 out_ref[:, width + PAIR * kept : width + PAIR * (kept + 1)] = value.astype(BF)
@@ -768,12 +793,10 @@
             def _(j=j):
                 if j > 0:
                     finish(j - 1)
-                dk_own[...] = dk_sum[0:rows, :]
-                dv_own[...] = dv_sum[0:rows, :]
                 for slot in range(others):
                     away = slice(rows * (slot + 1), rows * (slot + 2))
-                    parted[slot, j] = dk_sum[away, :].astype(BF)
-                    parted[slot, j + pairs] = dv_sum[away, :].astype(BF)
+                    parted[slot, j] = dk_sums[j % 2, away, :].astype(BF)
+                    parted[slot, j + pairs] = dv_sums[j % 2, away, :].astype(BF)
                 for move in key_moves[j] + key_moves[j + pairs]:
                     move.start()
                 if j == pairs - 1:
@@ -795,10 +818,8 @@
     )
     moved = jax.ShapeDtypeStruct(chunks.shape, chunks.dtype)
     scratch = [
-        pltpu.VMEM((keys, PAIR), F32),
-        pltpu.VMEM((keys, PAIR), F32),
-        pltpu.VMEM((rows, PAIR), F32),
-        pltpu.VMEM((rows, PAIR), F32),
+        pltpu.VMEM((2, keys, PAIR), F32),
+        pltpu.VMEM((2, keys, PAIR), F32),
         pltpu.VMEM((others, 2 * pairs, rows, PAIR), BF),
         pltpu.VMEM((others, 2 * pairs, rows, PAIR), BF),
         pltpu.VMEM((keys, PAIR), F32),
@@ -1157,7 +1178,7 @@
     dims = (big_y, big_x, n_band // 2, share)
     rows = images * band_rows
     shard = qkv_master.shape[0]
-    own_comm = shard % 8 == 0
+    own_comm = shard % 8 == 0 and big_y == big_x == 2
     both = ("img", "band")
 
     places = [[s * share + r for s in range(images)] for r in range(share)]

time: 360 us -> 355 us (0.986); the launches traced: 362 us -> 349 us
  Pallas kernels: 358 us -> 345 us
    pallas_call x1, Pallas kernels: 99.5 us -> 90.2 us  [attend_back(): pl.pallas_call(body, grid=(pairs,), in_specs=[column(0), column(pairs), c...]
where the time goes in v5:
time: 355 us; the launch traced here: 349 us
  Pallas kernels  345 us (97%)
    pallas_call x1, Pallas kernels, attend_back(): pl.pallas_call(body, grid=(pairs,), in_specs=[column(0), column(pairs), c...  90.2 us
    pallas_call x1, Pallas kernels, attend(): pl.pallas_call(body, grid=(pairs,), in_specs=[kept(tokens.shape), kept(we...  80.7 us
    pallas_call x1, Pallas kernels, finale_call(): pl.pallas_call(body, out_shape=shapes, in_specs=[ANY] * 4 + [vmem] * 3, o...  62.1 us
    pallas_call x1, Pallas kernels, mlp_call(): pl.pallas_call(body, grid=(steps + 1 + in_tiles + down_tiles,), in_specs=...  61.8 us
    pallas_call x1, Pallas kernels, gather_call(): pl.pallas_call(body, out_shape=shapes, in_specs=[ANY] * len(args), out_sp...  44 us

profile of v5, /device:TPU:0, one launch (start us, length us, event | category | flops | bytes accessed | tf_op | source)
XLA Modules:
  0.0 349.5 jit_solution(1076290631179895999)
XLA Ops:
  0.7 2.2 prepare.1
  2.9 44.0 %gather.1 = (bf16[2,2,4,2,24,2432]{5,4,3,2,1,0:T(8,128)(2,1)}, bf16[4,256,768]{2,1,0:T(8,128)(2,1)}) custom-call(bf16[24,2432]{1,0:T(8,128)(2,1)} %get-tuple-element.73.refs_0_, bf16[4,256,768]{2,1,0:T(8,128)(2,1)} %refs_1_.1), custom_call_target="tpu_custom_call" | custom-call | tf_op jit(solution)/shard_map/gather/pallas_call | solution.py:374
  46.9 80.7 %attend.1 = (bf16[1024,768]{1,0:T(8,128)(2,1)}, f32[1024,768]{1,0:T(8,128)}, bf16[1,12,1024,128]{3,2,1,0:T(8,128)(2,1)}, bf16[4,256,768]{2,1,0:T(8,128)(2,1)}, b...) custom-call(bf16[1024,768]{1,0:T(8,128)(2,1)} %bitcast.25, ...), custom_call_target="tpu_custom_call" | custom-call | flops 25769803776 | bytes 12582912 | tf_op jit(solution)/shard_map/attend/pallas_call | solution.py:660
  127.6 61.8 %mlp.1 = (bf16[1024,768]{1,0:T(8,128)(2,1)}, f32[1024,768]{1,0:T(8,128)}, bf16[1024,768]{1,0:T(8,128)(2,1)}, f32[8,768]{1,0:T(8,128)}, bf16[768,768]{1,0:T(8,128...) custom-call(bf16[1024,768]{1,0:T(8,128)(2,1)} %bitcast.26, ...), custom_call_target="tpu_custom_call" | custom-call | flops 32614907904 | bytes 42467328 | tf_op jit(solution)/shard_map/mlp/pallas_call | solution.py:951
  189.4 90.2 %attend_back.1 = (bf16[1024,2304]{1,0:T(8,128)(2,1)}, f32[24,768]{1,0:T(8,128)}, f32[24,4096]{1,0:T(8,128)}, f32[24,2048]{1,0:T(8,128)}, f32[8,128]{1,0:T(8,128)}, /*index=5*/bf16[4,256,768]{2,1,0:T(8,128)(2,1)}) custom-call(bf16[1024,2304]{1,0:T(8,128)(2,1)} %get-tuple-element.78.refs_0_.refs_1_.refs_2_, ...), custom_call_target="tpu_custom_call" | custom-call | flops 64424509440 | bytes 25165824 | tf_op jit(solution)/shard_map/attend_back/pallas_call | solution.py:832
  279.6 62.1 %finale.1 = (f32[24,2432]{1,0:T(8,128)}, bf16[4,256,768]{2,1,0:T(8,128)(2,1)}, f32[8,128]{1,0:T(8,128)}) custom-call(bf16[1024,768]{1,0:T(8,128)(2,1)} %bitcast.27, bf16[1024,2304]{1,0:T(8,128)(2,1)} %get-tuple-element.92.refs_1_, bf16[768,2432]{1,0:T(8,128)(2,1)} %bitcast.24, f32[1024,768]{1,0:T(8,128)} %get-tuple-element.93.refs_3_, ...), custom_call_target="tpu_custom_call" | custom-call | tf_op jit(solution)/shard_map/finale/pallas_call | solution.py:482
  341.7 0.0 copy-start
  341.8 4.4 %adam.1 = (f32[1,1]{1,0:T(1,128)}, f32[24,2304]{1,0:T(8,128)}, f32[24,768]{1,0:T(8,128)}, f32[24,4096]{1,0:T(8,128)}, f32[24,2048]{1,0:T(8,128)}, /*index=5*/f32...) custom-call(f32[8,128]{1,0:T(8,128)} %get-tuple-element.97.refs_0_, ...), custom_call_target="tpu_custom_call" | custom-call | tf_op jit(solution)/shard_map/adam/pallas_call | solution.py:1097
  346.2 0.0 copy-done
  346.2 0.0 copy-start.1
  346.2 1.1 copy.43
  347.3 0.8 copy-done.1
  348.2 1.1 copy.44
Async XLA Ops:
  341.7 4.4 %copy-start = (bf16[4,256,768]{2,1,0:T(8,128)(2,1)S(1)}, bf16[4,256,768]{2,1,0:T(8,128)(2,1)}, u32[]{:S(2)}) copy-start(bf16[4,256,768]{2,1,0:T(8,128)(2,1)} %get-tuple-element.146) | copy-start | bytes 4718596
  346.2 2.0 copy-start.1

commit v6 on v5

--- a/solution.py
+++ b/solution.py
@@ -871,7 +871,7 @@
     rows, width = tokens.shape
     hidden_units = (weights.shape[1] - width) // 3
     steps = rows // block
-    tile = 512
+    tile = 1024
     in_tiles, down_tiles = 2 * hidden_units // tile, hidden_units // tile
     part = 512
 
@@ -1222,7 +1222,7 @@
         row_keep,
         w_late,
         gain_rows,
-        min(512, rows),
+        min(256, rows),
     )
     result_low = result_low.reshape(images, band_rows, width)
     back_project, *late_sums, squares, output = attend_back(

time: 355 us -> 337 us (0.949); the launches traced: 349 us -> 337 us
  Pallas kernels: 345 us -> 333 us
    pallas_call x1, Pallas kernels: 61.8 us -> 49.3 us  [mlp_call(): pl.pallas_call(body, grid=(steps + 1 + in_tiles + down_tiles,), in_specs=...]
where the time goes in v6:
time: 337 us
  Pallas kernels  333 us (99%)
    pallas_call x1, Pallas kernels, attend_back(): pl.pallas_call(body, grid=(pairs,), in_specs=[column(0), column(pairs), c...  90.2 us
    pallas_call x1, Pallas kernels, attend(): pl.pallas_call(body, grid=(pairs,), in_specs=[kept(tokens.shape), kept(we...  80.7 us
    pallas_call x1, Pallas kernels, finale_call(): pl.pallas_call(body, out_shape=shapes, in_specs=[ANY] * 4 + [vmem] * 3, o...  62.1 us
    pallas_call x1, Pallas kernels, mlp_call(): pl.pallas_call(body, grid=(steps + 1 + in_tiles + down_tiles,), in_specs=...  49.3 us
    pallas_call x1, Pallas kernels, gather_call(): pl.pallas_call(body, out_shape=shapes, in_specs=[ANY] * len(args), out_sp...  44 us

profile of v6, /device:TPU:0, one launch (start us, length us, event | category | flops | bytes accessed | tf_op | source)
XLA Modules:
  0.0 336.7 jit_solution(11607349858826191446)
XLA Ops:
  0.7 2.2 prepare.1
  2.9 44.0 %gather.1 = (bf16[2,2,4,2,24,2432]{5,4,3,2,1,0:T(8,128)(2,1)}, bf16[4,256,768]{2,1,0:T(8,128)(2,1)}) custom-call(bf16[24,2432]{1,0:T(8,128)(2,1)} %get-tuple-element.73.refs_0_, bf16[4,256,768]{2,1,0:T(8,128)(2,1)} %refs_1_.1), custom_call_target="tpu_custom_call" | custom-call | tf_op jit(solution)/shard_map/gather/pallas_call | solution.py:374
  46.9 80.7 %attend.1 = (bf16[1024,768]{1,0:T(8,128)(2,1)}, f32[1024,768]{1,0:T(8,128)}, bf16[1,12,1024,128]{3,2,1,0:T(8,128)(2,1)}, bf16[4,256,768]{2,1,0:T(8,128)(2,1)}, b...) custom-call(bf16[1024,768]{1,0:T(8,128)(2,1)} %bitcast.25, ...), custom_call_target="tpu_custom_call" | custom-call | flops 25769803776 | bytes 12582912 | tf_op jit(solution)/shard_map/attend/pallas_call | solution.py:660
  127.6 49.3 %mlp.1 = (bf16[1024,768]{1,0:T(8,128)(2,1)}, f32[1024,768]{1,0:T(8,128)}, bf16[1024,768]{1,0:T(8,128)(2,1)}, f32[8,768]{1,0:T(8,128)}, bf16[768,768]{1,0:T(8,128...) custom-call(bf16[1024,768]{1,0:T(8,128)(2,1)} %bitcast.26, ...), custom_call_target="tpu_custom_call" | custom-call | flops 32614907904 | bytes 42467328 | tf_op jit(solution)/shard_map/mlp/pallas_call | solution.py:951
  176.9 90.2 %attend_back.1 = (bf16[1024,2304]{1,0:T(8,128)(2,1)}, f32[24,768]{1,0:T(8,128)}, f32[24,4096]{1,0:T(8,128)}, f32[24,2048]{1,0:T(8,128)}, f32[8,128]{1,0:T(8,128)}, /*index=5*/bf16[4,256,768]{2,1,0:T(8,128)(2,1)}) custom-call(bf16[1024,2304]{1,0:T(8,128)(2,1)} %get-tuple-element.78.refs_0_.refs_1_.refs_2_, ...), custom_call_target="tpu_custom_call" | custom-call | flops 64424509440 | bytes 25165824 | tf_op jit(solution)/shard_map/attend_back/pallas_call | solution.py:832
  267.1 62.1 %finale.1 = (f32[24,2432]{1,0:T(8,128)}, bf16[4,256,768]{2,1,0:T(8,128)(2,1)}, f32[8,128]{1,0:T(8,128)}) custom-call(bf16[1024,768]{1,0:T(8,128)(2,1)} %bitcast.27, bf16[1024,2304]{1,0:T(8,128)(2,1)} %get-tuple-element.92.refs_1_, bf16[768,2432]{1,0:T(8,128)(2,1)} %bitcast.24, f32[1024,768]{1,0:T(8,128)} %get-tuple-element.93.refs_3_, ...), custom_call_target="tpu_custom_call" | custom-call | tf_op jit(solution)/shard_map/finale/pallas_call | solution.py:482
  329.2 0.0 copy-start
  329.2 4.4 %adam.1 = (f32[1,1]{1,0:T(1,128)}, f32[24,2304]{1,0:T(8,128)}, f32[24,768]{1,0:T(8,128)}, f32[24,4096]{1,0:T(8,128)}, f32[24,2048]{1,0:T(8,128)}, /*index=5*/f32...) custom-call(f32[8,128]{1,0:T(8,128)} %get-tuple-element.97.refs_0_, ...), custom_call_target="tpu_custom_call" | custom-call | tf_op jit(solution)/shard_map/adam/pallas_call | solution.py:1097
  333.6 0.0 copy-done
  333.6 0.0 copy-start.1
  333.6 1.1 copy.43
  334.8 0.8 copy-done.1
  335.6 1.1 copy.44
Async XLA Ops:
  329.2 4.4 %copy-start = (bf16[4,256,768]{2,1,0:T(8,128)(2,1)S(1)}, bf16[4,256,768]{2,1,0:T(8,128)(2,1)}, u32[]{:S(2)}) copy-start(bf16[4,256,768]{2,1,0:T(8,128)(2,1)} %get-tuple-element.146) | copy-start | bytes 4718596
  333.6 2.0 copy-start.1

commit v7 on v6

--- a/solution.py
+++ b/solution.py
@@ -682,14 +682,14 @@
 LEAD = 4
 GATHER_SHARES = (1, 2, 2, 2, 2, 1)
 GATHER_TURNS = (
-    (0, 3, 6, 10, 12),
-    (0, 5, 10, 14, 18),
-    (1, 8, 14, 19, 22),
-    (2, 12, 19, 23, 26),
-    (3, 15, 22, 27, 28),
-    (5, 18, 25, 28, 28),
+    (0, 4, 7, 12, 14),
+    (0, 7, 12, 16, 20),
+    (1, 10, 16, 21, 24),
+    (2, 14, 21, 25, 28),
+    (3, 17, 24, 28, 28),
+    (5, 20, 27, 28, 28),
 )
-CHUNK_TURNS = (12, 28)
+CHUNK_TURNS = (14, 28)
 SCATTER_TURNS = (
     ((2, 5, 13, 20, 24),),
     ((0, 2, 8, 15, 21), (0, 3, 10, 17, 23)),

time: 337 us -> 335 us (level)
  no operation moved by 1% of the time
where the time goes in v7:
time: 335 us
  Pallas kernels  331 us (99%)
    pallas_call x1, Pallas kernels, attend_back(): pl.pallas_call(body, grid=(pairs,), in_specs=[column(0), column(pairs), c...  91.2 us
    pallas_call x1, Pallas kernels, attend(): pl.pallas_call(body, grid=(pairs,), in_specs=[kept(tokens.shape), kept(we...  78.2 us
    pallas_call x1, Pallas kernels, finale_call(): pl.pallas_call(body, out_shape=shapes, in_specs=[ANY] * 4 + [vmem] * 3, o...  61.5 us
    pallas_call x1, Pallas kernels, mlp_call(): pl.pallas_call(body, grid=(steps + 1 + in_tiles + down_tiles,), in_specs=...  49.3 us
    pallas_call x1, Pallas kernels, gather_call(): pl.pallas_call(body, out_shape=shapes, in_specs=[ANY] * len(args), out_sp...  44 us

profile of v7, /device:TPU:0, one launch (start us, length us, event | category | flops | bytes accessed | tf_op | source)
XLA Modules:
  0.0 334.7 jit_solution(5956929711966567762)
XLA Ops:
  0.7 2.2 prepare.1
  2.9 44.0 %gather.1 = (bf16[2,2,4,2,24,2432]{5,4,3,2,1,0:T(8,128)(2,1)}, bf16[4,256,768]{2,1,0:T(8,128)(2,1)}) custom-call(bf16[24,2432]{1,0:T(8,128)(2,1)} %get-tuple-element.73.refs_0_, bf16[4,256,768]{2,1,0:T(8,128)(2,1)} %refs_1_.1), custom_call_target="tpu_custom_call" | custom-call | tf_op jit(solution)/shard_map/gather/pallas_call | solution.py:374
  46.9 78.2 %attend.1 = (bf16[1024,768]{1,0:T(8,128)(2,1)}, f32[1024,768]{1,0:T(8,128)}, bf16[1,12,1024,128]{3,2,1,0:T(8,128)(2,1)}, bf16[4,256,768]{2,1,0:T(8,128)(2,1)}, b...) custom-call(bf16[1024,768]{1,0:T(8,128)(2,1)} %bitcast.25, ...), custom_call_target="tpu_custom_call" | custom-call | flops 25769803776 | bytes 12582912 | tf_op jit(solution)/shard_map/attend/pallas_call | solution.py:660
  125.1 49.3 %mlp.1 = (bf16[1024,768]{1,0:T(8,128)(2,1)}, f32[1024,768]{1,0:T(8,128)}, bf16[1024,768]{1,0:T(8,128)(2,1)}, f32[8,768]{1,0:T(8,128)}, bf16[768,768]{1,0:T(8,128...) custom-call(bf16[1024,768]{1,0:T(8,128)(2,1)} %bitcast.26, ...), custom_call_target="tpu_custom_call" | custom-call | flops 32614907904 | bytes 42467328 | tf_op jit(solution)/shard_map/mlp/pallas_call | solution.py:951
  174.4 91.2 %attend_back.1 = (bf16[1024,2304]{1,0:T(8,128)(2,1)}, f32[24,768]{1,0:T(8,128)}, f32[24,4096]{1,0:T(8,128)}, f32[24,2048]{1,0:T(8,128)}, f32[8,128]{1,0:T(8,128)}, /*index=5*/bf16[4,256,768]{2,1,0:T(8,128)(2,1)}) custom-call(bf16[1024,2304]{1,0:T(8,128)(2,1)} %get-tuple-element.78.refs_0_.refs_1_.refs_2_, ...), custom_call_target="tpu_custom_call" | custom-call | flops 64424509440 | bytes 25165824 | tf_op jit(solution)/shard_map/attend_back/pallas_call | solution.py:832
  265.6 61.5 %finale.1 = (f32[24,2432]{1,0:T(8,128)}, bf16[4,256,768]{2,1,0:T(8,128)(2,1)}, f32[8,128]{1,0:T(8,128)}) custom-call(bf16[1024,768]{1,0:T(8,128)(2,1)} %bitcast.27, bf16[1024,2304]{1,0:T(8,128)(2,1)} %get-tuple-element.92.refs_1_, bf16[768,2432]{1,0:T(8,128)(2,1)} %bitcast.24, f32[1024,768]{1,0:T(8,128)} %get-tuple-element.93.refs_3_, ...), custom_call_target="tpu_custom_call" | custom-call | tf_op jit(solution)/shard_map/finale/pallas_call | solution.py:482
  327.1 0.0 copy-start
  327.2 4.4 %adam.1 = (f32[1,1]{1,0:T(1,128)}, f32[24,2304]{1,0:T(8,128)}, f32[24,768]{1,0:T(8,128)}, f32[24,4096]{1,0:T(8,128)}, f32[24,2048]{1,0:T(8,128)}, /*index=5*/f32...) custom-call(f32[8,128]{1,0:T(8,128)} %get-tuple-element.97.refs_0_, ...), custom_call_target="tpu_custom_call" | custom-call | tf_op jit(solution)/shard_map/adam/pallas_call | solution.py:1097
  331.6 0.0 copy-done
  331.6 0.0 copy-start.1
  331.6 1.1 copy.43
  332.7 0.8 copy-done.1
  333.6 1.1 copy.44
Async XLA Ops:
  327.1 4.4 %copy-start = (bf16[4,256,768]{2,1,0:T(8,128)(2,1)S(1)}, bf16[4,256,768]{2,1,0:T(8,128)(2,1)}, u32[]{:S(2)}) copy-start(bf16[4,256,768]{2,1,0:T(8,128)(2,1)} %get-tuple-element.146) | copy-start | bytes 4718596
  331.6 2.0 copy-start.1

commit v8 on v7

--- a/solution.py
+++ b/solution.py
@@ -873,7 +873,7 @@
     steps = rows // block
     tile = 1024
     in_tiles, down_tiles = 2 * hidden_units // tile, hidden_units // tile
-    part = 512
+    part = 1024
 
     def body(
         x_ref, a_ref, c_ref, keep_ref, w_ref, g_ref,

time: 335 us -> 334 us (level)
  no operation moved by 1% of the time
where the time goes in v8:
time: 334 us
  Pallas kernels  330 us (99%)
    pallas_call x1, Pallas kernels, attend_back(): pl.pallas_call(body, grid=(pairs,), in_specs=[column(0), column(pairs), c...  91.2 us
    pallas_call x1, Pallas kernels, attend(): pl.pallas_call(body, grid=(pairs,), in_specs=[kept(tokens.shape), kept(we...  78.2 us
    pallas_call x1, Pallas kernels, finale_call(): pl.pallas_call(body, out_shape=shapes, in_specs=[ANY] * 4 + [vmem] * 3, o...  61.5 us
    pallas_call x1, Pallas kernels, mlp_call(): pl.pallas_call(body, grid=(steps + 1 + in_tiles + down_tiles,), in_specs=...  48.6 us
    pallas_call x1, Pallas kernels, gather_call(): pl.pallas_call(body, out_shape=shapes, in_specs=[ANY] * len(args), out_sp...  44 us

profile of v8, /device:TPU:0, one launch (start us, length us, event | category | flops | bytes accessed | tf_op | source)
XLA Modules:
  0.0 333.9 jit_solution(16875373174098040221)
XLA Ops:
  0.7 2.2 prepare.1
  2.9 44.0 %gather.1 = (bf16[2,2,4,2,24,2432]{5,4,3,2,1,0:T(8,128)(2,1)}, bf16[4,256,768]{2,1,0:T(8,128)(2,1)}) custom-call(bf16[24,2432]{1,0:T(8,128)(2,1)} %get-tuple-element.73.refs_0_, bf16[4,256,768]{2,1,0:T(8,128)(2,1)} %refs_1_.1), custom_call_target="tpu_custom_call" | custom-call | tf_op jit(solution)/shard_map/gather/pallas_call | solution.py:374
  46.9 78.2 %attend.1 = (bf16[1024,768]{1,0:T(8,128)(2,1)}, f32[1024,768]{1,0:T(8,128)}, bf16[1,12,1024,128]{3,2,1,0:T(8,128)(2,1)}, bf16[4,256,768]{2,1,0:T(8,128)(2,1)}, b...) custom-call(bf16[1024,768]{1,0:T(8,128)(2,1)} %bitcast.25, ...), custom_call_target="tpu_custom_call" | custom-call | flops 25769803776 | bytes 12582912 | tf_op jit(solution)/shard_map/attend/pallas_call | solution.py:660
  125.1 48.6 %mlp.1 = (bf16[1024,768]{1,0:T(8,128)(2,1)}, f32[1024,768]{1,0:T(8,128)}, bf16[1024,768]{1,0:T(8,128)(2,1)}, f32[8,768]{1,0:T(8,128)}, bf16[768,768]{1,0:T(8,128...) custom-call(bf16[1024,768]{1,0:T(8,128)(2,1)} %bitcast.26, ...), custom_call_target="tpu_custom_call" | custom-call | flops 32614907904 | bytes 42467328 | tf_op jit(solution)/shard_map/mlp/pallas_call | solution.py:951
  173.7 91.2 %attend_back.1 = (bf16[1024,2304]{1,0:T(8,128)(2,1)}, f32[24,768]{1,0:T(8,128)}, f32[24,4096]{1,0:T(8,128)}, f32[24,2048]{1,0:T(8,128)}, f32[8,128]{1,0:T(8,128)}, /*index=5*/bf16[4,256,768]{2,1,0:T(8,128)(2,1)}) custom-call(bf16[1024,2304]{1,0:T(8,128)(2,1)} %get-tuple-element.78.refs_0_.refs_1_.refs_2_, ...), custom_call_target="tpu_custom_call" | custom-call | flops 64424509440 | bytes 25165824 | tf_op jit(solution)/shard_map/attend_back/pallas_call | solution.py:832
  264.9 61.5 %finale.1 = (f32[24,2432]{1,0:T(8,128)}, bf16[4,256,768]{2,1,0:T(8,128)(2,1)}, f32[8,128]{1,0:T(8,128)}) custom-call(bf16[1024,768]{1,0:T(8,128)(2,1)} %bitcast.27, bf16[1024,2304]{1,0:T(8,128)(2,1)} %get-tuple-element.92.refs_1_, bf16[768,2432]{1,0:T(8,128)(2,1)} %bitcast.24, f32[1024,768]{1,0:T(8,128)} %get-tuple-element.93.refs_3_, ...), custom_call_target="tpu_custom_call" | custom-call | tf_op jit(solution)/shard_map/finale/pallas_call | solution.py:482
  326.4 0.0 copy-start
  326.4 4.4 %adam.1 = (f32[1,1]{1,0:T(1,128)}, f32[24,2304]{1,0:T(8,128)}, f32[24,768]{1,0:T(8,128)}, f32[24,4096]{1,0:T(8,128)}, f32[24,2048]{1,0:T(8,128)}, /*index=5*/f32...) custom-call(f32[8,128]{1,0:T(8,128)} %get-tuple-element.97.refs_0_, ...), custom_call_target="tpu_custom_call" | custom-call | tf_op jit(solution)/shard_map/adam/pallas_call | solution.py:1097
  330.8 0.0 copy-done
  330.8 0.0 copy-start.1
  330.8 1.1 copy.43
  332.0 0.8 copy-done.1
  332.8 1.1 copy.44
Async XLA Ops:
  326.4 4.4 %copy-start = (bf16[4,256,768]{2,1,0:T(8,128)(2,1)S(1)}, bf16[4,256,768]{2,1,0:T(8,128)(2,1)}, u32[]{:S(2)}) copy-start(bf16[4,256,768]{2,1,0:T(8,128)(2,1)} %get-tuple-element.146) | copy-start | bytes 4718596
  330.8 2.0 copy-start.1
